TPU v7x, 256 devices: a whole 4x4x8 slice. The times are simulated.
256 devices in a mesh: rows: 64 (over y_lo, z, x), cols: 4 (over y_hi, core).
Axes of the slice: x: 4, y: 4 (y_hi: 2, y_lo: 2; y = y_hi * 2 + y_lo), z: 8, core: 2. Of those that a mesh axis runs over, the one named last changes fastest.
Arguments:
- inputs: bfloat16 [2, 256, 512, 512], P(None, 'rows', 'cols'), may hold values from -6 to 6
- tight_conv_kernel: bfloat16 [3, 3, 512, 512], P(None, None, 'rows'), may hold values from -0.09375 to 0.09375
- wide_conv_kernel: bfloat16 [3, 3, 512, 512], P(None, None, 'rows'), may hold values from -0.09375 to 0.09375
- up_weight: bfloat16 [512, 2048], P(None, 'rows'), may hold values from -0.25 to 0.25
- down_weight: bfloat16 [2048, 512], P('rows'), may hold values from -0.125 to 0.125
Outputs:
- outputs: bfloat16 [2, 256, 512, 512], P(None, 'rows', 'cols')
All inputs are finite; a program needn't handle non-finite values.
Results may differ from a plain program's by a relative error of at most 0.007.
Values may be sent and summed in bfloat16 or wider, within the bound.
No kernel may reach another device: no remote copies, remote signals or barrier semaphores. Data moves between devices by JAX's collectives and lax.ppermute only.
A program may use at most 64 MiB of HBM per device.

v0:
```python
import functools

import jax
import jax.numpy as jnp
import numpy as np
from jax import lax
from jax.experimental import pallas as pl
from jax.experimental.pallas import tpu as pltpu
from jax.sharding import Mesh, PartitionSpec as P

AXES = ("ylo", "z", "x", "yhi", "core")
SIZES = (2, 8, 4, 2, 2)
PEERS = ("ylo", "z", "yhi", "core")
ROWS, COLS, PAIR = 16, 32, 2
LINE = COLS * PAIR
TAPS = 9
VMEM_LIMIT = 56 * 1024 * 1024


def moved(array, to):
    pairs = []
    for source, (ylo, z, x, yhi, core) in enumerate(np.ndindex(SIZES)):
        y, z, x, core = to(2 * yhi + ylo, z, x, core)
        y, z, x, core = y % 4, z % 8, x % 4, core % 2
        pairs.append((source, int(np.ravel_multi_index((y % 2, z, x, y // 2, core), SIZES))))
    return lax.ppermute(array, AXES, pairs)


def over_x(piece):
    parts = [piece] + [moved(piece, lambda y, z, x, c, k=k: (y, z, x + k, c)) for k in (1, 2, 3)]
    return jnp.stack(parts)


def over_z(piece):
    parts = [piece] + [moved(piece, lambda y, z, x, c, k=k: (y, z + k, x, c)) for k in range(1, 8)]
    return jnp.stack(parts)


def from_y(piece):
    return moved(piece, lambda y, z, x, c: (y + 1 - 2 * c, z, x, c))


def from_core(piece):
    return moved(piece, lambda y, z, x, c: (y, z, x, 1 - c))


def normalized(values):
    return values * lax.rsqrt(jnp.mean(values * values, axis=-1, keepdims=True) + 1e-06)


def conv_kernel(step, where, cells, *refs):
    weights, (out, shifted, kernel, total, sems) = refs[:4], refs[4:]
    x, ylo, core = where[0], where[1], where[2]
    copies = []
    for n, source in enumerate(weights):
        c = core if n < 2 else 1 - core
        y = ylo if n % 2 == 0 else 1 - ylo
        for k in range(4):
            copies.append(
                pltpu.make_async_copy(
                    source.at[k], kernel.at[c, :, y, :, (x + 4 - k) % 4], sems.at[n * 4 + k]
                )
            )
    for copy in copies:
        copy.start()
    ch = cells.shape[-1]
    blank = jnp.zeros((step, LINE, ch), jnp.bfloat16)
    for j in range(3):
        shifted[j, pl.ds(0, step)] = blank
        shifted[j, pl.ds(ROWS + step, step)] = blank
    column = lax.broadcasted_iota(jnp.int32, (LINE, ch), 0)
    by = step * PAIR

    def fill(r, _):
        row = normalized(cells[r].astype(jnp.float32))
        before = jnp.where(column >= by, pltpu.roll(row, by, 0), 0.0)
        after = jnp.where(column < LINE - by, pltpu.roll(row, LINE - by, 0), 0.0)
        shifted[0, r + step] = before.astype(jnp.bfloat16)
        shifted[1, r + step] = row.astype(jnp.bfloat16)
        shifted[2, r + step] = after.astype(jnp.bfloat16)
        return 0

    lax.fori_loop(0, ROWS, fill, 0)
    for copy in copies:
        copy.wait()
    half = ch // 2
    for c in range(2):
        total[c] = cells[...].reshape(ROWS * LINE, ch)[:, c * half : (c + 1) * half].astype(jnp.float32)

    def tap(t, _):
        i, j = t // 3, t % 3
        window = shifted[j, pl.ds(i * step, ROWS)].reshape(ROWS * LINE, ch)
        for c in range(2):
            part = kernel[c, t].reshape(ch, half)
            total[c] += jnp.dot(window, part, preferred_element_type=jnp.float32)
        return 0

    lax.fori_loop(0, TAPS, tap, 0)
    for c in range(2):
        out[:, :, c * half : (c + 1) * half] = total[c].astype(jnp.bfloat16).reshape(ROWS, LINE, half)


def conv_block(cells, weights, step, where):
    ch = cells.shape[-1]
    whole = pl.BlockSpec(memory_space=pltpu.VMEM)
    return pl.pallas_call(
        functools.partial(conv_kernel, step),
        out_shape=jax.ShapeDtypeStruct(cells.shape, jnp.bfloat16),
        in_specs=[pl.BlockSpec(memory_space=pltpu.SMEM), whole] + [pl.BlockSpec(memory_space=pl.ANY)] * 4,
        out_specs=whole,
        scratch_shapes=[
            pltpu.VMEM((3, ROWS + 2 * step, LINE, ch), jnp.bfloat16),
            pltpu.VMEM((2, TAPS, 2, 8, 4, 8, ch // 2), jnp.bfloat16),
            pltpu.VMEM((2, ROWS * LINE, ch // 2), jnp.float32),
            pltpu.SemaphoreType.DMA((16,)),
        ],
        compiler_params=pltpu.CompilerParams(vmem_limit_bytes=VMEM_LIMIT),
        cost_estimate=pl.CostEstimate(
            flops=2 * TAPS * ROWS * LINE * ch * ch, bytes_accessed=7 * 2**20, transcendentals=0
        ),
    )(where, cells, *weights)


def ffn_kernel(cells, *refs):
    pieces, (out, held, total, sems) = refs[:4], refs[4:]
    copies = [pltpu.make_async_copy(piece, held.at[n], sems.at[n]) for n, piece in enumerate(pieces)]
    for copy in copies:
        copy.start()
    ch = cells.shape[-1]
    total[...] = cells[...].reshape(-1, ch).astype(jnp.float32)
    rows = normalized(total[...]).astype(jnp.bfloat16)
    for n in range(4):
        copies[n].wait()
        up = held[n, :, 0].reshape(-1, ch)
        down = held[n, :, 1].reshape(-1, ch)
        hidden = lax.dot_general(rows, up, (((1,), (1,)), ((), ())), preferred_element_type=jnp.float32)
        hidden = jax.nn.gelu(hidden).astype(jnp.bfloat16)
        total[...] += jnp.dot(hidden, down, preferred_element_type=jnp.float32)
    out[...] = total[...].astype(jnp.bfloat16).reshape(out.shape)


def ffn_block(cells, pieces):
    ch = cells.shape[-1]
    whole = pl.BlockSpec(memory_space=pltpu.VMEM)
    return pl.pallas_call(
        ffn_kernel,
        out_shape=jax.ShapeDtypeStruct(cells.shape, jnp.bfloat16),
        in_specs=[whole] + [pl.BlockSpec(memory_space=pl.ANY)] * 4,
        out_specs=whole,
        scratch_shapes=[
            pltpu.VMEM((4,) + pieces[0].shape, jnp.bfloat16),
            pltpu.VMEM((ROWS * LINE, ch), jnp.float32),
            pltpu.SemaphoreType.DMA((4,)),
        ],
        compiler_params=pltpu.CompilerParams(vmem_limit_bytes=VMEM_LIMIT),
        cost_estimate=pl.CostEstimate(
            flops=4 * ROWS * LINE * ch * 4 * ch, bytes_accessed=6 * 2**20, transcendentals=ROWS * LINE * 4 * ch
        ),
    )(cells, *pieces)


def shards(inputs, tight, wide, up, down):
    core = lax.axis_index("core")
    where = jnp.stack([lax.axis_index("x"), lax.axis_index("ylo"), core]).astype(jnp.int32)
    s, i, cols, ch = inputs.shape
    n = down.shape[0] // 2
    both = jnp.stack([tight, wide]).reshape(2, TAPS, -1, ch)
    both = lax.dynamic_slice_in_dim(both, core * (ch // 2), ch // 2, axis=3)
    mlp = jnp.stack([lax.dynamic_slice_in_dim(up.T, core * n, n, 0), lax.dynamic_slice_in_dim(down, core * n, n, 0)])

    cells = inputs.reshape(s, i, 8, 8, PAIR, ch).transpose(0, 1, 3, 2, 4, 5).reshape(64, 16, ch)
    both_z = lax.all_to_all(jnp.broadcast_to(both[None], (8,) + both.shape), "z", 0, 0)
    both_z, cells, mlp = lax.optimization_barrier((both_z, cells, mlp))
    both_z = both_z.transpose(1, 2, 0, 3, 4)
    cells = lax.all_to_all(cells, PEERS, 0, 0).reshape(ROWS, LINE, ch)

    t_own = over_x(both_z[0])
    t_other = over_x(from_y(both_z[0]))
    tight_parts = [t_own, t_other, from_core(t_own), from_core(t_other)]

    w_own = over_x(both_z[1])
    w_other = from_y(w_own)
    wide_parts = [w_own, w_other, from_core(w_own), from_core(w_other)]

    f_z = over_z(mlp).transpose(1, 0, 2, 3)
    f_own = over_x(f_z)
    f_other = from_y(f_own)
    mlp_parts = [f_own, f_other, from_core(f_own), from_core(f_other)]

    near = conv_block(cells, tight_parts, 1, where)
    far = conv_block(near, wide_parts, 4, where)
    out = ffn_block(far, mlp_parts)
    out = lax.all_to_all(out.reshape(64, 16, ch), PEERS, 0, 0)
    return out.reshape(s, i, 8, 8, PAIR, ch).transpose(0, 1, 3, 2, 4, 5).reshape(inputs.shape)


def solution(mesh):
    grid = Mesh(mesh.devices.reshape(SIZES), AXES)
    rows, columns = ("ylo", "z", "x"), ("yhi", "core")
    placed = (
        P(None, rows, columns, None),
        P(None, None, rows, None),
        P(None, None, rows, None),
        P(None, rows),
        P(rows, None),
    )
    return jax.shard_map(shards, mesh=grid, in_specs=placed, out_specs=P(None, rows, columns, None), check_vma=False)
```

profile of v0, /device:TPU:33, one launch (start us, length us, event | category | flops | bytes accessed | tf_op | source)
XLA Modules:
  0.0 209.2 jit_solution(10899624699034995395)
XLA Ops:
  1.7 8.0 %all-to-all-start = ((bf16[8,2,9,8,256]{4,3,2,1,0:T(8,128)(2,1)}), bf16[8,2,9,8,256]{4,3,2,1,0:T(8,128)(2,1)S(1)}, u32[]{:S(2)}, u32[]{:S(2)}) async-start(bf16[8,2,9,8,256]{4,3,2,1,0:T(8,128)(2,1)} %broadcast_in_dim.2), calls=%async_computation | async-start | bytes 1179648 | tf_op jit(solution)/shard_map/all_to_all | solution.py:172
  12.7 12.4 %all-to-all-done = bf16[8,2,9,8,256]{4,3,2,1,0:T(8,128)(2,1)S(1)} async-done(((bf16[8,2,9,8,256]{4,3,2,1,0:T(8,128)(2,1)}), bf16[8,2,9,8,256]{4,3,2,1,0:T(8,128)(2,1)S(1)}, u32[]{:S(2)}, u32[]{:S(2)}) %all-to-all-start) | async-done | bytes 589856 | tf_op jit(solution)/shard_map/all_to_all | solution.py:172
  25.2 2.6 %collective-permute-start.11 = (bf16[9,8,8,256]{3,2,1,0:T(8,128)(2,1)S(1)}, bf16[9,8,8,256]{3,2,1,0:T(8,128)(2,1)S(1)}, u32[]{:S(2)}, u32[]{:S(2)}) collective-permute-start(bf16[9,8,8,256]{3,2,1,0:T(8,128)(2,1)S(1)} %get-tuple-element.13), channel_id=1, source_target_pairs={{0,12},{1,13},{2,14},{3,15},{4,0},{5,1},{6,2},{7,3},{8,4},{9,5},{1... | collective-permute-start | bytes 884744 | tf_op jit(solution)/shard_map/ppermute | solution.py:26
  30.1 14.4 %all-to-all-start.1 = ((bf16[64,16,512]{2,1,0:T(8,128)(2,1)}), bf16[64,16,512]{2,1,0:T(8,128)(2,1)}, u32[]{:S(2)}, u32[]{:S(2)}) async-start(bf16[64,16,512]{2,1,0:T(8,128)(2,1)} %reshape.25), calls=%async_computation.1 | async-start | bytes 2097152 | tf_op jit(solution)/shard_map/all_to_all | solution.py:175
  44.5 4.3 %collective-permute-start.17 = (bf16[2,16,512]{2,1,0:T(8,128)(2,1)S(1)}, bf16[2,16,512]{2,1,0:T(8,128)(2,1)S(1)}, u32[]{:S(2)}, u32[]{:S(2)}) collective-permute-start(bf16[2,16,512]{2,1,0:T(8,128)(2,1)S(1)} %pad_maximum_fusion.4), channel_id=1, source_target_pairs={{0,48},{1,49},{2,50},{3,51},{4,52},{5,53},{6,54},{7,55},{8,56},{9,... | collective-permute-start | bytes 98312 | tf_op jit(solution)/shard_map/ppermute | solution.py:26
  49.0 22.3 %collective-permute-done.17 = bf16[2,16,512]{2,1,0:T(8,128)(2,1)S(1)} collective-permute-done((bf16[2,16,512]{2,1,0:T(8,128)(2,1)S(1)}, bf16[2,16,512]{2,1,0:T(8,128)(2,1)S(1)}, u32[]{:S(2)}, u32[]{:S(2)}) %collective-permute-start.17) | collective-permute-done | bytes 32800 | tf_op jit(solution)/shard_map/ppermute | solution.py:26
  71.3 2.0 collective-permute-start.19
  73.3 2.5 %collective-permute-start.20 = (bf16[2,16,512]{2,1,0:T(8,128)(2,1)S(1)}, bf16[2,16,512]{2,1,0:T(8,128)(2,1)S(1)}, u32[]{:S(2)}, u32[]{:S(2)}) collective-permute-start(bf16[2,16,512]{2,1,0:T(8,128)(2,1)S(1)} %pad_maximum_fusion.4), channel_id=1, source_target_pairs={{0,96},{1,97},{2,98},{3,99},{4,100},{5,101},{6,102},{7,103},{8,104... | collective-permute-start | bytes 98312 | tf_op jit(solution)/shard_map/ppermute | solution.py:26
  75.8 1.7 collective-permute-done.19
  77.5 2.1 collective-permute-start.2
  80.8 3.1 %collective-permute-start.3 = (bf16[9,8,8,256]{3,2,1,0:T(8,128)(2,1)S(1)}, bf16[9,8,8,256]{3,2,1,0:T(8,128)(2,1)S(1)}, u32[]{:S(2)}, u32[]{:S(2)}) collective-permute-start(bf16[9,8,8,256]{3,2,1,0:T(8,128)(2,1)S(1)} %get-tuple-element.12), channel_id=1, source_target_pairs={{0,128},{1,131},{2,130},{3,129},{4,132},{5,135},{6,134},{7,133},{8... | collective-permute-start | bytes 884744 | tf_op jit(solution)/shard_map/ppermute | solution.py:26
  83.9 2.3 %collective-permute-start.21 = (bf16[2,16,512]{2,1,0:T(8,128)(2,1)S(1)}, bf16[2,16,512]{2,1,0:T(8,128)(2,1)S(1)}, u32[]{:S(2)}, u32[]{:S(2)}) collective-permute-start(bf16[2,16,512]{2,1,0:T(8,128)(2,1)S(1)} %pad_maximum_fusion.4), channel_id=1, source_target_pairs={{0,112},{1,113},{2,114},{3,115},{4,116},{5,117},{6,118},{7,119},{8... | collective-permute-start | bytes 98312 | tf_op jit(solution)/shard_map/ppermute | solution.py:26
  90.7 4.6 %collective-permute-done = bf16[9,8,8,256]{3,2,1,0:T(8,128)(2,1)S(1)} collective-permute-done((bf16[9,8,8,256]{3,2,1,0:T(8,128)(2,1)S(1)}, bf16[9,8,8,256]{3,2,1,0:T(8,128)(2,1)S(1)}, u32[]{:S(2)}, u32[]{:S(2)}) %collective-permute-start) | collective-permute-done | bytes 294944 | tf_op jit(solution)/shard_map/ppermute | solution.py:26
  95.3 2.7 %collective-permute-start.6 = (bf16[9,8,8,256]{3,2,1,0:T(8,128)(2,1)S(1)}, bf16[9,8,8,256]{3,2,1,0:T(8,128)(2,1)S(1)}, u32[]{:S(2)}, u32[]{:S(2)}) collective-permute-start(bf16[9,8,8,256]{3,2,1,0:T(8,128)(2,1)S(1)} %collective-permute-done.3), channel_id=1, source_target_pairs={{0,12},{1,13},{2,14},{3,15},{4,0},{5,1},{6,2},{7,3},{8,4},{9,5},{1... | collective-permute-start | bytes 884744 | tf_op jit(solution)/shard_map/ppermute | solution.py:26
  99.0 1.9 collective-permute-start.4
  101.1 1.7 collective-permute-done.22
  102.8 12.0 %collective-permute-start.7 = (bf16[4,9,8,8,256]{4,3,2,1,0:T(8,128)(2,1)S(1)}, bf16[4,9,8,8,256]{4,3,2,1,0:T(8,128)(2,1)S(1)}, u32[]{:S(2)}, u32[]{:S(2)}) collective-permute-start(bf16[4,9,8,8,256]{4,3,2,1,0:T(8,128)(2,1)S(1)} %pad_maximum_fusion.refs_0_), channel_id=1, source_target_pairs={{0,1},{1,0},{2,3},{3,2},{4,5},{5,4},{6,7},{7,6},{8,9},{9,8},{10,11... | collective-permute-start | bytes 3538952 | tf_op jit(solution)/shard_map/ppermute | solution.py:26
  116.0 3.3 %collective-permute-start.25 = (bf16[4,2,8,16,512]{4,3,2,1,0:T(8,128)(2,1)}, bf16[4,2,8,16,512]{4,3,2,1,0:T(8,128)(2,1)}, u32[]{:S(2)}, u32[]{:S(2)}) collective-permute-start(bf16[4,2,8,16,512]{4,3,2,1,0:T(8,128)(2,1)} %pad_maximum_fusion.3.refs_0_), channel_id=1, source_target_pairs={{0,128},{1,131},{2,130},{3,129},{4,132},{5,135},{6,134},{7,133},{8... | collective-permute-start | bytes 3145736 | tf_op jit(solution)/shard_map/ppermute | solution.py:26
  122.5 9.4 %collective-permute-done.25.refs_1_ = bf16[4,2,8,16,512]{4,3,2,1,0:T(8,128)(2,1)} collective-permute-done((bf16[4,2,8,16,512]{4,3,2,1,0:T(8,128)(2,1)}, bf16[4,2,8,16,512]{4,3,2,1,0:T(8,128)(2,1)}, u32[]{:S(2)}, u32[]{:S(2)}) %collective-permute-start.25) | collective-permute-done | bytes 1048608 | tf_op jit(solution)/shard_map/ppermute | solution.py:26
  131.9 1.9 collective-permute-start.26
  135.5 11.3 %shard_map.55.cells = bf16[16,64,512]{2,1,0:T(8,128)(2,1)} custom-call(s32[3]{0:T(128)} %pad_add_fusion.where, bf16[16,64,512]{2,1,0:T(8,128)(2,1)} %bitcast.9.cells, bf16[4,9,8,8,256]{4,3,2,1,0:T(8,128)(2,1)} %copy-done.2, bf16[4,9,8,8,256]{4,3,2,1,0:T(8,128)(2,1)} %pad_maximum_fusion.1.refs_1_, bf16[4,9,8,8,256]{4,3,2,1,0:T(8,128)(2,1)} %copy-done.5, ...), custom_call_target="tpu_custom_call" | custom-call | flops 4831838208 | bytes 7340032 | tf_op jit(solution)/shard_map/pallas_call | solution.py:106
  146.8 11.3 %shard_map.56.cells = bf16[16,64,512]{2,1,0:T(8,128)(2,1)} custom-call(s32[3]{0:T(128)} %pad_add_fusion.where, bf16[16,64,512]{2,1,0:T(8,128)(2,1)} %shard_map.55.cells, bf16[4,9,8,8,256]{4,3,2,1,0:T(8,128)(2,1)} %copy-done.1, bf16[4,9,8,8,256]{4,3,2,1,0:T(8,128)(2,1)} %collective-permute-done.12.refs_1_, ...), custom_call_target="tpu_custom_call" | custom-call | flops 4831838208 | bytes 7340032 | tf_op jit(solution)/shard_map/pallas_call | solution.py:106
  159.2 9.5 %shard_map.57 = bf16[16,64,512]{2,1,0:T(8,128)(2,1)} custom-call(bf16[16,64,512]{2,1,0:T(8,128)(2,1)} %shard_map.56.cells, bf16[4,2,8,16,512]{4,3,2,1,0:T(8,128)(2,1)} %pad_maximum_fusion.3.refs_0_, bf16[4,2,8,16,512]{4,3,2,1,0:T(8,128)(2,1)} %collective-permute-done.25.refs_1_, bf16[4,2,8,16,512]{4,3,2,1,0:T(8,128)(2,1)} %collective-permute-done.26.refs_2_, ...), custom_call_target="tpu_custom_call" | custom-call | flops 4294967296 | bytes 6291456 | tf_op jit(solution)/shard_map/pallas_call | solution.py:145
  168.7 37.6 %all_to_all.15 = bf16[64,16,512]{2,1,0:T(8,128)(2,1)S(1)} all-to-all(bf16[64,16,512]{2,1,0:T(8,128)(2,1)} %bitcast.75), channel_id=1, replica_groups=mesh['ylo'=2,'z'=8,'x'=4,'yhi'=2,'core'=2] {'ylo','z','yhi','core'}, dimensions={0} | all-to-all | bytes 2097152 | tf_op jit(solution)/shard_map/all_to_all | solution.py:193
  (80 shorter events, 24.0 us)
Async XLA Ops:
  1.7 23.3 %all-to-all-start = ((bf16[8,2,9,8,256]{4,3,2,1,0:T(8,128)(2,1)}), bf16[8,2,9,8,256]{4,3,2,1,0:T(8,128)(2,1)S(1)}, u32[]{:S(2)}, u32[]{:S(2)}) async-start(bf16[8,2,9,8,256]{4,3,2,1,0:T(8,128)(2,1)} %broadcast_in_dim.2), calls=%async_computation | async-start | bytes 1179648 | tf_op jit(solution)/shard_map/all_to_all | solution.py:172
  25.2 55.6 %collective-permute-start.11 = (bf16[9,8,8,256]{3,2,1,0:T(8,128)(2,1)S(1)}, bf16[9,8,8,256]{3,2,1,0:T(8,128)(2,1)S(1)}, u32[]{:S(2)}, u32[]{:S(2)}) collective-permute-start(bf16[9,8,8,256]{3,2,1,0:T(8,128)(2,1)S(1)} %get-tuple-element.13), channel_id=1, source_target_pairs={{0,12},{1,13},{2,14},{3,15},{4,0},{5,1},{6,2},{7,3},{8,4},{9,5},{1... | collective-permute-start | bytes 884744 | tf_op jit(solution)/shard_map/ppermute | solution.py:26
  27.8 53.1 %collective-permute-start.10 = (bf16[9,8,8,256]{3,2,1,0:T(8,128)(2,1)S(1)}, bf16[9,8,8,256]{3,2,1,0:T(8,128)(2,1)S(1)}, u32[]{:S(2)}, u32[]{:S(2)}) collective-permute-start(bf16[9,8,8,256]{3,2,1,0:T(8,128)(2,1)S(1)} %get-tuple-element.13), channel_id=1, source_target_pairs={{0,8},{1,9},{2,10},{3,11},{4,12},{5,13},{6,14},{7,15},{8,0},{9,1},... | collective-permute-start | bytes 884744 | tf_op jit(solution)/shard_map/ppermute | solution.py:26
  28.3 55.6 %collective-permute-start.9 = (bf16[9,8,8,256]{3,2,1,0:T(8,128)(2,1)S(1)}, bf16[9,8,8,256]{3,2,1,0:T(8,128)(2,1)S(1)}, u32[]{:S(2)}, u32[]{:S(2)}) collective-permute-start(bf16[9,8,8,256]{3,2,1,0:T(8,128)(2,1)S(1)} %get-tuple-element.13), channel_id=1, source_target_pairs={{0,4},{1,5},{2,6},{3,7},{4,8},{5,9},{6,10},{7,11},{8,12},{9,13},{1... | collective-permute-start | bytes 884744 | tf_op jit(solution)/shard_map/ppermute | solution.py:26
  28.9 15.6 %collective-permute-start.15 = (bf16[2,16,512]{2,1,0:T(8,128)(2,1)S(1)}, bf16[2,16,512]{2,1,0:T(8,128)(2,1)S(1)}, u32[]{:S(2)}, u32[]{:S(2)}) collective-permute-start(bf16[2,16,512]{2,1,0:T(8,128)(2,1)S(1)} %pad_maximum_fusion.4), channel_id=1, source_target_pairs={{0,16},{1,17},{2,18},{3,19},{4,20},{5,21},{6,22},{7,23},{8,24},{9,... | collective-permute-start | bytes 98312 | tf_op jit(solution)/shard_map/ppermute | solution.py:26
  29.3 19.5 %collective-permute-start.16 = (bf16[2,16,512]{2,1,0:T(8,128)(2,1)S(1)}, bf16[2,16,512]{2,1,0:T(8,128)(2,1)S(1)}, u32[]{:S(2)}, u32[]{:S(2)}) collective-permute-start(bf16[2,16,512]{2,1,0:T(8,128)(2,1)S(1)} %pad_maximum_fusion.4), channel_id=1, source_target_pairs={{0,32},{1,33},{2,34},{3,35},{4,36},{5,37},{6,38},{7,39},{8,40},{9,... | collective-permute-start | bytes 98312 | tf_op jit(solution)/shard_map/ppermute | solution.py:26
  30.1 105.4 %all-to-all-start.1 = ((bf16[64,16,512]{2,1,0:T(8,128)(2,1)}), bf16[64,16,512]{2,1,0:T(8,128)(2,1)}, u32[]{:S(2)}, u32[]{:S(2)}) async-start(bf16[64,16,512]{2,1,0:T(8,128)(2,1)} %reshape.25), calls=%async_computation.1 | async-start | bytes 2097152 | tf_op jit(solution)/shard_map/all_to_all | solution.py:175
  44.5 26.7 %collective-permute-start.17 = (bf16[2,16,512]{2,1,0:T(8,128)(2,1)S(1)}, bf16[2,16,512]{2,1,0:T(8,128)(2,1)S(1)}, u32[]{:S(2)}, u32[]{:S(2)}) collective-permute-start(bf16[2,16,512]{2,1,0:T(8,128)(2,1)S(1)} %pad_maximum_fusion.4), channel_id=1, source_target_pairs={{0,48},{1,49},{2,50},{3,51},{4,52},{5,53},{6,54},{7,55},{8,56},{9,... | collective-permute-start | bytes 98312 | tf_op jit(solution)/shard_map/ppermute | solution.py:26
  48.8 24.5 %collective-permute-start.18 = (bf16[2,16,512]{2,1,0:T(8,128)(2,1)S(1)}, bf16[2,16,512]{2,1,0:T(8,128)(2,1)S(1)}, u32[]{:S(2)}, u32[]{:S(2)}) collective-permute-start(bf16[2,16,512]{2,1,0:T(8,128)(2,1)S(1)} %pad_maximum_fusion.4), channel_id=1, source_target_pairs={{0,64},{1,65},{2,66},{3,67},{4,68},{5,69},{6,70},{7,71},{8,72},{9,... | collective-permute-start | bytes 98312 | tf_op jit(solution)/shard_map/ppermute | solution.py:26
  77.5 10.6 %collective-permute-start.2 = (bf16[9,8,8,256]{3,2,1,0:T(8,128)(2,1)S(1)}, bf16[9,8,8,256]{3,2,1,0:T(8,128)(2,1)S(1)}, u32[]{:S(2)}, u32[]{:S(2)}) collective-permute-start(bf16[9,8,8,256]{3,2,1,0:T(8,128)(2,1)S(1)} %get-tuple-element.12), channel_id=1, source_target_pairs={{0,12},{1,13},{2,14},{3,15},{4,0},{5,1},{6,2},{7,3},{8,4},{9,5},{1... | collective-permute-start | bytes 884744 | tf_op jit(solution)/shard_map/ppermute | solution.py:26
  79.6 10.2 %collective-permute-start.1 = (bf16[9,8,8,256]{3,2,1,0:T(8,128)(2,1)S(1)}, bf16[9,8,8,256]{3,2,1,0:T(8,128)(2,1)S(1)}, u32[]{:S(2)}, u32[]{:S(2)}) collective-permute-start(bf16[9,8,8,256]{3,2,1,0:T(8,128)(2,1)S(1)} %get-tuple-element.12), channel_id=1, source_target_pairs={{0,8},{1,9},{2,10},{3,11},{4,12},{5,13},{6,14},{7,15},{8,0},{9,1},... | collective-permute-start | bytes 884744 | tf_op jit(solution)/shard_map/ppermute | solution.py:26
  80.8 14.5 %collective-permute-start = (bf16[9,8,8,256]{3,2,1,0:T(8,128)(2,1)S(1)}, bf16[9,8,8,256]{3,2,1,0:T(8,128)(2,1)S(1)}, u32[]{:S(2)}, u32[]{:S(2)}) collective-permute-start(bf16[9,8,8,256]{3,2,1,0:T(8,128)(2,1)S(1)} %get-tuple-element.12), channel_id=1, source_target_pairs={{0,4},{1,5},{2,6},{3,7},{4,8},{5,9},{6,10},{7,11},{8,12},{9,13},{1... | collective-permute-start | bytes 884744 | tf_op jit(solution)/shard_map/ppermute | solution.py:26
  80.8 14.5 %collective-permute-start.3 = (bf16[9,8,8,256]{3,2,1,0:T(8,128)(2,1)S(1)}, bf16[9,8,8,256]{3,2,1,0:T(8,128)(2,1)S(1)}, u32[]{:S(2)}, u32[]{:S(2)}) collective-permute-start(bf16[9,8,8,256]{3,2,1,0:T(8,128)(2,1)S(1)} %get-tuple-element.12), channel_id=1, source_target_pairs={{0,128},{1,131},{2,130},{3,129},{4,132},{5,135},{6,134},{7,133},{8... | collective-permute-start | bytes 884744 | tf_op jit(solution)/shard_map/ppermute | solution.py:26
  87.6 34.4 %collective-permute-start.12 = (bf16[4,9,8,8,256]{4,3,2,1,0:T(8,128)(2,1)S(1)}, bf16[4,9,8,8,256]{4,3,2,1,0:T(8,128)(2,1)}, u32[]{:S(2)}, u32[]{:S(2)}) collective-permute-start(bf16[4,9,8,8,256]{4,3,2,1,0:T(8,128)(2,1)S(1)} %pad_maximum_fusion.2.refs_0_), channel_id=1, source_target_pairs={{0,128},{1,131},{2,130},{3,129},{4,132},{5,135},{6,134},{7,133},{8... | collective-permute-start | bytes 3538952 | tf_op jit(solution)/shard_map/ppermute | solution.py:26
  95.3 20.7 %collective-permute-start.6 = (bf16[9,8,8,256]{3,2,1,0:T(8,128)(2,1)S(1)}, bf16[9,8,8,256]{3,2,1,0:T(8,128)(2,1)S(1)}, u32[]{:S(2)}, u32[]{:S(2)}) collective-permute-start(bf16[9,8,8,256]{3,2,1,0:T(8,128)(2,1)S(1)} %collective-permute-done.3), channel_id=1, source_target_pairs={{0,12},{1,13},{2,14},{3,15},{4,0},{5,1},{6,2},{7,3},{8,4},{9,5},{1... | collective-permute-start | bytes 884744 | tf_op jit(solution)/shard_map/ppermute | solution.py:26
  98.0 21.3 %collective-permute-start.5 = (bf16[9,8,8,256]{3,2,1,0:T(8,128)(2,1)S(1)}, bf16[9,8,8,256]{3,2,1,0:T(8,128)(2,1)S(1)}, u32[]{:S(2)}, u32[]{:S(2)}) collective-permute-start(bf16[9,8,8,256]{3,2,1,0:T(8,128)(2,1)S(1)} %collective-permute-done.3), channel_id=1, source_target_pairs={{0,8},{1,9},{2,10},{3,11},{4,12},{5,13},{6,14},{7,15},{8,0},{9,1},... | collective-permute-start | bytes 884744 | tf_op jit(solution)/shard_map/ppermute | solution.py:26
  99.0 20.3 %collective-permute-start.4 = (bf16[9,8,8,256]{3,2,1,0:T(8,128)(2,1)S(1)}, bf16[9,8,8,256]{3,2,1,0:T(8,128)(2,1)S(1)}, u32[]{:S(2)}, u32[]{:S(2)}) collective-permute-start(bf16[9,8,8,256]{3,2,1,0:T(8,128)(2,1)S(1)} %collective-permute-done.3), channel_id=1, source_target_pairs={{0,4},{1,5},{2,6},{3,7},{4,8},{5,9},{6,10},{7,11},{8,12},{9,13},{1... | collective-permute-start | bytes 884744 | tf_op jit(solution)/shard_map/ppermute | solution.py:26
  102.8 31.0 %collective-permute-start.7 = (bf16[4,9,8,8,256]{4,3,2,1,0:T(8,128)(2,1)S(1)}, bf16[4,9,8,8,256]{4,3,2,1,0:T(8,128)(2,1)S(1)}, u32[]{:S(2)}, u32[]{:S(2)}) collective-permute-start(bf16[4,9,8,8,256]{4,3,2,1,0:T(8,128)(2,1)S(1)} %pad_maximum_fusion.refs_0_), channel_id=1, source_target_pairs={{0,1},{1,0},{2,3},{3,2},{4,5},{5,4},{6,7},{7,6},{8,9},{9,8},{10,11... | collective-permute-start | bytes 3538952 | tf_op jit(solution)/shard_map/ppermute | solution.py:26
  116.0 15.9 %collective-permute-start.25 = (bf16[4,2,8,16,512]{4,3,2,1,0:T(8,128)(2,1)}, bf16[4,2,8,16,512]{4,3,2,1,0:T(8,128)(2,1)}, u32[]{:S(2)}, u32[]{:S(2)}) collective-permute-start(bf16[4,2,8,16,512]{4,3,2,1,0:T(8,128)(2,1)} %pad_maximum_fusion.3.refs_0_), channel_id=1, source_target_pairs={{0,128},{1,131},{2,130},{3,129},{4,132},{5,135},{6,134},{7,133},{8... | collective-permute-start | bytes 3145736 | tf_op jit(solution)/shard_map/ppermute | solution.py:26
  120.5 15.1 %collective-permute-start.8 = (bf16[4,9,8,8,256]{4,3,2,1,0:T(8,128)(2,1)}, bf16[4,9,8,8,256]{4,3,2,1,0:T(8,128)(2,1)}, u32[]{:S(2)}, u32[]{:S(2)}) collective-permute-start(bf16[4,9,8,8,256]{4,3,2,1,0:T(8,128)(2,1)} %pad_maximum_fusion.1.refs_1_), channel_id=1, source_target_pairs={{0,1},{1,0},{2,3},{3,2},{4,5},{5,4},{6,7},{7,6},{8,9},{9,8},{10,11... | collective-permute-start | bytes 3538952 | tf_op jit(solution)/shard_map/ppermute | solution.py:26
  122.0 24.9 %collective-permute-start.13 = (bf16[4,9,8,8,256]{4,3,2,1,0:T(8,128)(2,1)S(1)}, bf16[4,9,8,8,256]{4,3,2,1,0:T(8,128)(2,1)}, u32[]{:S(2)}, u32[]{:S(2)}) collective-permute-start(bf16[4,9,8,8,256]{4,3,2,1,0:T(8,128)(2,1)S(1)} %pad_maximum_fusion.2.refs_0_), channel_id=1, source_target_pairs={{0,1},{1,0},{2,3},{3,2},{4,5},{5,4},{6,7},{7,6},{8,9},{9,8},{10,11... | collective-permute-start | bytes 3538952 | tf_op jit(solution)/shard_map/ppermute | solution.py:26
  122.1 24.8 %collective-permute-start.14 = (bf16[4,9,8,8,256]{4,3,2,1,0:T(8,128)(2,1)}, bf16[4,9,8,8,256]{4,3,2,1,0:T(8,128)(2,1)}, u32[]{:S(2)}, u32[]{:S(2)}) collective-permute-start(bf16[4,9,8,8,256]{4,3,2,1,0:T(8,128)(2,1)} %collective-permute-done.12.refs_1_), channel_id=1, source_target_pairs={{0,1},{1,0},{2,3},{3,2},{4,5},{5,4},{6,7},{7,6},{8,9},{9,8},{10,11... | collective-permute-start | bytes 3538952 | tf_op jit(solution)/shard_map/ppermute | solution.py:26
  131.9 26.3 %collective-permute-start.26 = (bf16[4,2,8,16,512]{4,3,2,1,0:T(8,128)(2,1)}, bf16[4,2,8,16,512]{4,3,2,1,0:T(8,128)(2,1)}, u32[]{:S(2)}, u32[]{:S(2)}) collective-permute-start(bf16[4,2,8,16,512]{4,3,2,1,0:T(8,128)(2,1)} %pad_maximum_fusion.3.refs_0_), channel_id=1, source_target_pairs={{0,1},{1,0},{2,3},{3,2},{4,5},{5,4},{6,7},{7,6},{8,9},{9,8},{10,11... | collective-permute-start | bytes 3145736 | tf_op jit(solution)/shard_map/ppermute | solution.py:26
  134.9 23.3 %collective-permute-start.27 = (bf16[4,2,8,16,512]{4,3,2,1,0:T(8,128)(2,1)}, bf16[4,2,8,16,512]{4,3,2,1,0:T(8,128)(2,1)S(1)}, u32[]{:S(2)}, u32[]{:S(2)}) collective-permute-start(bf16[4,2,8,16,512]{4,3,2,1,0:T(8,128)(2,1)} %collective-permute-done.25.refs_1_), channel_id=1, source_target_pairs={{0,1},{1,0},{2,3},{3,2},{4,5},{5,4},{6,7},{7,6},{8,9},{9,8},{10,11... | collective-permute-start | bytes 3145736 | tf_op jit(solution)/shard_map/ppermute | solution.py:26
  (13 other events, 123.4 us)
where the time goes:
time: 210 us; the launch traced here: 209 us
  starting transfers between devices  72.9 us (35%)
  waiting for transfers between devices  53.4 us (25%)
  blocking collectives  37.6 us (18%)
  Pallas kernels  32.1 us (15%)
  local copies, waits for them, and re-layouts  8.79 us (4%)
  other arithmetic  4.13 us (2%)
    ppermute x28, starting transfers between devices, moved(): return lax.ppermute(array, AXES, pairs)  50.5 us
    ppermute x28, waiting for transfers between devices, moved(): return lax.ppermute(array, AXES, pairs)  41 us
    all_to_all x1, blocking collectives, shards(): out = lax.all_to_all(out.reshape(64, 16, ch), PEERS, 0, 0)  37.6 us
    pallas_call x2, Pallas kernels, conv_block(): pl.pallas_call(functools.partial(conv_kernel, step), out_shape=jax.ShapeD...  22.6 us
    all_to_all x1, starting transfers between devices, shards(): cells = lax.all_to_all(cells, PEERS, 0, 0).reshape(ROWS, LINE, ch)  14.4 us
    all_to_all x1, waiting for transfers between devices, shards(): lax.all_to_all(jnp.broadcast_to(both[None], (8,) + both.shape), 'z', 0, 0)  12.4 us
    pallas_call x1, Pallas kernels, ffn_block(): pl.pallas_call(ffn_kernel, out_shape=jax.ShapeDtypeStruct(cells.shape, jn...  9.51 us
    all_to_all x1, starting transfers between devices, shards(): lax.all_to_all(jnp.broadcast_to(both[None], (8,) + both.shape), 'z', 0, 0)  8.01 us
  transfers between devices with their start and end apart: 30, of which 7 were waited for; matrix products, arithmetic and copies ran while one was open for 3% of the time, Pallas kernels for 11%

commit v1 on v0

v1 whole, which is shorter than its diff:
```python
import functools

import jax
import jax.numpy as jnp
import numpy as np
from jax import lax
from jax.experimental import pallas as pl
from jax.experimental.pallas import tpu as pltpu
from jax.sharding import Mesh, PartitionSpec as P

AXES = ("ylo", "z", "x", "yhi", "core")
SIZES = (2, 8, 4, 2, 2)
PEERS = ("ylo", "z", "yhi", "core")
ROWS, COLS, PAIR = 16, 32, 2
LINE = COLS * PAIR
CELLS = ROWS * LINE
TAPS = 9
MLP = 8
VMEM_LIMIT = 56 * 1024 * 1024


def moved(array, to):
    pairs = []
    for source, (ylo, z, x, yhi, core) in enumerate(np.ndindex(SIZES)):
        y, z, x, core = to(2 * yhi + ylo, z, x, core)
        y, z, x, core = y % 4, z % 8, x % 4, core % 2
        pairs.append((source, int(np.ravel_multi_index((y % 2, z, x, y // 2, core), SIZES))))
    return lax.ppermute(array, AXES, pairs)


def from_x(piece, turn):
    return moved(piece, lambda y, z, x, c: (y, z, x ^ (3 if c != turn else 1), c))


def from_z(piece, bit):
    def partner(y, z, x, c):
        if bit == 2:
            return y, z ^ 4, x, c
        if bit == 1:
            return y, z ^ (6 if c else 2), x, c
        return y, z + (1 if (z + c) % 2 == 0 else -1), x, c

    return moved(piece, partner)


def joined(mine, theirs, place):
    pair = [jnp.where(place == 0, mine, theirs), jnp.where(place == 0, theirs, mine)]
    n, pieces, rows, width = mine.shape
    return jnp.stack(pair, axis=2).reshape(n, 2 * pieces, rows, width)


def from_y(piece):
    return moved(piece, lambda y, z, x, c: (y + 1 - 2 * c, z, x, c))


def from_core(piece):
    return moved(piece, lambda y, z, x, c: (y, z, x, 1 - c))


def x_slots(x, core):
    first = jnp.where(core == 0, x ^ 1, x ^ 3)
    return x, first, x ^ first ^ (x ^ 2), x ^ 2


def normalized(values):
    return values * lax.rsqrt(jnp.mean(values * values, axis=-1, keepdims=True) + 1e-06)


def weight_copies(split_y, where, sources, kernel, sems):
    x, ylo, core = where[0], where[1], where[2]
    copies = []

    def add(source, c, y, at):
        copies.append(pltpu.make_async_copy(source, kernel.at[c, :, y, :, at], sems.at[len(copies)]))

    for far in range(2):
        c = core if far == 0 else 1 - core
        slots = x_slots(x, c)
        for y in range(2):
            y_of = ylo if y == 0 else 1 - ylo
            for part in range(2):
                for k in range(2):
                    if split_y:
                        source = sources[far * 4 + y * 2 + part].at[k, pl.ds(0, TAPS)]
                    else:
                        source = sources[far * 2 + part].at[k, y]
                    add(source, c, y_of, slots[part * 2 + k])
    return copies


def conv_kernel(step, split_y, n_weights, where, cells, *refs):
    weights, (out, shifted, kernel, total, sems) = refs[:n_weights], refs[n_weights:]
    copies = weight_copies(split_y, where, weights, kernel, sems)
    for copy in copies:
        copy.start()
    ch = cells.shape[-1]
    half = ch // 2
    blank = jnp.zeros((step, LINE, 3 * ch), jnp.bfloat16)
    shifted[pl.ds(0, step)] = blank
    shifted[pl.ds(ROWS + step, step)] = blank
    column = lax.broadcasted_iota(jnp.int32, (LINE, ch), 0)
    by = step * PAIR

    def fill(r, _):
        raw = cells[r].astype(jnp.float32)
        for c in range(2):
            total[c, pl.ds(r * LINE, LINE)] = raw[:, c * half : (c + 1) * half]
        row = normalized(raw)
        before = jnp.where(column >= by, pltpu.roll(row, by, 0), 0.0)
        after = jnp.where(column < LINE - by, pltpu.roll(row, LINE - by, 0), 0.0)
        for j, values in enumerate((before, row, after)):
            shifted[r + step, :, j * ch : (j + 1) * ch] = values.astype(jnp.bfloat16)
        return 0

    lax.fori_loop(0, ROWS, fill, 0)
    for copy in copies:
        copy.wait()

    def taps(i, _):
        window = shifted[pl.ds(i * step, ROWS)].reshape(CELLS, 3 * ch)
        for c in range(2):
            part = kernel[c, pl.ds(3 * i, 3)].reshape(3 * ch, half)
            total[c] += jnp.dot(window, part, preferred_element_type=jnp.float32)
        return 0

    lax.fori_loop(0, 3, taps, 0)
    for c in range(2):
        out[:, :, c * half : (c + 1) * half] = total[c].astype(jnp.bfloat16).reshape(ROWS, LINE, half)


def conv_block(cells, weights, step, split_y, where):
    ch = cells.shape[-1]
    whole = pl.BlockSpec(memory_space=pltpu.VMEM)
    return pl.pallas_call(
        functools.partial(conv_kernel, step, split_y, len(weights)),
        out_shape=jax.ShapeDtypeStruct(cells.shape, jnp.bfloat16),
        in_specs=[pl.BlockSpec(memory_space=pltpu.SMEM), whole] + [pl.BlockSpec(memory_space=pl.ANY)] * len(weights),
        out_specs=whole,
        scratch_shapes=[
            pltpu.VMEM((ROWS + 2 * step, LINE, 3 * ch), jnp.bfloat16),
            pltpu.VMEM((2, TAPS, 2, 8, 4, 8, ch // 2), jnp.bfloat16),
            pltpu.VMEM((2, CELLS, ch // 2), jnp.float32),
            pltpu.SemaphoreType.DMA((16,)),
        ],
        compiler_params=pltpu.CompilerParams(vmem_limit_bytes=VMEM_LIMIT),
        cost_estimate=pl.CostEstimate(
            flops=1000, bytes_accessed=1000, transcendentals=0
        ),
    )(where, cells, *weights)


def ffn_kernel(cells, *refs):
    pieces, (out, held, total, sems) = refs[:8], refs[8:]
    copies = []
    for n, piece in enumerate(pieces):
        group = []
        for part in range(4):
            group.append(
                pltpu.make_async_copy(
                    piece.at[:, pl.ds(TAPS + 2 * part, 2)], held.at[part // 2, part % 2, n], sems.at[n * 4 + part]
                )
            )
        copies.append(group)
    for group in copies:
        for copy in group:
            copy.start()
    ch = cells.shape[-1]
    half = ch // 2
    raw = cells[...].reshape(CELLS, ch).astype(jnp.float32)
    rows = normalized(raw).astype(jnp.bfloat16)
    for c in range(2):
        total[c] = raw[:, c * half : (c + 1) * half]
    for n in range(0, 8, 2):
        for copy in copies[n] + copies[n + 1]:
            copy.wait()
        hidden = None
        for c in range(2):
            up = held[c, 0, n : n + 2].reshape(-1, half)
            part = lax.dot_general(
                rows[:, c * half : (c + 1) * half], up, (((1,), (1,)), ((), ())), preferred_element_type=jnp.float32
            )
            hidden = part if hidden is None else hidden + part
        hidden = jax.nn.gelu(hidden).astype(jnp.bfloat16)
        for c in range(2):
            down = held[c, 1, n : n + 2].reshape(-1, half)
            total[c] += jnp.dot(hidden, down, preferred_element_type=jnp.float32)
    for c in range(2):
        out[:, :, c * half : (c + 1) * half] = total[c].astype(jnp.bfloat16).reshape(ROWS, LINE, half)


def ffn_block(cells, pieces):
    ch = cells.shape[-1]
    whole = pl.BlockSpec(memory_space=pltpu.VMEM)
    return pl.pallas_call(
        ffn_kernel,
        out_shape=jax.ShapeDtypeStruct(cells.shape, jnp.bfloat16),
        in_specs=[whole] + [pl.BlockSpec(memory_space=pl.ANY)] * 8,
        out_specs=whole,
        scratch_shapes=[
            pltpu.VMEM((2, 2, 8, 2, 2, 8, 8, ch // 2), jnp.bfloat16),
            pltpu.VMEM((2, CELLS, ch // 2), jnp.float32),
            pltpu.SemaphoreType.DMA((32,)),
        ],
        compiler_params=pltpu.CompilerParams(vmem_limit_bytes=VMEM_LIMIT),
        cost_estimate=pl.CostEstimate(
            flops=1000, bytes_accessed=1000, transcendentals=0
        ),
    )(cells, *pieces)


def shards(inputs, tight, wide, up, down):
    core = lax.axis_index("core")
    where = jnp.stack([lax.axis_index("x"), lax.axis_index("ylo"), core]).astype(jnp.int32)
    s, i, cols, ch = inputs.shape
    half, n = ch // 2, down.shape[0] // 2
    kernels = jnp.concatenate([tight.reshape(TAPS, 8, ch), wide.reshape(TAPS, 8, ch)])
    kernels = lax.dynamic_slice_in_dim(kernels, core * half, half, axis=2)
    mlp = jnp.stack([lax.dynamic_slice_in_dim(up.T, core * n, n, 0), lax.dynamic_slice_in_dim(down, core * n, n, 0)])
    mlp = jnp.stack([mlp[:, :, :half], mlp[:, :, half:]]).reshape(MLP, 8, half)
    shard = jnp.concatenate([kernels, mlp])

    cells = inputs.reshape(s, i, 8, 8, PAIR, ch).transpose(0, 1, 3, 2, 4, 5).reshape(64, 16, ch)
    shard = shard.reshape(-1, 1, 8, half)
    for bit in (2, 1, 0):
        shard = joined(shard, from_z(shard, bit), (lax.axis_index("z") >> bit) & 1)
    shard = shard.reshape(-1, 8, 8, half)
    shard, cells = lax.optimization_barrier((shard, cells))
    cells = lax.all_to_all(cells, PEERS, 0, 0).reshape(ROWS, LINE, ch)

    near_half = jnp.stack([shard[:TAPS], from_y(shard[:TAPS])])
    rest = shard[TAPS:]
    first = jnp.stack([rest, from_x(rest, 0)])
    second = from_x(first, 1)
    first_y = from_y(first)
    t_first = jnp.stack([near_half, from_x(near_half, 0)])
    t_second = from_x(t_first, 1)
    t_second, cells = lax.optimization_barrier((t_second, cells))
    tight_parts = [t_first, t_second, from_core(t_first), from_core(t_second)]
    second, first_y = lax.optimization_barrier((second, first_y))
    own = [first, second, first_y, from_y(second)]
    parts = own + [from_core(piece) for piece in own]

    near = conv_block(cells, tight_parts, 1, False, where)
    far = conv_block(near, parts, 4, True, where)
    out = ffn_block(far, parts)
    out = lax.all_to_all(out.reshape(64, 16, ch), PEERS, 0, 0)
    return out.reshape(s, i, 8, 8, PAIR, ch).transpose(0, 1, 3, 2, 4, 5).reshape(inputs.shape)


def solution(mesh):
    grid = Mesh(mesh.devices.reshape(SIZES), AXES)
    rows, columns = ("ylo", "z", "x"), ("yhi", "core")
    placed = (
        P(None, rows, columns, None),
        P(None, None, rows, None),
        P(None, None, rows, None),
        P(None, rows),
        P(rows, None),
    )
    return jax.shard_map(shards, mesh=grid, in_specs=placed, out_specs=P(None, rows, columns, None), check_vma=False)
```

time: 210 us -> 162 us (0.77)
  starting transfers between devices: 72.9 us -> 40.5 us
  waiting for transfers between devices: 53.4 us -> 43.2 us
  other arithmetic: 4.13 us -> 2 us
    ppermute x28 -> x16, starting transfers between devices: 50.5 us -> 27.6 us  [moved(): return lax.ppermute(array, AXES, pairs)]
    all_to_all x1, waiting for transfers between devices: 0.01 us -> 15.5 us  [shards(): cells = lax.all_to_all(cells, PEERS, 0, 0).reshape(ROWS, LINE, ch)]
    ppermute x28 -> x16, waiting for transfers between devices: 41 us -> 27.7 us  [moved(): return lax.ppermute(array, AXES, pairs)]
    all_to_all x1 -> x0, waiting for transfers between devices: 12.4 us -> none  [shards(): lax.all_to_all(jnp.broadcast_to(both[None], (8,) + both.shape), 'z', 0, 0)]
    all_to_all x1 -> x0, starting transfers between devices: 8.01 us -> none  [shards(): lax.all_to_all(jnp.broadcast_to(both[None], (8,) + both.shape), 'z', 0, 0)]
    another operation x6 -> x10, other arithmetic: 3.48 us -> 0.55 us  [the longest x5 0.25 us: joined(): return jnp.stack(pair, axis=2).reshape(n, 2 * pieces, rows, width)]
    pallas_call x2, Pallas kernels: 22.6 us -> 20.3 us  [conv_block(): pl.pallas_call(functools.partial(conv_kernel, step, split_y, len(weights)...]
  transfers between devices with their start and end apart: 30 -> 17, of which waited for: 7 -> 7; matrix products, arithmetic and copies ran while one was open for 3% -> 2% of each run, Pallas kernels for 11% -> 6%
where the time goes in v1:
time: 162 us
  waiting for transfers between devices  43.2 us (27%)
  starting transfers between devices  40.5 us (25%)
  blocking collectives  38.2 us (24%)
  Pallas kernels  30.1 us (19%)
  local copies, waits for them, and re-layouts  7.37 us (5%)
  other arithmetic  2 us (1%)
    all_to_all x1, blocking collectives, shards(): out = lax.all_to_all(out.reshape(64, 16, ch), PEERS, 0, 0)  38.2 us
    ppermute x16, waiting for transfers between devices, moved(): return lax.ppermute(array, AXES, pairs)  27.7 us
    ppermute x16, starting transfers between devices, moved(): return lax.ppermute(array, AXES, pairs)  27.6 us
    pallas_call x2, Pallas kernels, conv_block(): pl.pallas_call(functools.partial(conv_kernel, step, split_y, len(weights)...  20.3 us
    all_to_all x1, waiting for transfers between devices, shards(): cells = lax.all_to_all(cells, PEERS, 0, 0).reshape(ROWS, LINE, ch)  15.5 us
    all_to_all x1, starting transfers between devices, shards(): cells = lax.all_to_all(cells, PEERS, 0, 0).reshape(ROWS, LINE, ch)  12.9 us
    pallas_call x1, Pallas kernels, ffn_block(): pl.pallas_call(ffn_kernel, out_shape=jax.ShapeDtypeStruct(cells.shape, jn...  9.84 us
  transfers between devices with their start and end apart: 17, of which 7 were waited for; matrix products, arithmetic and copies ran while one was open for 2% of the time, Pallas kernels for 6%

profile of v1, /device:TPU:33, one launch (start us, length us, event | category | flops | bytes accessed | tf_op | source)
XLA Modules:
  0.0 161.7 jit_solution(9726372423218571682)
XLA Ops:
  0.0 0.8 copy-done
  1.5 0.8 fusion
  2.3 6.1 %collective-permute-start = (bf16[26,1,8,256]{3,2,0,1:T(8,128)(2,1)S(1)}, bf16[26,1,8,256]{3,2,0,1:T(8,128)(2,1)S(1)}, u32[]{:S(2)}, u32[]{:S(2)}) collective-permute-start(bf16[26,1,8,256]{3,2,0,1:T(8,128)(2,1)S(1)} %maximum_bitcast_fusion.1), channel_id=1, source_target_pairs={{0,64},{1,65},{2,66},{3,67},{4,68},{5,69},{6,70},{7,71},{8,72},{9,... | collective-permute-start | bytes 319496 | tf_op jit(solution)/shard_map/ppermute | solution.py:28
  8.4 2.7 %collective-permute-done = bf16[26,1,8,256]{3,2,0,1:T(8,128)(2,1)S(1)} collective-permute-done((bf16[26,1,8,256]{3,2,0,1:T(8,128)(2,1)S(1)}, bf16[26,1,8,256]{3,2,0,1:T(8,128)(2,1)S(1)}, u32[]{:S(2)}, u32[]{:S(2)}) %collective-permute-start) | collective-permute-done | bytes 106528 | tf_op jit(solution)/shard_map/ppermute | solution.py:28
  11.2 6.2 %collective-permute-start.1 = (bf16[26,2,8,256]{3,2,0,1:T(8,128)(2,1)S(1)}, bf16[26,2,8,256]{3,2,0,1:T(8,128)(2,1)S(1)}, u32[]{:S(2)}, u32[]{:S(2)}) collective-permute-start(bf16[26,2,8,256]{3,2,0,1:T(8,128)(2,1)S(1)} %maximum_bitcast_fusion), channel_id=1, source_target_pairs={{0,32},{1,97},{2,34},{3,99},{4,36},{5,101},{6,38},{7,103},{8,40},{... | collective-permute-start | bytes 638984 | tf_op jit(solution)/shard_map/ppermute | solution.py:28
  17.4 5.5 %collective-permute-done.1 = bf16[26,2,8,256]{3,2,0,1:T(8,128)(2,1)S(1)} collective-permute-done((bf16[26,2,8,256]{3,2,0,1:T(8,128)(2,1)S(1)}, bf16[26,2,8,256]{3,2,0,1:T(8,128)(2,1)S(1)}, u32[]{:S(2)}, u32[]{:S(2)}) %collective-permute-start.1) | collective-permute-done | bytes 213024 | tf_op jit(solution)/shard_map/ppermute | solution.py:28
  23.6 1.2 copy.8
  24.8 1.2 reshape.47
  26.0 4.4 %collective-permute-done.2 = bf16[26,4,8,256]{3,2,1,0:T(8,128)(2,1)S(1)} collective-permute-done((bf16[26,4,8,256]{3,2,1,0:T(8,128)(2,1)S(1)}, bf16[26,4,8,256]{3,2,1,0:T(8,128)(2,1)S(1)}, u32[]{:S(2)}, u32[]{:S(2)}) %collective-permute-start.2) | collective-permute-done | bytes 426016 | tf_op jit(solution)/shard_map/ppermute | solution.py:28
  30.7 2.6 %collective-permute-start.8 = (bf16[17,8,8,256]{3,2,1,0:T(8,128)(2,1)S(1)}, bf16[17,8,8,256]{3,2,1,0:T(8,128)(2,1)S(1)}, u32[]{:S(2)}, u32[]{:S(2)}) collective-permute-start(bf16[17,8,8,256]{3,2,1,0:T(8,128)(2,1)S(1)} %get-tuple-element.18), channel_id=1, source_target_pairs={{0,4},{1,13},{2,6},{3,15},{4,0},{5,9},{6,2},{7,11},{8,12},{9,5},{1... | collective-permute-start | bytes 1671176 | tf_op jit(solution)/shard_map/ppermute | solution.py:28
  33.3 2.8 %collective-permute-start.3 = (bf16[9,8,8,256]{3,2,1,0:T(8,128)(2,1)S(1)}, bf16[9,8,8,256]{3,2,1,0:T(8,128)(2,1)S(1)}, u32[]{:S(2)}, u32[]{:S(2)}) collective-permute-start(bf16[9,8,8,256]{3,2,1,0:T(8,128)(2,1)S(1)} %get-tuple-element.20), channel_id=1, source_target_pairs={{0,128},{1,131},{2,130},{3,129},{4,132},{5,135},{6,134},{7,133},{8... | collective-permute-start | bytes 884744 | tf_op jit(solution)/shard_map/ppermute | solution.py:28
  36.1 4.5 %collective-permute-done.8 = bf16[17,8,8,256]{3,2,1,0:T(8,128)(2,1)S(1)} collective-permute-done((bf16[17,8,8,256]{3,2,1,0:T(8,128)(2,1)S(1)}, bf16[17,8,8,256]{3,2,1,0:T(8,128)(2,1)S(1)}, u32[]{:S(2)}, u32[]{:S(2)}) %collective-permute-start.8) | collective-permute-done | bytes 557088 | tf_op jit(solution)/shard_map/ppermute | solution.py:28
  40.9 2.7 %collective-permute-start.10 = (bf16[2,17,8,8,256]{4,3,2,1,0:T(8,128)(2,1)S(1)}, bf16[2,17,8,8,256]{4,3,2,1,0:T(8,128)(2,1)}, u32[]{:S(2)}, u32[]{:S(2)}) collective-permute-start(bf16[2,17,8,8,256]{4,3,2,1,0:T(8,128)(2,1)S(1)} %pad_maximum_fusion.1.refs_0_), channel_id=1, source_target_pairs={{0,128},{1,131},{2,130},{3,129},{4,132},{5,135},{6,134},{7,133},{8... | collective-permute-start | bytes 3342344 | tf_op jit(solution)/shard_map/ppermute | solution.py:28
  43.6 12.9 %all-to-all-start = ((bf16[64,16,512]{2,1,0:T(8,128)(2,1)}), bf16[64,16,512]{2,1,0:T(8,128)(2,1)}, u32[]{:S(2)}, u32[]{:S(2)}) async-start(bf16[64,16,512]{2,1,0:T(8,128)(2,1)} %reshape.47), calls=%async_computation | async-start | bytes 2097152 | tf_op jit(solution)/shard_map/all_to_all | solution.py:228
  56.9 10.1 %collective-permute-done.4 = bf16[2,9,8,8,256]{4,3,2,1,0:T(8,128)(2,1)S(1)} collective-permute-done((bf16[2,9,8,8,256]{4,3,2,1,0:T(8,128)(2,1)S(1)}, bf16[2,9,8,8,256]{4,3,2,1,0:T(8,128)(2,1)S(1)}, u32[]{:S(2)}, u32[]{:S(2)}) %collective-permute-start.4) | collective-permute-done | bytes 589856 | tf_op jit(solution)/shard_map/ppermute | solution.py:28
  67.7 2.6 %collective-permute-start.11 = (bf16[2,17,8,8,256]{4,3,2,1,0:T(8,128)(2,1)S(1)}, bf16[2,17,8,8,256]{4,3,2,1,0:T(8,128)(2,1)}, u32[]{:S(2)}, u32[]{:S(2)}) collective-permute-start(bf16[2,17,8,8,256]{4,3,2,1,0:T(8,128)(2,1)S(1)} %collective-permute-done.9.refs_1_), channel_id=1, source_target_pairs={{0,128},{1,131},{2,130},{3,129},{4,132},{5,135},{6,134},{7,133},{8... | collective-permute-start | bytes 3342344 | tf_op jit(solution)/shard_map/ppermute | solution.py:28
  70.3 15.5 %all-to-all-done = bf16[64,16,512]{2,1,0:T(8,128)(2,1)} async-done(((bf16[64,16,512]{2,1,0:T(8,128)(2,1)}), bf16[64,16,512]{2,1,0:T(8,128)(2,1)}, u32[]{:S(2)}, u32[]{:S(2)}) %all-to-all-start) | async-done | bytes 1048608 | tf_op jit(solution)/shard_map/all_to_all | solution.py:228
  87.2 2.6 %collective-permute-start.15 = (bf16[2,17,8,8,256]{4,3,2,1,0:T(8,128)(2,1)}, bf16[2,17,8,8,256]{4,3,2,1,0:T(8,128)(2,1)}, u32[]{:S(2)}, u32[]{:S(2)}) collective-permute-start(bf16[2,17,8,8,256]{4,3,2,1,0:T(8,128)(2,1)} %collective-permute-done.11.refs_3_), channel_id=1, source_target_pairs={{0,1},{1,0},{2,3},{3,2},{4,5},{5,4},{6,7},{7,6},{8,9},{9,8},{10,11... | collective-permute-start | bytes 3342344 | tf_op jit(solution)/shard_map/ppermute | solution.py:28
  90.5 10.1 %shard_map.55.cells = bf16[16,64,512]{2,1,0:T(8,128)(2,1)} custom-call(s32[3]{0:T(128)} %pad_add_fusion.where, bf16[16,64,512]{2,1,0:T(8,128)(2,1)} %bitcast.27.cells, bf16[2,2,9,8,8,256]{5,4,3,2,1,0:T(8,128)(2,1)} %copy-done.2, bf16[2,2,9,8,8,256]{5,4,3,2,1,0:T(8,128)(2,1)} %collective-permute-done.5.refs_1_, ...), custom_call_target="tpu_custom_call" | custom-call | flops 1000 | bytes 1000 | tf_op jit(solution)/shard_map/pallas_call | solution.py:134
  100.6 10.1 %shard_map.56.cells = bf16[16,64,512]{2,1,0:T(8,128)(2,1)} custom-call(s32[3]{0:T(128)} %pad_add_fusion.where, bf16[16,64,512]{2,1,0:T(8,128)(2,1)} %shard_map.55.cells, bf16[2,17,8,8,256]{4,3,2,1,0:T(8,128)(2,1)} %copy-done.1, bf16[2,17,8,8,256]{4,3,2,1,0:T(8,128)(2,1)} %copy-done.3, bf16[2,17,8,8,256]{4,3,2,1,0:T(8,128)(2,1)} %collective-permute-done.10.refs_2_, ...), custom_call_target="tpu_custom_call" | custom-call | flops 1000 | bytes 1000 | tf_op jit(solution)/shard_map/pallas_call | solution.py:134
  110.8 9.8 %shard_map.57 = bf16[16,64,512]{2,1,0:T(8,128)(2,1)} custom-call(bf16[16,64,512]{2,1,0:T(8,128)(2,1)} %shard_map.56.cells, bf16[2,17,8,8,256]{4,3,2,1,0:T(8,128)(2,1)} %copy-done.1, bf16[2,17,8,8,256]{4,3,2,1,0:T(8,128)(2,1)} %copy-done.3, bf16[2,17,8,8,256]{4,3,2,1,0:T(8,128)(2,1)} %collective-permute-done.10.refs_2_, ...), custom_call_target="tpu_custom_call" | custom-call | flops 1000 | bytes 1000 | tf_op jit(solution)/shard_map/pallas_call | solution.py:194
  120.6 38.2 %all_to_all.10 = bf16[64,16,512]{2,1,0:T(8,128)(2,1)S(1)} all-to-all(bf16[64,16,512]{2,1,0:T(8,128)(2,1)} %bitcast.63), channel_id=1, replica_groups=mesh['ylo'=2,'z'=8,'x'=4,'yhi'=2,'core'=2] {'ylo','z','yhi','core'}, dimensions={0} | all-to-all | bytes 2097152 | tf_op jit(solution)/shard_map/all_to_all | solution.py:246
  159.3 1.2 copy.11
  160.5 1.2 reshape.51
  (49 shorter events, 5.4 us)
Async XLA Ops:
  0.0 0.8 copy-start
  2.3 8.8 %collective-permute-start = (bf16[26,1,8,256]{3,2,0,1:T(8,128)(2,1)S(1)}, bf16[26,1,8,256]{3,2,0,1:T(8,128)(2,1)S(1)}, u32[]{:S(2)}, u32[]{:S(2)}) collective-permute-start(bf16[26,1,8,256]{3,2,0,1:T(8,128)(2,1)S(1)} %maximum_bitcast_fusion.1), channel_id=1, source_target_pairs={{0,64},{1,65},{2,66},{3,67},{4,68},{5,69},{6,70},{7,71},{8,72},{9,... | collective-permute-start | bytes 319496 | tf_op jit(solution)/shard_map/ppermute | solution.py:28
  11.2 11.7 %collective-permute-start.1 = (bf16[26,2,8,256]{3,2,0,1:T(8,128)(2,1)S(1)}, bf16[26,2,8,256]{3,2,0,1:T(8,128)(2,1)S(1)}, u32[]{:S(2)}, u32[]{:S(2)}) collective-permute-start(bf16[26,2,8,256]{3,2,0,1:T(8,128)(2,1)S(1)} %maximum_bitcast_fusion), channel_id=1, source_target_pairs={{0,32},{1,97},{2,34},{3,99},{4,36},{5,101},{6,38},{7,103},{8,40},{... | collective-permute-start | bytes 638984 | tf_op jit(solution)/shard_map/ppermute | solution.py:28
  17.4 5.8 %copy-start.4 = (bf16[2,4,128,512]{3,2,1,0:T(8,128)(2,1)S(1)}, bf16[2,4,128,512]{3,2,1,0:T(8,128)(2,1)}, u32[]{:S(2)}) copy-start(bf16[2,4,128,512]{3,2,1,0:T(8,128)(2,1)} %param.5) | copy-start | bytes 3145732
  23.0 7.4 %collective-permute-start.2 = (bf16[26,4,8,256]{3,2,1,0:T(8,128)(2,1)S(1)}, bf16[26,4,8,256]{3,2,1,0:T(8,128)(2,1)S(1)}, u32[]{:S(2)}, u32[]{:S(2)}) collective-permute-start(bf16[26,4,8,256]{3,2,1,0:T(8,128)(2,1)S(1)} %bitcast.66), channel_id=1, source_target_pairs={{0,16},{1,113},{2,18},{3,115},{4,20},{5,117},{6,22},{7,119},{8,24}... | collective-permute-start | bytes 1277960 | tf_op jit(solution)/shard_map/ppermute | solution.py:28
  30.7 10.0 %collective-permute-start.8 = (bf16[17,8,8,256]{3,2,1,0:T(8,128)(2,1)S(1)}, bf16[17,8,8,256]{3,2,1,0:T(8,128)(2,1)S(1)}, u32[]{:S(2)}, u32[]{:S(2)}) collective-permute-start(bf16[17,8,8,256]{3,2,1,0:T(8,128)(2,1)S(1)} %get-tuple-element.18), channel_id=1, source_target_pairs={{0,4},{1,13},{2,6},{3,15},{4,0},{5,9},{6,2},{7,11},{8,12},{9,5},{1... | collective-permute-start | bytes 1671176 | tf_op jit(solution)/shard_map/ppermute | solution.py:28
  33.3 23.2 %collective-permute-start.3 = (bf16[9,8,8,256]{3,2,1,0:T(8,128)(2,1)S(1)}, bf16[9,8,8,256]{3,2,1,0:T(8,128)(2,1)S(1)}, u32[]{:S(2)}, u32[]{:S(2)}) collective-permute-start(bf16[9,8,8,256]{3,2,1,0:T(8,128)(2,1)S(1)} %get-tuple-element.20), channel_id=1, source_target_pairs={{0,128},{1,131},{2,130},{3,129},{4,132},{5,135},{6,134},{7,133},{8... | collective-permute-start | bytes 884744 | tf_op jit(solution)/shard_map/ppermute | solution.py:28
  40.8 45.0 %copy-start.1 = (bf16[2,17,8,8,256]{4,3,2,1,0:T(8,128)(2,1)}, bf16[2,17,8,8,256]{4,3,2,1,0:T(8,128)(2,1)S(1)}, u32[]{:S(2)}) copy-start(bf16[2,17,8,8,256]{4,3,2,1,0:T(8,128)(2,1)S(1)} %pad_maximum_fusion.1.refs_0_) | copy-start | bytes 3342340
  40.8 26.9 %collective-permute-start.9 = (bf16[2,17,8,8,256]{4,3,2,1,0:T(8,128)(2,1)S(1)}, bf16[2,17,8,8,256]{4,3,2,1,0:T(8,128)(2,1)S(1)}, u32[]{:S(2)}, u32[]{:S(2)}) collective-permute-start(bf16[2,17,8,8,256]{4,3,2,1,0:T(8,128)(2,1)S(1)} %pad_maximum_fusion.1.refs_0_), channel_id=1, source_target_pairs={{0,12},{1,5},{2,14},{3,7},{4,8},{5,1},{6,10},{7,3},{8,4},{9,13},{1... | collective-permute-start | bytes 3342344 | tf_op jit(solution)/shard_map/ppermute | solution.py:28
  40.9 26.8 %collective-permute-start.10 = (bf16[2,17,8,8,256]{4,3,2,1,0:T(8,128)(2,1)S(1)}, bf16[2,17,8,8,256]{4,3,2,1,0:T(8,128)(2,1)}, u32[]{:S(2)}, u32[]{:S(2)}) collective-permute-start(bf16[2,17,8,8,256]{4,3,2,1,0:T(8,128)(2,1)S(1)} %pad_maximum_fusion.1.refs_0_), channel_id=1, source_target_pairs={{0,128},{1,131},{2,130},{3,129},{4,132},{5,135},{6,134},{7,133},{8... | collective-permute-start | bytes 3342344 | tf_op jit(solution)/shard_map/ppermute | solution.py:28
  43.6 42.2 %all-to-all-start = ((bf16[64,16,512]{2,1,0:T(8,128)(2,1)}), bf16[64,16,512]{2,1,0:T(8,128)(2,1)}, u32[]{:S(2)}, u32[]{:S(2)}) async-start(bf16[64,16,512]{2,1,0:T(8,128)(2,1)} %reshape.47), calls=%async_computation | async-start | bytes 2097152 | tf_op jit(solution)/shard_map/all_to_all | solution.py:228
  56.6 10.4 %collective-permute-start.4 = (bf16[2,9,8,8,256]{4,3,2,1,0:T(8,128)(2,1)S(1)}, bf16[2,9,8,8,256]{4,3,2,1,0:T(8,128)(2,1)S(1)}, u32[]{:S(2)}, u32[]{:S(2)}) collective-permute-start(bf16[2,9,8,8,256]{4,3,2,1,0:T(8,128)(2,1)S(1)} %get-tuple-element.24), channel_id=1, source_target_pairs={{0,4},{1,13},{2,6},{3,15},{4,0},{5,9},{6,2},{7,11},{8,12},{9,5},{1... | collective-permute-start | bytes 1769480 | tf_op jit(solution)/shard_map/ppermute | solution.py:28
  67.2 23.3 %copy-start.2 = (bf16[2,2,9,8,8,256]{5,4,3,2,1,0:T(8,128)(2,1)}, bf16[2,2,9,8,8,256]{5,4,3,2,1,0:T(8,128)(2,1)S(1)}, u32[]{:S(2)}) copy-start(bf16[2,2,9,8,8,256]{5,4,3,2,1,0:T(8,128)(2,1)S(1)} %pad_maximum_fusion.refs_0_) | copy-start | bytes 3538948
  67.2 18.6 %collective-permute-start.5 = (bf16[2,2,9,8,8,256]{5,4,3,2,1,0:T(8,128)(2,1)S(1)}, bf16[2,2,9,8,8,256]{5,4,3,2,1,0:T(8,128)(2,1)}, u32[]{:S(2)}, u32[]{:S(2)}) collective-permute-start(bf16[2,2,9,8,8,256]{5,4,3,2,1,0:T(8,128)(2,1)S(1)} %pad_maximum_fusion.refs_0_), channel_id=1, source_target_pairs={{0,12},{1,5},{2,14},{3,7},{4,8},{5,1},{6,10},{7,3},{8,4},{9,13},{1... | collective-permute-start | bytes 3538952 | tf_op jit(solution)/shard_map/ppermute | solution.py:28
  67.3 19.1 %collective-permute-start.6 = (bf16[2,2,9,8,8,256]{5,4,3,2,1,0:T(8,128)(2,1)S(1)}, bf16[2,2,9,8,8,256]{5,4,3,2,1,0:T(8,128)(2,1)}, u32[]{:S(2)}, u32[]{:S(2)}) collective-permute-start(bf16[2,2,9,8,8,256]{5,4,3,2,1,0:T(8,128)(2,1)S(1)} %pad_maximum_fusion.refs_0_), channel_id=1, source_target_pairs={{0,1},{1,0},{2,3},{3,2},{4,5},{5,4},{6,7},{7,6},{8,9},{9,8},{10,11... | collective-permute-start | bytes 3538952 | tf_op jit(solution)/shard_map/ppermute | solution.py:28
  67.7 32.9 %copy-start.3 = (bf16[2,17,8,8,256]{4,3,2,1,0:T(8,128)(2,1)}, bf16[2,17,8,8,256]{4,3,2,1,0:T(8,128)(2,1)S(1)}, u32[]{:S(2)}) copy-start(bf16[2,17,8,8,256]{4,3,2,1,0:T(8,128)(2,1)S(1)} %collective-permute-done.9.refs_1_) | copy-start | bytes 3342340
  67.7 19.5 %collective-permute-start.11 = (bf16[2,17,8,8,256]{4,3,2,1,0:T(8,128)(2,1)S(1)}, bf16[2,17,8,8,256]{4,3,2,1,0:T(8,128)(2,1)}, u32[]{:S(2)}, u32[]{:S(2)}) collective-permute-start(bf16[2,17,8,8,256]{4,3,2,1,0:T(8,128)(2,1)S(1)} %collective-permute-done.9.refs_1_), channel_id=1, source_target_pairs={{0,128},{1,131},{2,130},{3,129},{4,132},{5,135},{6,134},{7,133},{8... | collective-permute-start | bytes 3342344 | tf_op jit(solution)/shard_map/ppermute | solution.py:28
  85.8 4.6 %collective-permute-start.7 = (bf16[2,2,9,8,8,256]{5,4,3,2,1,0:T(8,128)(2,1)}, bf16[2,2,9,8,8,256]{5,4,3,2,1,0:T(8,128)(2,1)}, u32[]{:S(2)}, u32[]{:S(2)}) collective-permute-start(bf16[2,2,9,8,8,256]{5,4,3,2,1,0:T(8,128)(2,1)} %collective-permute-done.5.refs_1_), channel_id=1, source_target_pairs={{0,1},{1,0},{2,3},{3,2},{4,5},{5,4},{6,7},{7,6},{8,9},{9,8},{10,11... | collective-permute-start | bytes 3538952 | tf_op jit(solution)/shard_map/ppermute | solution.py:28
  85.8 14.8 %collective-permute-start.12 = (bf16[2,17,8,8,256]{4,3,2,1,0:T(8,128)(2,1)S(1)}, bf16[2,17,8,8,256]{4,3,2,1,0:T(8,128)(2,1)}, u32[]{:S(2)}, u32[]{:S(2)}) collective-permute-start(bf16[2,17,8,8,256]{4,3,2,1,0:T(8,128)(2,1)S(1)} %pad_maximum_fusion.1.refs_0_), channel_id=1, source_target_pairs={{0,1},{1,0},{2,3},{3,2},{4,5},{5,4},{6,7},{7,6},{8,9},{9,8},{10,11... | collective-permute-start | bytes 3342344 | tf_op jit(solution)/shard_map/ppermute | solution.py:28
  86.3 14.3 %collective-permute-start.13 = (bf16[2,17,8,8,256]{4,3,2,1,0:T(8,128)(2,1)S(1)}, bf16[2,17,8,8,256]{4,3,2,1,0:T(8,128)(2,1)}, u32[]{:S(2)}, u32[]{:S(2)}) collective-permute-start(bf16[2,17,8,8,256]{4,3,2,1,0:T(8,128)(2,1)S(1)} %collective-permute-done.9.refs_1_), channel_id=1, source_target_pairs={{0,1},{1,0},{2,3},{3,2},{4,5},{5,4},{6,7},{7,6},{8,9},{9,8},{10,11... | collective-permute-start | bytes 3342344 | tf_op jit(solution)/shard_map/ppermute | solution.py:28
  86.4 14.2 %collective-permute-start.14 = (bf16[2,17,8,8,256]{4,3,2,1,0:T(8,128)(2,1)}, bf16[2,17,8,8,256]{4,3,2,1,0:T(8,128)(2,1)}, u32[]{:S(2)}, u32[]{:S(2)}) collective-permute-start(bf16[2,17,8,8,256]{4,3,2,1,0:T(8,128)(2,1)} %collective-permute-done.10.refs_2_), channel_id=1, source_target_pairs={{0,1},{1,0},{2,3},{3,2},{4,5},{5,4},{6,7},{7,6},{8,9},{9,8},{10,11... | collective-permute-start | bytes 3342344 | tf_op jit(solution)/shard_map/ppermute | solution.py:28
  87.2 13.4 %collective-permute-start.15 = (bf16[2,17,8,8,256]{4,3,2,1,0:T(8,128)(2,1)}, bf16[2,17,8,8,256]{4,3,2,1,0:T(8,128)(2,1)}, u32[]{:S(2)}, u32[]{:S(2)}) collective-permute-start(bf16[2,17,8,8,256]{4,3,2,1,0:T(8,128)(2,1)} %collective-permute-done.11.refs_3_), channel_id=1, source_target_pairs={{0,1},{1,0},{2,3},{3,2},{4,5},{5,4},{6,7},{7,6},{8,9},{9,8},{10,11... | collective-permute-start | bytes 3342344 | tf_op jit(solution)/shard_map/ppermute | solution.py:28

commit v2 on v1

v2 whole, which is shorter than its diff:
```python
import functools

import jax
import jax.numpy as jnp
import numpy as np
from jax import lax
from jax.experimental import pallas as pl
from jax.experimental.pallas import tpu as pltpu
from jax.sharding import Mesh, PartitionSpec as P

AXES = ("ylo", "z", "x", "yhi", "core")
SIZES = (2, 8, 4, 2, 2)
PEERS = ("ylo", "z", "yhi", "core")
ROWS, COLS, PAIR = 16, 32, 2
LINE = COLS * PAIR
CELLS = ROWS * LINE
TAPS = 9
MLP = 8
VMEM_LIMIT = 56 * 1024 * 1024


def moved(array, to):
    pairs = []
    for source, (ylo, z, x, yhi, core) in enumerate(np.ndindex(SIZES)):
        y, z, x, core = to(2 * yhi + ylo, z, x, core)
        y, z, x, core = y % 4, z % 8, x % 4, core % 2
        pairs.append((source, int(np.ravel_multi_index((y % 2, z, x, y // 2, core), SIZES))))
    return lax.ppermute(array, AXES, pairs)


def from_x(piece, turn):
    return moved(piece, lambda y, z, x, c: (y, z, x ^ (3 if c != turn else 1), c))


def from_z(piece, bit):
    def partner(y, z, x, c):
        if bit == 2:
            return y, z ^ 4, x, c
        if bit == 1:
            return y, z ^ (6 if c else 2), x, c
        return y, z + (1 if (z + c) % 2 == 0 else -1), x, c

    return moved(piece, partner)


def joined(mine, theirs, place):
    pair = [jnp.where(place == 0, mine, theirs), jnp.where(place == 0, theirs, mine)]
    n, pieces, rows, width = mine.shape
    return jnp.stack(pair, axis=2).reshape(n, 2 * pieces, rows, width)


def from_y(piece):
    return moved(piece, lambda y, z, x, c: (y + 1 - 2 * c, z, x, c))


def from_core(piece):
    return moved(piece, lambda y, z, x, c: (y, z, x, 1 - c))


def x_slots(x, core):
    first = jnp.where(core == 0, x ^ 1, x ^ 3)
    return x, first, x ^ first ^ (x ^ 2), x ^ 2


def normalized(values):
    return values * lax.rsqrt(jnp.mean(values * values, axis=-1, keepdims=True) + 1e-06)


def weight_copies(split_y, where, sources, kernel, sems):
    x, ylo, core = where[0], where[1], where[2]
    groups = [[], [], []]
    for i in range(3):
        taps = pl.ds(3 * i, 3)
        for far in range(2):
            c = core if far == 0 else 1 - core
            slots = x_slots(x, c)
            for y in range(2):
                y_of = ylo if y == 0 else 1 - ylo
                for part in range(2):
                    for k in range(2):
                        if split_y:
                            source = sources[far * 4 + y * 2 + part].at[k, taps]
                        else:
                            source = sources[far * 2 + part].at[k, y, taps]
                        place = kernel.at[c, taps, y_of, :, slots[part * 2 + k]]
                        groups[i].append(pltpu.make_async_copy(source, place, sems.at[i * 16 + len(groups[i])]))
    return groups


def convolve(step, cells, groups, shifted, kernel, total):
    ch = cells.shape[-1]
    half = ch // 2
    blank = jnp.zeros((step, LINE, 3 * ch), jnp.bfloat16)
    shifted[pl.ds(0, step)] = blank
    shifted[pl.ds(ROWS + step, step)] = blank
    by = step * PAIR

    def fill(r, _):
        raw = cells[r].astype(jnp.float32)
        for c in range(2):
            total[c, pl.ds(pl.multiple_of(r * LINE, LINE), LINE)] = raw[:, c * half : (c + 1) * half]
        row = normalized(raw)
        edge = jnp.zeros((by, ch), jnp.float32)
        if by % 8 == 0:
            before = jnp.concatenate([edge, row[: LINE - by]], axis=0)
            after = jnp.concatenate([row[by:], edge], axis=0)
        else:
            column = lax.broadcasted_iota(jnp.int32, (LINE, ch), 0)
            before = jnp.where(column >= by, pltpu.roll(row, by, 0), 0.0)
            after = jnp.where(column < LINE - by, pltpu.roll(row, LINE - by, 0), 0.0)
        for j, values in enumerate((before, row, after)):
            shifted[r + step, :, j * ch : (j + 1) * ch] = values.astype(jnp.bfloat16)
        return 0

    lax.fori_loop(0, ROWS, fill, 0)
    for i in range(3):
        for copy in groups[i]:
            copy.wait()
        window = shifted[pl.ds(i * step, ROWS)].reshape(CELLS, 3 * ch)
        for c in range(2):
            part = kernel[c, pl.ds(3 * i, 3)].reshape(3 * ch, half)
            total[c] += jnp.dot(window, part, preferred_element_type=jnp.float32)


def store(total, out):
    half = total.shape[-1]
    for c in range(2):
        out[:, :, c * half : (c + 1) * half] = total[c].astype(jnp.bfloat16).reshape(ROWS, LINE, half)


def near_kernel(step, where, cells, *refs):
    weights, (out, shifted, kernel, total, sems) = refs[:4], refs[4:]
    groups = weight_copies(False, where, weights, kernel, sems)
    for copy in sum(groups, []):
        copy.start()
    convolve(step, cells, groups, shifted, kernel, total)
    store(total, out)


def far_kernel(step, where, cells, *refs):
    pieces, (out, shifted, kernel, total, up_rows, down_rows, sems, mlp_sems) = refs[:8], refs[8:]
    ch = cells.shape[-1]
    half = ch // 2
    groups = weight_copies(True, where, pieces, kernel, sems)
    for copy in sum(groups, []):
        copy.start()
    mlp = []
    for n, piece in enumerate(pieces):
        mlp.append([])
        for c in range(2):
            for kind, rows in enumerate((up_rows, down_rows)):
                blocks = piece.at[:, pl.ds(TAPS + 4 * c + 2 * kind, 2)]
                place = rows.at[n, :, :, :, :, pl.ds(c * half, half)]
                mlp[n].append(pltpu.make_async_copy(blocks, place, mlp_sems.at[n * 4 + 2 * c + kind]))
    for copy in sum(mlp, []):
        copy.start()
    convolve(step, cells, groups, shifted, kernel, total)
    squares = 0.0
    for c in range(2):
        value = total[c].astype(jnp.bfloat16).astype(jnp.float32)
        total[c] = value
        squares = squares + jnp.sum(value * value, axis=-1, keepdims=True)
    scale = lax.rsqrt(squares / ch + 1e-06)
    rows = jnp.concatenate([(total[c] * scale).astype(jnp.bfloat16) for c in range(2)], axis=1)
    for n in range(0, 8, 2):
        for copy in mlp[n] + mlp[n + 1]:
            copy.wait()
        up = up_rows[n : n + 2].reshape(-1, ch)
        down = down_rows[n : n + 2].reshape(-1, ch)
        hidden = lax.dot_general(rows, up, (((1,), (1,)), ((), ())), preferred_element_type=jnp.float32)
        hidden = jax.nn.gelu(hidden).astype(jnp.bfloat16)
        for c in range(2):
            total[c] += jnp.dot(hidden, down[:, c * half : (c + 1) * half], preferred_element_type=jnp.float32)
    store(total, out)


def block(kernel, cells, weights, step, where, mlp):
    ch = cells.shape[-1]
    whole = pl.BlockSpec(memory_space=pltpu.VMEM)
    scratch = [
        pltpu.VMEM((ROWS + 2 * step, LINE, 3 * ch), jnp.bfloat16),
        pltpu.VMEM((2, TAPS, 2, 8, 4, 8, ch // 2), jnp.bfloat16),
        pltpu.VMEM((2, CELLS, ch // 2), jnp.float32),
    ]
    semaphores = [pltpu.SemaphoreType.DMA((48,))]
    if mlp:
        scratch += [pltpu.VMEM((8, 2, 2, 8, 8, ch), jnp.bfloat16)] * 2
        semaphores += [pltpu.SemaphoreType.DMA((32,))]
    return pl.pallas_call(
        functools.partial(kernel, step),
        out_shape=jax.ShapeDtypeStruct(cells.shape, jnp.bfloat16),
        in_specs=[pl.BlockSpec(memory_space=pltpu.SMEM), whole] + [pl.BlockSpec(memory_space=pl.ANY)] * len(weights),
        out_specs=whole,
        scratch_shapes=scratch + semaphores,
        compiler_params=pltpu.CompilerParams(vmem_limit_bytes=VMEM_LIMIT),
        cost_estimate=pl.CostEstimate(flops=1000, bytes_accessed=1000, transcendentals=0),
    )(where, cells, *weights)


def shards(inputs, tight, wide, up, down):
    core = lax.axis_index("core")
    where = jnp.stack([lax.axis_index("x"), lax.axis_index("ylo"), core]).astype(jnp.int32)
    s, i, cols, ch = inputs.shape
    half, n = ch // 2, down.shape[0] // 2
    kernels = jnp.concatenate([tight.reshape(TAPS, 8, ch), wide.reshape(TAPS, 8, ch)])
    kernels = lax.dynamic_slice_in_dim(kernels, core * half, half, axis=2)
    mlp = jnp.stack([lax.dynamic_slice_in_dim(up.T, core * n, n, 0), lax.dynamic_slice_in_dim(down, core * n, n, 0)])
    mlp = jnp.stack([mlp[:, :, :half], mlp[:, :, half:]]).reshape(MLP, 8, half)
    shard = jnp.concatenate([kernels, mlp])

    cells = inputs.reshape(s, i, 8, 8, PAIR, ch).transpose(0, 1, 3, 2, 4, 5).reshape(64, 16, ch)
    shard = shard.reshape(-1, 1, 8, half)
    for bit in (2, 1, 0):
        shard = joined(shard, from_z(shard, bit), (lax.axis_index("z") >> bit) & 1)
    shard = shard.reshape(-1, 8, 8, half)
    shard, cells = lax.optimization_barrier((shard, cells))
    cells = lax.all_to_all(cells, PEERS, 0, 0).reshape(ROWS, LINE, ch)

    near_half = jnp.stack([shard[:TAPS], from_y(shard[:TAPS])])
    rest = shard[TAPS:]
    first = jnp.stack([rest, from_x(rest, 0)])
    second = from_x(first, 1)
    first_y = from_y(first)
    t_first = jnp.stack([near_half, from_x(near_half, 0)])
    t_second = from_x(t_first, 1)
    t_second, cells = lax.optimization_barrier((t_second, cells))
    tight_parts = [t_first, t_second, from_core(t_first), from_core(t_second)]
    second, first_y = lax.optimization_barrier((second, first_y))
    own = [first, second, first_y, from_y(second)]
    parts = own + [from_core(piece) for piece in own]

    near = block(near_kernel, cells, tight_parts, 1, where, False)
    out = block(far_kernel, near, parts, 4, where, True)
    out = lax.all_to_all(out.reshape(64, 16, ch), PEERS, 0, 0)
    return out.reshape(s, i, 8, 8, PAIR, ch).transpose(0, 1, 3, 2, 4, 5).reshape(inputs.shape)


def solution(mesh):
    grid = Mesh(mesh.devices.reshape(SIZES), AXES)
    rows, columns = ("ylo", "z", "x"), ("yhi", "core")
    placed = (
        P(None, rows, columns, None),
        P(None, None, rows, None),
        P(None, None, rows, None),
        P(None, rows),
        P(rows, None),
    )
    return jax.shard_map(shards, mesh=grid, in_specs=placed, out_specs=P(None, rows, columns, None), check_vma=False)
```

time: 162 us -> 158 us (0.975)
  Pallas kernels: 30.1 us -> 26.5 us
    pallas_call x3 -> x2, Pallas kernels: 30.1 us -> 26.5 us  [block(): pl.pallas_call(functools.partial(kernel, step), out_shape=jax.ShapeDtypeS...]
where the time goes in v2:
time: 158 us
  waiting for transfers between devices  43.4 us (27%)
  starting transfers between devices  40.2 us (25%)
  blocking collectives  38.1 us (24%)
  Pallas kernels  26.5 us (17%)
  local copies, waits for them, and re-layouts  7.37 us (5%)
  other arithmetic  2.05 us (1%)
    all_to_all x1, blocking collectives, shards(): out = lax.all_to_all(out.reshape(64, 16, ch), PEERS, 0, 0)  38.1 us
    ppermute x16, waiting for transfers between devices, moved(): return lax.ppermute(array, AXES, pairs)  27.7 us
    ppermute x16, starting transfers between devices, moved(): return lax.ppermute(array, AXES, pairs)  27.4 us
    pallas_call x2, Pallas kernels, block(): pl.pallas_call(functools.partial(kernel, step), out_shape=jax.ShapeDtypeS...  26.5 us
    all_to_all x1, waiting for transfers between devices, shards(): cells = lax.all_to_all(cells, PEERS, 0, 0).reshape(ROWS, LINE, ch)  15.7 us
    all_to_all x1, starting transfers between devices, shards(): cells = lax.all_to_all(cells, PEERS, 0, 0).reshape(ROWS, LINE, ch)  12.8 us
  transfers between devices with their start and end apart: 17, of which 7 were waited for; matrix products, arithmetic and copies ran while one was open for 2% of the time, Pallas kernels for 6%

profile of v2, /device:TPU:33, one launch (start us, length us, event | category | flops | bytes accessed | tf_op | source)
XLA Modules:
  0.0 157.8 jit_solution(4096629752459488177)
XLA Ops:
  0.0 0.8 copy-done
  0.8 0.7 dynamic-slice_bitcast_fusion
  1.5 0.8 fusion
  2.3 6.1 %collective-permute-start = (bf16[26,1,8,256]{3,2,0,1:T(8,128)(2,1)S(1)}, bf16[26,1,8,256]{3,2,0,1:T(8,128)(2,1)S(1)}, u32[]{:S(2)}, u32[]{:S(2)}) collective-permute-start(bf16[26,1,8,256]{3,2,0,1:T(8,128)(2,1)S(1)} %maximum_bitcast_fusion.1), channel_id=1, source_target_pairs={{0,64},{1,65},{2,66},{3,67},{4,68},{5,69},{6,70},{7,71},{8,72},{9,... | collective-permute-start | bytes 319496 | tf_op jit(solution)/shard_map/ppermute | solution.py:28
  8.4 2.7 %collective-permute-done = bf16[26,1,8,256]{3,2,0,1:T(8,128)(2,1)S(1)} collective-permute-done((bf16[26,1,8,256]{3,2,0,1:T(8,128)(2,1)S(1)}, bf16[26,1,8,256]{3,2,0,1:T(8,128)(2,1)S(1)}, u32[]{:S(2)}, u32[]{:S(2)}) %collective-permute-start) | collective-permute-done | bytes 106528 | tf_op jit(solution)/shard_map/ppermute | solution.py:28
  11.2 6.2 %collective-permute-start.1 = (bf16[26,2,8,256]{3,2,0,1:T(8,128)(2,1)S(1)}, bf16[26,2,8,256]{3,2,0,1:T(8,128)(2,1)S(1)}, u32[]{:S(2)}, u32[]{:S(2)}) collective-permute-start(bf16[26,2,8,256]{3,2,0,1:T(8,128)(2,1)S(1)} %maximum_bitcast_fusion), channel_id=1, source_target_pairs={{0,32},{1,97},{2,34},{3,99},{4,36},{5,101},{6,38},{7,103},{8,40},{... | collective-permute-start | bytes 638984 | tf_op jit(solution)/shard_map/ppermute | solution.py:28
  17.4 5.5 %collective-permute-done.1 = bf16[26,2,8,256]{3,2,0,1:T(8,128)(2,1)S(1)} collective-permute-done((bf16[26,2,8,256]{3,2,0,1:T(8,128)(2,1)S(1)}, bf16[26,2,8,256]{3,2,0,1:T(8,128)(2,1)S(1)}, u32[]{:S(2)}, u32[]{:S(2)}) %collective-permute-start.1) | collective-permute-done | bytes 213024 | tf_op jit(solution)/shard_map/ppermute | solution.py:28
  23.6 1.2 copy.8
  24.8 1.2 reshape.47
  26.0 4.4 %collective-permute-done.2 = bf16[26,4,8,256]{3,2,1,0:T(8,128)(2,1)S(1)} collective-permute-done((bf16[26,4,8,256]{3,2,1,0:T(8,128)(2,1)S(1)}, bf16[26,4,8,256]{3,2,1,0:T(8,128)(2,1)S(1)}, u32[]{:S(2)}, u32[]{:S(2)}) %collective-permute-start.2) | collective-permute-done | bytes 426016 | tf_op jit(solution)/shard_map/ppermute | solution.py:28
  30.7 2.6 %collective-permute-start.8 = (bf16[17,8,8,256]{3,2,1,0:T(8,128)(2,1)S(1)}, bf16[17,8,8,256]{3,2,1,0:T(8,128)(2,1)S(1)}, u32[]{:S(2)}, u32[]{:S(2)}) collective-permute-start(bf16[17,8,8,256]{3,2,1,0:T(8,128)(2,1)S(1)} %get-tuple-element.18), channel_id=1, source_target_pairs={{0,4},{1,13},{2,6},{3,15},{4,0},{5,9},{6,2},{7,11},{8,12},{9,5},{1... | collective-permute-start | bytes 1671176 | tf_op jit(solution)/shard_map/ppermute | solution.py:28
  33.3 2.8 %collective-permute-start.3 = (bf16[9,8,8,256]{3,2,1,0:T(8,128)(2,1)S(1)}, bf16[9,8,8,256]{3,2,1,0:T(8,128)(2,1)S(1)}, u32[]{:S(2)}, u32[]{:S(2)}) collective-permute-start(bf16[9,8,8,256]{3,2,1,0:T(8,128)(2,1)S(1)} %get-tuple-element.20), channel_id=1, source_target_pairs={{0,128},{1,131},{2,130},{3,129},{4,132},{5,135},{6,134},{7,133},{8... | collective-permute-start | bytes 884744 | tf_op jit(solution)/shard_map/ppermute | solution.py:28
  36.1 4.5 %collective-permute-done.8 = bf16[17,8,8,256]{3,2,1,0:T(8,128)(2,1)S(1)} collective-permute-done((bf16[17,8,8,256]{3,2,1,0:T(8,128)(2,1)S(1)}, bf16[17,8,8,256]{3,2,1,0:T(8,128)(2,1)S(1)}, u32[]{:S(2)}, u32[]{:S(2)}) %collective-permute-start.8) | collective-permute-done | bytes 557088 | tf_op jit(solution)/shard_map/ppermute | solution.py:28
  40.9 2.7 %collective-permute-start.10 = (bf16[2,17,8,8,256]{4,3,2,1,0:T(8,128)(2,1)S(1)}, bf16[2,17,8,8,256]{4,3,2,1,0:T(8,128)(2,1)}, u32[]{:S(2)}, u32[]{:S(2)}) collective-permute-start(bf16[2,17,8,8,256]{4,3,2,1,0:T(8,128)(2,1)S(1)} %pad_maximum_fusion.1.refs_0_), channel_id=1, source_target_pairs={{0,128},{1,131},{2,130},{3,129},{4,132},{5,135},{6,134},{7,133},{8... | collective-permute-start | bytes 3342344 | tf_op jit(solution)/shard_map/ppermute | solution.py:28
  43.6 12.8 %all-to-all-start = ((bf16[64,16,512]{2,1,0:T(8,128)(2,1)}), bf16[64,16,512]{2,1,0:T(8,128)(2,1)S(1)}, u32[]{:S(2)}, u32[]{:S(2)}) async-start(bf16[64,16,512]{2,1,0:T(8,128)(2,1)} %reshape.47), calls=%async_computation | async-start | bytes 2097152 | tf_op jit(solution)/shard_map/all_to_all | solution.py:217
  56.7 10.0 %collective-permute-done.4 = bf16[2,9,8,8,256]{4,3,2,1,0:T(8,128)(2,1)S(1)} collective-permute-done((bf16[2,9,8,8,256]{4,3,2,1,0:T(8,128)(2,1)S(1)}, bf16[2,9,8,8,256]{4,3,2,1,0:T(8,128)(2,1)S(1)}, u32[]{:S(2)}, u32[]{:S(2)}) %collective-permute-start.4) | collective-permute-done | bytes 589856 | tf_op jit(solution)/shard_map/ppermute | solution.py:28
  67.5 2.5 %collective-permute-start.11 = (bf16[2,17,8,8,256]{4,3,2,1,0:T(8,128)(2,1)}, bf16[2,17,8,8,256]{4,3,2,1,0:T(8,128)(2,1)}, u32[]{:S(2)}, u32[]{:S(2)}) collective-permute-start(bf16[2,17,8,8,256]{4,3,2,1,0:T(8,128)(2,1)} %collective-permute-done.9.refs_1_), channel_id=1, source_target_pairs={{0,128},{1,131},{2,130},{3,129},{4,132},{5,135},{6,134},{7,133},{8... | collective-permute-start | bytes 3342344 | tf_op jit(solution)/shard_map/ppermute | solution.py:28
  70.0 15.7 %all-to-all-done = bf16[64,16,512]{2,1,0:T(8,128)(2,1)S(1)} async-done(((bf16[64,16,512]{2,1,0:T(8,128)(2,1)}), bf16[64,16,512]{2,1,0:T(8,128)(2,1)S(1)}, u32[]{:S(2)}, u32[]{:S(2)}) %all-to-all-start) | async-done | bytes 1048608 | tf_op jit(solution)/shard_map/all_to_all | solution.py:217
  87.3 2.4 %collective-permute-start.15 = (bf16[2,17,8,8,256]{4,3,2,1,0:T(8,128)(2,1)}, bf16[2,17,8,8,256]{4,3,2,1,0:T(8,128)(2,1)}, u32[]{:S(2)}, u32[]{:S(2)}) collective-permute-start(bf16[2,17,8,8,256]{4,3,2,1,0:T(8,128)(2,1)} %collective-permute-done.11.refs_3_), channel_id=1, source_target_pairs={{0,1},{1,0},{2,3},{3,2},{4,5},{5,4},{6,7},{7,6},{8,9},{9,8},{10,11... | collective-permute-start | bytes 3342344 | tf_op jit(solution)/shard_map/ppermute | solution.py:28
  90.4 10.0 %shard_map.55.cells = bf16[16,64,512]{2,1,0:T(8,128)(2,1)} custom-call(s32[3]{0:T(128)} %pad_add_fusion.where, bf16[16,64,512]{2,1,0:T(8,128)(2,1)} %bitcast.63, bf16[2,2,9,8,8,256]{5,4,3,2,1,0:T(8,128)(2,1)} %copy-done.1, bf16[2,2,9,8,8,256]{5,4,3,2,1,0:T(8,128)(2,1)} %collective-permute-done.5.refs_1_, ...), custom_call_target="tpu_custom_call" | custom-call | flops 1000 | bytes 1000 | tf_op jit(solution)/shard_map/pallas_call | solution.py:189
  100.5 16.4 %shard_map.56 = bf16[16,64,512]{2,1,0:T(8,128)(2,1)} custom-call(s32[3]{0:T(128)} %pad_add_fusion.where, bf16[16,64,512]{2,1,0:T(8,128)(2,1)} %shard_map.55.cells, bf16[2,17,8,8,256]{4,3,2,1,0:T(8,128)(2,1)} %copy-done.2, bf16[2,17,8,8,256]{4,3,2,1,0:T(8,128)(2,1)} %collective-permute-done.9.refs_1_, ...), custom_call_target="tpu_custom_call" | custom-call | flops 1000 | bytes 1000 | tf_op jit(solution)/shard_map/pallas_call | solution.py:189
  116.9 38.1 %all_to_all.10 = bf16[64,16,512]{2,1,0:T(8,128)(2,1)S(1)} all-to-all(bf16[64,16,512]{2,1,0:T(8,128)(2,1)} %bitcast.64), channel_id=1, replica_groups=mesh['ylo'=2,'z'=8,'x'=4,'yhi'=2,'core'=2] {'ylo','z','yhi','core'}, dimensions={0} | all-to-all | bytes 2097152 | tf_op jit(solution)/shard_map/all_to_all | solution.py:234
  155.4 1.2 copy.11
  156.6 1.2 reshape.51
  (48 shorter events, 5.0 us)
Async XLA Ops:
  0.0 0.8 copy-start
  2.3 8.8 %collective-permute-start = (bf16[26,1,8,256]{3,2,0,1:T(8,128)(2,1)S(1)}, bf16[26,1,8,256]{3,2,0,1:T(8,128)(2,1)S(1)}, u32[]{:S(2)}, u32[]{:S(2)}) collective-permute-start(bf16[26,1,8,256]{3,2,0,1:T(8,128)(2,1)S(1)} %maximum_bitcast_fusion.1), channel_id=1, source_target_pairs={{0,64},{1,65},{2,66},{3,67},{4,68},{5,69},{6,70},{7,71},{8,72},{9,... | collective-permute-start | bytes 319496 | tf_op jit(solution)/shard_map/ppermute | solution.py:28
  11.2 11.7 %collective-permute-start.1 = (bf16[26,2,8,256]{3,2,0,1:T(8,128)(2,1)S(1)}, bf16[26,2,8,256]{3,2,0,1:T(8,128)(2,1)S(1)}, u32[]{:S(2)}, u32[]{:S(2)}) collective-permute-start(bf16[26,2,8,256]{3,2,0,1:T(8,128)(2,1)S(1)} %maximum_bitcast_fusion), channel_id=1, source_target_pairs={{0,32},{1,97},{2,34},{3,99},{4,36},{5,101},{6,38},{7,103},{8,40},{... | collective-permute-start | bytes 638984 | tf_op jit(solution)/shard_map/ppermute | solution.py:28
  17.4 5.8 %copy-start.4 = (bf16[2,4,128,512]{3,2,1,0:T(8,128)(2,1)S(1)}, bf16[2,4,128,512]{3,2,1,0:T(8,128)(2,1)}, u32[]{:S(2)}) copy-start(bf16[2,4,128,512]{3,2,1,0:T(8,128)(2,1)} %param.5) | copy-start | bytes 3145732
  23.0 7.4 %collective-permute-start.2 = (bf16[26,4,8,256]{3,2,1,0:T(8,128)(2,1)S(1)}, bf16[26,4,8,256]{3,2,1,0:T(8,128)(2,1)S(1)}, u32[]{:S(2)}, u32[]{:S(2)}) collective-permute-start(bf16[26,4,8,256]{3,2,1,0:T(8,128)(2,1)S(1)} %bitcast.67), channel_id=1, source_target_pairs={{0,16},{1,113},{2,18},{3,115},{4,20},{5,117},{6,22},{7,119},{8,24}... | collective-permute-start | bytes 1277960 | tf_op jit(solution)/shard_map/ppermute | solution.py:28
  30.7 10.0 %collective-permute-start.8 = (bf16[17,8,8,256]{3,2,1,0:T(8,128)(2,1)S(1)}, bf16[17,8,8,256]{3,2,1,0:T(8,128)(2,1)S(1)}, u32[]{:S(2)}, u32[]{:S(2)}) collective-permute-start(bf16[17,8,8,256]{3,2,1,0:T(8,128)(2,1)S(1)} %get-tuple-element.18), channel_id=1, source_target_pairs={{0,4},{1,13},{2,6},{3,15},{4,0},{5,9},{6,2},{7,11},{8,12},{9,5},{1... | collective-permute-start | bytes 1671176 | tf_op jit(solution)/shard_map/ppermute | solution.py:28
  33.3 23.1 %collective-permute-start.3 = (bf16[9,8,8,256]{3,2,1,0:T(8,128)(2,1)S(1)}, bf16[9,8,8,256]{3,2,1,0:T(8,128)(2,1)S(1)}, u32[]{:S(2)}, u32[]{:S(2)}) collective-permute-start(bf16[9,8,8,256]{3,2,1,0:T(8,128)(2,1)S(1)} %get-tuple-element.20), channel_id=1, source_target_pairs={{0,128},{1,131},{2,130},{3,129},{4,132},{5,135},{6,134},{7,133},{8... | collective-permute-start | bytes 884744 | tf_op jit(solution)/shard_map/ppermute | solution.py:28
  40.8 44.9 %copy-start.2 = (bf16[2,17,8,8,256]{4,3,2,1,0:T(8,128)(2,1)}, bf16[2,17,8,8,256]{4,3,2,1,0:T(8,128)(2,1)S(1)}, u32[]{:S(2)}) copy-start(bf16[2,17,8,8,256]{4,3,2,1,0:T(8,128)(2,1)S(1)} %pad_maximum_fusion.1.refs_0_) | copy-start | bytes 3342340
  40.8 26.7 %collective-permute-start.9 = (bf16[2,17,8,8,256]{4,3,2,1,0:T(8,128)(2,1)S(1)}, bf16[2,17,8,8,256]{4,3,2,1,0:T(8,128)(2,1)}, u32[]{:S(2)}, u32[]{:S(2)}) collective-permute-start(bf16[2,17,8,8,256]{4,3,2,1,0:T(8,128)(2,1)S(1)} %pad_maximum_fusion.1.refs_0_), channel_id=1, source_target_pairs={{0,12},{1,5},{2,14},{3,7},{4,8},{5,1},{6,10},{7,3},{8,4},{9,13},{1... | collective-permute-start | bytes 3342344 | tf_op jit(solution)/shard_map/ppermute | solution.py:28
  40.9 26.6 %collective-permute-start.10 = (bf16[2,17,8,8,256]{4,3,2,1,0:T(8,128)(2,1)S(1)}, bf16[2,17,8,8,256]{4,3,2,1,0:T(8,128)(2,1)}, u32[]{:S(2)}, u32[]{:S(2)}) collective-permute-start(bf16[2,17,8,8,256]{4,3,2,1,0:T(8,128)(2,1)S(1)} %pad_maximum_fusion.1.refs_0_), channel_id=1, source_target_pairs={{0,128},{1,131},{2,130},{3,129},{4,132},{5,135},{6,134},{7,133},{8... | collective-permute-start | bytes 3342344 | tf_op jit(solution)/shard_map/ppermute | solution.py:28
  43.6 42.1 %all-to-all-start = ((bf16[64,16,512]{2,1,0:T(8,128)(2,1)}), bf16[64,16,512]{2,1,0:T(8,128)(2,1)S(1)}, u32[]{:S(2)}, u32[]{:S(2)}) async-start(bf16[64,16,512]{2,1,0:T(8,128)(2,1)} %reshape.47), calls=%async_computation | async-start | bytes 2097152 | tf_op jit(solution)/shard_map/all_to_all | solution.py:217
  56.5 10.3 %collective-permute-start.4 = (bf16[2,9,8,8,256]{4,3,2,1,0:T(8,128)(2,1)S(1)}, bf16[2,9,8,8,256]{4,3,2,1,0:T(8,128)(2,1)S(1)}, u32[]{:S(2)}, u32[]{:S(2)}) collective-permute-start(bf16[2,9,8,8,256]{4,3,2,1,0:T(8,128)(2,1)S(1)} %get-tuple-element.24), channel_id=1, source_target_pairs={{0,4},{1,13},{2,6},{3,15},{4,0},{5,9},{6,2},{7,11},{8,12},{9,5},{1... | collective-permute-start | bytes 1769480 | tf_op jit(solution)/shard_map/ppermute | solution.py:28
  66.9 23.5 %copy-start.1 = (bf16[2,2,9,8,8,256]{5,4,3,2,1,0:T(8,128)(2,1)}, bf16[2,2,9,8,8,256]{5,4,3,2,1,0:T(8,128)(2,1)S(1)}, u32[]{:S(2)}) copy-start(bf16[2,2,9,8,8,256]{5,4,3,2,1,0:T(8,128)(2,1)S(1)} %pad_maximum_fusion.refs_0_) | copy-start | bytes 3538948
  66.9 18.8 %collective-permute-start.5 = (bf16[2,2,9,8,8,256]{5,4,3,2,1,0:T(8,128)(2,1)S(1)}, bf16[2,2,9,8,8,256]{5,4,3,2,1,0:T(8,128)(2,1)}, u32[]{:S(2)}, u32[]{:S(2)}) collective-permute-start(bf16[2,2,9,8,8,256]{5,4,3,2,1,0:T(8,128)(2,1)S(1)} %pad_maximum_fusion.refs_0_), channel_id=1, source_target_pairs={{0,12},{1,5},{2,14},{3,7},{4,8},{5,1},{6,10},{7,3},{8,4},{9,13},{1... | collective-permute-start | bytes 3538952 | tf_op jit(solution)/shard_map/ppermute | solution.py:28
  67.0 19.3 %collective-permute-start.6 = (bf16[2,2,9,8,8,256]{5,4,3,2,1,0:T(8,128)(2,1)S(1)}, bf16[2,2,9,8,8,256]{5,4,3,2,1,0:T(8,128)(2,1)}, u32[]{:S(2)}, u32[]{:S(2)}) collective-permute-start(bf16[2,2,9,8,8,256]{5,4,3,2,1,0:T(8,128)(2,1)S(1)} %pad_maximum_fusion.refs_0_), channel_id=1, source_target_pairs={{0,1},{1,0},{2,3},{3,2},{4,5},{5,4},{6,7},{7,6},{8,9},{9,8},{10,11... | collective-permute-start | bytes 3538952 | tf_op jit(solution)/shard_map/ppermute | solution.py:28
  67.5 19.8 %collective-permute-start.11 = (bf16[2,17,8,8,256]{4,3,2,1,0:T(8,128)(2,1)}, bf16[2,17,8,8,256]{4,3,2,1,0:T(8,128)(2,1)}, u32[]{:S(2)}, u32[]{:S(2)}) collective-permute-start(bf16[2,17,8,8,256]{4,3,2,1,0:T(8,128)(2,1)} %collective-permute-done.9.refs_1_), channel_id=1, source_target_pairs={{0,128},{1,131},{2,130},{3,129},{4,132},{5,135},{6,134},{7,133},{8... | collective-permute-start | bytes 3342344 | tf_op jit(solution)/shard_map/ppermute | solution.py:28
  85.7 4.7 %copy-start.3 = (bf16[64,16,512]{2,1,0:T(8,128)(2,1)}, bf16[64,16,512]{2,1,0:T(8,128)(2,1)S(1)}, u32[]{:S(2)}) copy-start(bf16[64,16,512]{2,1,0:T(8,128)(2,1)S(1)} %all-to-all-done) | copy-start | bytes 3145732
  85.7 4.7 %collective-permute-start.7 = (bf16[2,2,9,8,8,256]{5,4,3,2,1,0:T(8,128)(2,1)}, bf16[2,2,9,8,8,256]{5,4,3,2,1,0:T(8,128)(2,1)}, u32[]{:S(2)}, u32[]{:S(2)}) collective-permute-start(bf16[2,2,9,8,8,256]{5,4,3,2,1,0:T(8,128)(2,1)} %collective-permute-done.5.refs_1_), channel_id=1, source_target_pairs={{0,1},{1,0},{2,3},{3,2},{4,5},{5,4},{6,7},{7,6},{8,9},{9,8},{10,11... | collective-permute-start | bytes 3538952 | tf_op jit(solution)/shard_map/ppermute | solution.py:28
  85.7 14.7 %collective-permute-start.12 = (bf16[2,17,8,8,256]{4,3,2,1,0:T(8,128)(2,1)S(1)}, bf16[2,17,8,8,256]{4,3,2,1,0:T(8,128)(2,1)}, u32[]{:S(2)}, u32[]{:S(2)}) collective-permute-start(bf16[2,17,8,8,256]{4,3,2,1,0:T(8,128)(2,1)S(1)} %pad_maximum_fusion.1.refs_0_), channel_id=1, source_target_pairs={{0,1},{1,0},{2,3},{3,2},{4,5},{5,4},{6,7},{7,6},{8,9},{9,8},{10,11... | collective-permute-start | bytes 3342344 | tf_op jit(solution)/shard_map/ppermute | solution.py:28
  86.2 14.2 %collective-permute-start.13 = (bf16[2,17,8,8,256]{4,3,2,1,0:T(8,128)(2,1)}, bf16[2,17,8,8,256]{4,3,2,1,0:T(8,128)(2,1)}, u32[]{:S(2)}, u32[]{:S(2)}) collective-permute-start(bf16[2,17,8,8,256]{4,3,2,1,0:T(8,128)(2,1)} %collective-permute-done.9.refs_1_), channel_id=1, source_target_pairs={{0,1},{1,0},{2,3},{3,2},{4,5},{5,4},{6,7},{7,6},{8,9},{9,8},{10,11... | collective-permute-start | bytes 3342344 | tf_op jit(solution)/shard_map/ppermute | solution.py:28
  86.3 14.1 %collective-permute-start.14 = (bf16[2,17,8,8,256]{4,3,2,1,0:T(8,128)(2,1)}, bf16[2,17,8,8,256]{4,3,2,1,0:T(8,128)(2,1)}, u32[]{:S(2)}, u32[]{:S(2)}) collective-permute-start(bf16[2,17,8,8,256]{4,3,2,1,0:T(8,128)(2,1)} %collective-permute-done.10.refs_2_), channel_id=1, source_target_pairs={{0,1},{1,0},{2,3},{3,2},{4,5},{5,4},{6,7},{7,6},{8,9},{9,8},{10,11... | collective-permute-start | bytes 3342344 | tf_op jit(solution)/shard_map/ppermute | solution.py:28
  87.3 13.2 %collective-permute-start.15 = (bf16[2,17,8,8,256]{4,3,2,1,0:T(8,128)(2,1)}, bf16[2,17,8,8,256]{4,3,2,1,0:T(8,128)(2,1)}, u32[]{:S(2)}, u32[]{:S(2)}) collective-permute-start(bf16[2,17,8,8,256]{4,3,2,1,0:T(8,128)(2,1)} %collective-permute-done.11.refs_3_), channel_id=1, source_target_pairs={{0,1},{1,0},{2,3},{3,2},{4,5},{5,4},{6,7},{7,6},{8,9},{9,8},{10,11... | collective-permute-start | bytes 3342344 | tf_op jit(solution)/shard_map/ppermute | solution.py:28

commit v3 on v2

--- a/solution.py
+++ b/solution.py
@@ -32,12 +32,8 @@
     return moved(piece, lambda y, z, x, c: (y, z, x ^ (3 if c != turn else 1), c))
 
 
-def from_z(piece, bit):
+def from_z(piece):
     def partner(y, z, x, c):
-        if bit == 2:
-            return y, z ^ 4, x, c
-        if bit == 1:
-            return y, z ^ (6 if c else 2), x, c
         return y, z + (1 if (z + c) % 2 == 0 else -1), x, c
 
     return moved(piece, partner)
@@ -112,7 +108,7 @@
             shifted[r + step, :, j * ch : (j + 1) * ch] = values.astype(jnp.bfloat16)
         return 0
 
-    lax.fori_loop(0, ROWS, fill, 0)
+    lax.fori_loop(0, ROWS, fill, 0, unroll=2)
     for i in range(3):
         for copy in groups[i]:
             copy.wait()
@@ -210,8 +206,12 @@
 
     cells = inputs.reshape(s, i, 8, 8, PAIR, ch).transpose(0, 1, 3, 2, 4, 5).reshape(64, 16, ch)
     shard = shard.reshape(-1, 1, 8, half)
-    for bit in (2, 1, 0):
-        shard = joined(shard, from_z(shard, bit), (lax.axis_index("z") >> bit) & 1)
+    quarters = [shard] + [moved(shard, lambda y, z, x, c, k=k: (y, z ^ k, x, c)) for k in (2, 4, 6)]
+    for bit in (0, 1):
+        turned = (lax.axis_index("z") >> (bit + 1)) & 1 == 1
+        quarters = [jnp.where(turned, quarters[q ^ (1 << bit)], quarters[q]) for q in range(4)]
+    shard = jnp.concatenate(quarters, axis=1)
+    shard = joined(shard, from_z(shard), lax.axis_index("z") & 1)
     shard = shard.reshape(-1, 8, 8, half)
     shard, cells = lax.optimization_barrier((shard, cells))
     cells = lax.all_to_all(cells, PEERS, 0, 0).reshape(ROWS, LINE, ch)

time: 158 us -> 153 us (0.968)
  starting transfers between devices: 40.2 us -> 38.2 us
  waiting for transfers between devices: 43.4 us -> 41.6 us
    all_to_all x1, waiting for transfers between devices: 15.7 us -> 3.24 us  [shards(): cells = lax.all_to_all(cells, PEERS, 0, 0).reshape(ROWS, LINE, ch)]
    ppermute x16 -> x17, waiting for transfers between devices: 27.7 us -> 38.4 us  [moved(): return lax.ppermute(array, AXES, pairs)]
    ppermute x16 -> x17, starting transfers between devices: 27.4 us -> 23.4 us  [moved(): return lax.ppermute(array, AXES, pairs)]
    all_to_all x1, starting transfers between devices: 12.8 us -> 14.8 us  [shards(): cells = lax.all_to_all(cells, PEERS, 0, 0).reshape(ROWS, LINE, ch)]
  transfers between devices with their start and end apart: 17 -> 18, of which waited for: 7 -> 9; matrix products, arithmetic and copies ran while one was open for 2% -> 3% of each run, Pallas kernels for 6% -> 6%
where the time goes in v3:
time: 153 us
  waiting for transfers between devices  41.6 us (27%)
  starting transfers between devices  38.2 us (25%)
  blocking collectives  37.5 us (25%)
  Pallas kernels  25.1 us (16%)
  local copies, waits for them, and re-layouts  8.04 us (5%)
  other arithmetic  2.13 us (1%)
    ppermute x17, waiting for transfers between devices, moved(): return lax.ppermute(array, AXES, pairs)  38.4 us
    all_to_all x1, blocking collectives, shards(): out = lax.all_to_all(out.reshape(64, 16, ch), PEERS, 0, 0)  37.5 us
    pallas_call x2, Pallas kernels, block(): pl.pallas_call(functools.partial(kernel, step), out_shape=jax.ShapeDtypeS...  25.1 us
    ppermute x17, starting transfers between devices, moved(): return lax.ppermute(array, AXES, pairs)  23.4 us
    all_to_all x1, starting transfers between devices, shards(): cells = lax.all_to_all(cells, PEERS, 0, 0).reshape(ROWS, LINE, ch)  14.8 us
    all_to_all x1, waiting for transfers between devices, shards(): cells = lax.all_to_all(cells, PEERS, 0, 0).reshape(ROWS, LINE, ch)  3.24 us
  transfers between devices with their start and end apart: 18, of which 9 were waited for; matrix products, arithmetic and copies ran while one was open for 3% of the time, Pallas kernels for 6%

profile of v3, /device:TPU:33, one launch (start us, length us, event | category | flops | bytes accessed | tf_op | source)
XLA Modules:
  0.0 152.8 jit_solution(17681751896242941134)
XLA Ops:
  2.4 5.2 %collective-permute-start = (bf16[26,1,8,256]{3,2,1,0:T(8,128)(2,1)S(1)}, bf16[26,1,8,256]{3,2,1,0:T(8,128)(2,1)S(1)}, u32[]{:S(2)}, u32[]{:S(2)}) collective-permute-start(bf16[26,1,8,256]{3,2,1,0:T(8,128)(2,1)S(1)} %maximum_bitcast_fusion), channel_id=1, source_target_pairs={{0,96},{1,97},{2,98},{3,99},{4,100},{5,101},{6,102},{7,103},{8,104... | collective-permute-start | bytes 319496 | tf_op jit(solution)/shard_map/ppermute | solution.py:28
  7.6 1.2 collective-permute-start.1
  8.8 1.0 collective-permute-start.2
  9.8 3.1 %collective-permute-done = bf16[26,1,8,256]{3,2,1,0:T(8,128)(2,1)S(1)} collective-permute-done((bf16[26,1,8,256]{3,2,1,0:T(8,128)(2,1)S(1)}, bf16[26,1,8,256]{3,2,1,0:T(8,128)(2,1)S(1)}, u32[]{:S(2)}, u32[]{:S(2)}) %collective-permute-start) | collective-permute-done | bytes 106528 | tf_op jit(solution)/shard_map/ppermute | solution.py:28
  12.9 2.6 %collective-permute-done.1 = bf16[26,1,8,256]{3,2,1,0:T(8,128)(2,1)S(1)} collective-permute-done((bf16[26,1,8,256]{3,2,1,0:T(8,128)(2,1)S(1)}, bf16[26,1,8,256]{3,2,1,0:T(8,128)(2,1)S(1)}, u32[]{:S(2)}, u32[]{:S(2)}) %collective-permute-start.1) | collective-permute-done | bytes 106528 | tf_op jit(solution)/shard_map/ppermute | solution.py:28
  15.5 2.3 %collective-permute-done.2 = bf16[26,1,8,256]{3,2,1,0:T(8,128)(2,1)S(1)} collective-permute-done((bf16[26,1,8,256]{3,2,1,0:T(8,128)(2,1)S(1)}, bf16[26,1,8,256]{3,2,1,0:T(8,128)(2,1)S(1)}, u32[]{:S(2)}, u32[]{:S(2)}) %collective-permute-start.2) | collective-permute-done | bytes 106528 | tf_op jit(solution)/shard_map/ppermute | solution.py:28
  19.1 1.2 copy.7
  20.3 1.2 reshape.39
  21.6 3.7 %collective-permute-done.3 = bf16[26,4,8,256]{3,2,1,0:T(8,128)(2,1)S(1)} collective-permute-done((bf16[26,4,8,256]{3,2,1,0:T(8,128)(2,1)S(1)}, bf16[26,4,8,256]{3,2,1,0:T(8,128)(2,1)S(1)}, u32[]{:S(2)}, u32[]{:S(2)}) %collective-permute-start.3) | collective-permute-done | bytes 426016 | tf_op jit(solution)/shard_map/ppermute | solution.py:28
  25.6 2.6 %collective-permute-start.9 = (bf16[17,8,8,256]{3,2,1,0:T(8,128)(2,1)S(1)}, bf16[17,8,8,256]{3,2,1,0:T(8,128)(2,1)S(1)}, u32[]{:S(2)}, u32[]{:S(2)}) collective-permute-start(bf16[17,8,8,256]{3,2,1,0:T(8,128)(2,1)S(1)} %get-tuple-element.18), channel_id=1, source_target_pairs={{0,4},{1,13},{2,6},{3,15},{4,0},{5,9},{6,2},{7,11},{8,12},{9,5},{1... | collective-permute-start | bytes 1671176 | tf_op jit(solution)/shard_map/ppermute | solution.py:28
  28.9 2.7 %collective-permute-start.4 = (bf16[9,8,8,256]{3,2,1,0:T(8,128)(2,1)}, bf16[9,8,8,256]{3,2,1,0:T(8,128)(2,1)S(1)}, u32[]{:S(2)}, u32[]{:S(2)}) collective-permute-start(bf16[9,8,8,256]{3,2,1,0:T(8,128)(2,1)} %get-tuple-element.20), channel_id=1, source_target_pairs={{0,128},{1,131},{2,130},{3,129},{4,132},{5,135},{6,134},{7,133},{8... | collective-permute-start | bytes 884744 | tf_op jit(solution)/shard_map/ppermute | solution.py:28
  31.7 3.6 %collective-permute-done.9 = bf16[17,8,8,256]{3,2,1,0:T(8,128)(2,1)S(1)} collective-permute-done((bf16[17,8,8,256]{3,2,1,0:T(8,128)(2,1)S(1)}, bf16[17,8,8,256]{3,2,1,0:T(8,128)(2,1)S(1)}, u32[]{:S(2)}, u32[]{:S(2)}) %collective-permute-start.9) | collective-permute-done | bytes 557088 | tf_op jit(solution)/shard_map/ppermute | solution.py:28
  35.8 2.7 %collective-permute-start.11 = (bf16[2,17,8,8,256]{4,3,2,1,0:T(8,128)(2,1)S(1)}, bf16[2,17,8,8,256]{4,3,2,1,0:T(8,128)(2,1)}, u32[]{:S(2)}, u32[]{:S(2)}) collective-permute-start(bf16[2,17,8,8,256]{4,3,2,1,0:T(8,128)(2,1)S(1)} %pad_maximum_fusion.1.refs_0_), channel_id=1, source_target_pairs={{0,128},{1,131},{2,130},{3,129},{4,132},{5,135},{6,134},{7,133},{8... | collective-permute-start | bytes 3342344 | tf_op jit(solution)/shard_map/ppermute | solution.py:28
  38.5 14.8 %all-to-all-start = ((bf16[64,16,512]{2,1,0:T(8,128)(2,1)}), bf16[64,16,512]{2,1,0:T(8,128)(2,1)S(1)}, u32[]{:S(2)}, u32[]{:S(2)}) async-start(bf16[64,16,512]{2,1,0:T(8,128)(2,1)} %reshape.39), calls=%async_computation | async-start | bytes 2097152 | tf_op jit(solution)/shard_map/all_to_all | solution.py:217
  53.6 10.0 %collective-permute-done.5 = bf16[2,9,8,8,256]{4,3,2,1,0:T(8,128)(2,1)S(1)} collective-permute-done((bf16[2,9,8,8,256]{4,3,2,1,0:T(8,128)(2,1)S(1)}, bf16[2,9,8,8,256]{4,3,2,1,0:T(8,128)(2,1)S(1)}, u32[]{:S(2)}, u32[]{:S(2)}) %collective-permute-start.5) | collective-permute-done | bytes 589856 | tf_op jit(solution)/shard_map/ppermute | solution.py:28
  64.4 2.5 %collective-permute-start.12 = (bf16[2,17,8,8,256]{4,3,2,1,0:T(8,128)(2,1)}, bf16[2,17,8,8,256]{4,3,2,1,0:T(8,128)(2,1)}, u32[]{:S(2)}, u32[]{:S(2)}) collective-permute-start(bf16[2,17,8,8,256]{4,3,2,1,0:T(8,128)(2,1)} %collective-permute-done.10.refs_1_), channel_id=1, source_target_pairs={{0,128},{1,131},{2,130},{3,129},{4,132},{5,135},{6,134},{7,133},{8... | collective-permute-start | bytes 3342344 | tf_op jit(solution)/shard_map/ppermute | solution.py:28
  66.9 12.4 %collective-permute-done.6.refs_1_ = bf16[2,2,9,8,8,256]{5,4,3,2,1,0:T(8,128)(2,1)} collective-permute-done((bf16[2,2,9,8,8,256]{5,4,3,2,1,0:T(8,128)(2,1)S(1)}, bf16[2,2,9,8,8,256]{5,4,3,2,1,0:T(8,128)(2,1)}, u32[]{:S(2)}, u32[]{:S(2)}) %collective-permute-start.6) | collective-permute-done | bytes 1179680 | tf_op jit(solution)/shard_map/ppermute | solution.py:28
  79.4 3.2 %all-to-all-done = bf16[64,16,512]{2,1,0:T(8,128)(2,1)S(1)} async-done(((bf16[64,16,512]{2,1,0:T(8,128)(2,1)}), bf16[64,16,512]{2,1,0:T(8,128)(2,1)S(1)}, u32[]{:S(2)}, u32[]{:S(2)}) %all-to-all-start) | async-done | bytes 1048608 | tf_op jit(solution)/shard_map/all_to_all | solution.py:217
  84.2 2.4 %collective-permute-start.16 = (bf16[2,17,8,8,256]{4,3,2,1,0:T(8,128)(2,1)}, bf16[2,17,8,8,256]{4,3,2,1,0:T(8,128)(2,1)}, u32[]{:S(2)}, u32[]{:S(2)}) collective-permute-start(bf16[2,17,8,8,256]{4,3,2,1,0:T(8,128)(2,1)} %collective-permute-done.12.refs_3_), channel_id=1, source_target_pairs={{0,1},{1,0},{2,3},{3,2},{4,5},{5,4},{6,7},{7,6},{8,9},{9,8},{10,11... | collective-permute-start | bytes 3342344 | tf_op jit(solution)/shard_map/ppermute | solution.py:28
  87.3 9.4 %shard_map.55.cells = bf16[16,64,512]{2,1,0:T(8,128)(2,1)} custom-call(s32[3]{0:T(128)} %pad_add_fusion.where, bf16[16,64,512]{2,1,0:T(8,128)(2,1)} %bitcast.52, bf16[2,2,9,8,8,256]{5,4,3,2,1,0:T(8,128)(2,1)} %copy-done.1, bf16[2,2,9,8,8,256]{5,4,3,2,1,0:T(8,128)(2,1)} %collective-permute-done.6.refs_1_, ...), custom_call_target="tpu_custom_call" | custom-call | flops 1000 | bytes 1000 | tf_op jit(solution)/shard_map/pallas_call | solution.py:185
  96.7 15.8 %shard_map.56 = bf16[16,64,512]{2,1,0:T(8,128)(2,1)} custom-call(s32[3]{0:T(128)} %pad_add_fusion.where, bf16[16,64,512]{2,1,0:T(8,128)(2,1)} %shard_map.55.cells, bf16[2,17,8,8,256]{4,3,2,1,0:T(8,128)(2,1)} %copy-done.2, bf16[2,17,8,8,256]{4,3,2,1,0:T(8,128)(2,1)} %collective-permute-done.10.refs_1_, ...), custom_call_target="tpu_custom_call" | custom-call | flops 1000 | bytes 1000 | tf_op jit(solution)/shard_map/pallas_call | solution.py:185
  112.5 37.5 %all_to_all.10 = bf16[64,16,512]{2,1,0:T(8,128)(2,1)S(1)} all-to-all(bf16[64,16,512]{2,1,0:T(8,128)(2,1)} %bitcast.53), channel_id=1, replica_groups=mesh['ylo'=2,'z'=8,'x'=4,'yhi'=2,'core'=2] {'ylo','z','yhi','core'}, dimensions={0} | all-to-all | bytes 2097152 | tf_op jit(solution)/shard_map/all_to_all | solution.py:234
  150.4 1.2 copy.10
  151.6 1.2 reshape.43
  (47 shorter events, 9.0 us)
Async XLA Ops:
  0.0 0.8 copy-start
  1.5 17.2 %copy-start.4 = (bf16[2,4,128,512]{3,2,1,0:T(8,128)(2,1)S(1)}, bf16[2,4,128,512]{3,2,1,0:T(8,128)(2,1)}, u32[]{:S(2)}) copy-start(bf16[2,4,128,512]{3,2,1,0:T(8,128)(2,1)} %param.5) | copy-start | bytes 3145732
  2.4 10.5 %collective-permute-start = (bf16[26,1,8,256]{3,2,1,0:T(8,128)(2,1)S(1)}, bf16[26,1,8,256]{3,2,1,0:T(8,128)(2,1)S(1)}, u32[]{:S(2)}, u32[]{:S(2)}) collective-permute-start(bf16[26,1,8,256]{3,2,1,0:T(8,128)(2,1)S(1)} %maximum_bitcast_fusion), channel_id=1, source_target_pairs={{0,96},{1,97},{2,98},{3,99},{4,100},{5,101},{6,102},{7,103},{8,104... | collective-permute-start | bytes 319496 | tf_op jit(solution)/shard_map/ppermute | solution.py:28
  7.6 7.9 %collective-permute-start.1 = (bf16[26,1,8,256]{3,2,1,0:T(8,128)(2,1)S(1)}, bf16[26,1,8,256]{3,2,1,0:T(8,128)(2,1)S(1)}, u32[]{:S(2)}, u32[]{:S(2)}) collective-permute-start(bf16[26,1,8,256]{3,2,1,0:T(8,128)(2,1)S(1)} %maximum_bitcast_fusion), channel_id=1, source_target_pairs={{0,64},{1,65},{2,66},{3,67},{4,68},{5,69},{6,70},{7,71},{8,72},{9,... | collective-permute-start | bytes 319496 | tf_op jit(solution)/shard_map/ppermute | solution.py:28
  8.8 9.0 %collective-permute-start.2 = (bf16[26,1,8,256]{3,2,1,0:T(8,128)(2,1)S(1)}, bf16[26,1,8,256]{3,2,1,0:T(8,128)(2,1)S(1)}, u32[]{:S(2)}, u32[]{:S(2)}) collective-permute-start(bf16[26,1,8,256]{3,2,1,0:T(8,128)(2,1)S(1)} %maximum_bitcast_fusion), channel_id=1, source_target_pairs={{0,32},{1,33},{2,34},{3,35},{4,36},{5,37},{6,38},{7,39},{8,40},{9,... | collective-permute-start | bytes 319496 | tf_op jit(solution)/shard_map/ppermute | solution.py:28
  17.9 7.4 %collective-permute-start.3 = (bf16[26,4,8,256]{3,2,1,0:T(8,128)(2,1)S(1)}, bf16[26,4,8,256]{3,2,1,0:T(8,128)(2,1)S(1)}, u32[]{:S(2)}, u32[]{:S(2)}) collective-permute-start(bf16[26,4,8,256]{3,2,1,0:T(8,128)(2,1)S(1)} %pad_maximum_fusion.4), channel_id=1, source_target_pairs={{0,16},{1,113},{2,18},{3,115},{4,20},{5,117},{6,22},{7,119},{8,24}... | collective-permute-start | bytes 1277960 | tf_op jit(solution)/shard_map/ppermute | solution.py:28
  25.6 9.7 %collective-permute-start.9 = (bf16[17,8,8,256]{3,2,1,0:T(8,128)(2,1)S(1)}, bf16[17,8,8,256]{3,2,1,0:T(8,128)(2,1)S(1)}, u32[]{:S(2)}, u32[]{:S(2)}) collective-permute-start(bf16[17,8,8,256]{3,2,1,0:T(8,128)(2,1)S(1)} %get-tuple-element.18), channel_id=1, source_target_pairs={{0,4},{1,13},{2,6},{3,15},{4,0},{5,9},{6,2},{7,11},{8,12},{9,5},{1... | collective-permute-start | bytes 1671176 | tf_op jit(solution)/shard_map/ppermute | solution.py:28
  28.9 24.3 %collective-permute-start.4 = (bf16[9,8,8,256]{3,2,1,0:T(8,128)(2,1)}, bf16[9,8,8,256]{3,2,1,0:T(8,128)(2,1)S(1)}, u32[]{:S(2)}, u32[]{:S(2)}) collective-permute-start(bf16[9,8,8,256]{3,2,1,0:T(8,128)(2,1)} %get-tuple-element.20), channel_id=1, source_target_pairs={{0,128},{1,131},{2,130},{3,129},{4,132},{5,135},{6,134},{7,133},{8... | collective-permute-start | bytes 884744 | tf_op jit(solution)/shard_map/ppermute | solution.py:28
  35.4 47.2 %copy-start.2 = (bf16[2,17,8,8,256]{4,3,2,1,0:T(8,128)(2,1)}, bf16[2,17,8,8,256]{4,3,2,1,0:T(8,128)(2,1)S(1)}, u32[]{:S(2)}) copy-start(bf16[2,17,8,8,256]{4,3,2,1,0:T(8,128)(2,1)S(1)} %pad_maximum_fusion.1.refs_0_) | copy-start | bytes 3342340
  35.4 29.0 %collective-permute-start.10 = (bf16[2,17,8,8,256]{4,3,2,1,0:T(8,128)(2,1)S(1)}, bf16[2,17,8,8,256]{4,3,2,1,0:T(8,128)(2,1)}, u32[]{:S(2)}, u32[]{:S(2)}) collective-permute-start(bf16[2,17,8,8,256]{4,3,2,1,0:T(8,128)(2,1)S(1)} %pad_maximum_fusion.1.refs_0_), channel_id=1, source_target_pairs={{0,12},{1,5},{2,14},{3,7},{4,8},{5,1},{6,10},{7,3},{8,4},{9,13},{1... | collective-permute-start | bytes 3342344 | tf_op jit(solution)/shard_map/ppermute | solution.py:28
  35.8 28.6 %collective-permute-start.11 = (bf16[2,17,8,8,256]{4,3,2,1,0:T(8,128)(2,1)S(1)}, bf16[2,17,8,8,256]{4,3,2,1,0:T(8,128)(2,1)}, u32[]{:S(2)}, u32[]{:S(2)}) collective-permute-start(bf16[2,17,8,8,256]{4,3,2,1,0:T(8,128)(2,1)S(1)} %pad_maximum_fusion.1.refs_0_), channel_id=1, source_target_pairs={{0,128},{1,131},{2,130},{3,129},{4,132},{5,135},{6,134},{7,133},{8... | collective-permute-start | bytes 3342344 | tf_op jit(solution)/shard_map/ppermute | solution.py:28
  38.5 44.1 %all-to-all-start = ((bf16[64,16,512]{2,1,0:T(8,128)(2,1)}), bf16[64,16,512]{2,1,0:T(8,128)(2,1)S(1)}, u32[]{:S(2)}, u32[]{:S(2)}) async-start(bf16[64,16,512]{2,1,0:T(8,128)(2,1)} %reshape.39), calls=%async_computation | async-start | bytes 2097152 | tf_op jit(solution)/shard_map/all_to_all | solution.py:217
  53.4 10.3 %collective-permute-start.5 = (bf16[2,9,8,8,256]{4,3,2,1,0:T(8,128)(2,1)S(1)}, bf16[2,9,8,8,256]{4,3,2,1,0:T(8,128)(2,1)S(1)}, u32[]{:S(2)}, u32[]{:S(2)}) collective-permute-start(bf16[2,9,8,8,256]{4,3,2,1,0:T(8,128)(2,1)S(1)} %get-tuple-element.24), channel_id=1, source_target_pairs={{0,4},{1,13},{2,6},{3,15},{4,0},{5,9},{6,2},{7,11},{8,12},{9,5},{1... | collective-permute-start | bytes 1769480 | tf_op jit(solution)/shard_map/ppermute | solution.py:28
  63.8 23.5 %copy-start.1 = (bf16[2,2,9,8,8,256]{5,4,3,2,1,0:T(8,128)(2,1)}, bf16[2,2,9,8,8,256]{5,4,3,2,1,0:T(8,128)(2,1)S(1)}, u32[]{:S(2)}) copy-start(bf16[2,2,9,8,8,256]{5,4,3,2,1,0:T(8,128)(2,1)S(1)} %pad_maximum_fusion.refs_0_) | copy-start | bytes 3538948
  63.8 15.5 %collective-permute-start.6 = (bf16[2,2,9,8,8,256]{5,4,3,2,1,0:T(8,128)(2,1)S(1)}, bf16[2,2,9,8,8,256]{5,4,3,2,1,0:T(8,128)(2,1)}, u32[]{:S(2)}, u32[]{:S(2)}) collective-permute-start(bf16[2,2,9,8,8,256]{5,4,3,2,1,0:T(8,128)(2,1)S(1)} %pad_maximum_fusion.refs_0_), channel_id=1, source_target_pairs={{0,12},{1,5},{2,14},{3,7},{4,8},{5,1},{6,10},{7,3},{8,4},{9,13},{1... | collective-permute-start | bytes 3538952 | tf_op jit(solution)/shard_map/ppermute | solution.py:28
  63.9 19.3 %collective-permute-start.7 = (bf16[2,2,9,8,8,256]{5,4,3,2,1,0:T(8,128)(2,1)S(1)}, bf16[2,2,9,8,8,256]{5,4,3,2,1,0:T(8,128)(2,1)}, u32[]{:S(2)}, u32[]{:S(2)}) collective-permute-start(bf16[2,2,9,8,8,256]{5,4,3,2,1,0:T(8,128)(2,1)S(1)} %pad_maximum_fusion.refs_0_), channel_id=1, source_target_pairs={{0,1},{1,0},{2,3},{3,2},{4,5},{5,4},{6,7},{7,6},{8,9},{9,8},{10,11... | collective-permute-start | bytes 3538952 | tf_op jit(solution)/shard_map/ppermute | solution.py:28
  64.4 19.8 %collective-permute-start.12 = (bf16[2,17,8,8,256]{4,3,2,1,0:T(8,128)(2,1)}, bf16[2,17,8,8,256]{4,3,2,1,0:T(8,128)(2,1)}, u32[]{:S(2)}, u32[]{:S(2)}) collective-permute-start(bf16[2,17,8,8,256]{4,3,2,1,0:T(8,128)(2,1)} %collective-permute-done.10.refs_1_), channel_id=1, source_target_pairs={{0,128},{1,131},{2,130},{3,129},{4,132},{5,135},{6,134},{7,133},{8... | collective-permute-start | bytes 3342344 | tf_op jit(solution)/shard_map/ppermute | solution.py:28
  82.6 4.7 %copy-start.3 = (bf16[64,16,512]{2,1,0:T(8,128)(2,1)}, bf16[64,16,512]{2,1,0:T(8,128)(2,1)S(1)}, u32[]{:S(2)}) copy-start(bf16[64,16,512]{2,1,0:T(8,128)(2,1)S(1)} %all-to-all-done) | copy-start | bytes 3145732
  82.6 4.7 %collective-permute-start.8 = (bf16[2,2,9,8,8,256]{5,4,3,2,1,0:T(8,128)(2,1)}, bf16[2,2,9,8,8,256]{5,4,3,2,1,0:T(8,128)(2,1)}, u32[]{:S(2)}, u32[]{:S(2)}) collective-permute-start(bf16[2,2,9,8,8,256]{5,4,3,2,1,0:T(8,128)(2,1)} %collective-permute-done.6.refs_1_), channel_id=1, source_target_pairs={{0,1},{1,0},{2,3},{3,2},{4,5},{5,4},{6,7},{7,6},{8,9},{9,8},{10,11... | collective-permute-start | bytes 3538952 | tf_op jit(solution)/shard_map/ppermute | solution.py:28
  82.6 14.1 %collective-permute-start.13 = (bf16[2,17,8,8,256]{4,3,2,1,0:T(8,128)(2,1)S(1)}, bf16[2,17,8,8,256]{4,3,2,1,0:T(8,128)(2,1)}, u32[]{:S(2)}, u32[]{:S(2)}) collective-permute-start(bf16[2,17,8,8,256]{4,3,2,1,0:T(8,128)(2,1)S(1)} %pad_maximum_fusion.1.refs_0_), channel_id=1, source_target_pairs={{0,1},{1,0},{2,3},{3,2},{4,5},{5,4},{6,7},{7,6},{8,9},{9,8},{10,11... | collective-permute-start | bytes 3342344 | tf_op jit(solution)/shard_map/ppermute | solution.py:28
  83.1 13.6 %collective-permute-start.14 = (bf16[2,17,8,8,256]{4,3,2,1,0:T(8,128)(2,1)}, bf16[2,17,8,8,256]{4,3,2,1,0:T(8,128)(2,1)}, u32[]{:S(2)}, u32[]{:S(2)}) collective-permute-start(bf16[2,17,8,8,256]{4,3,2,1,0:T(8,128)(2,1)} %collective-permute-done.10.refs_1_), channel_id=1, source_target_pairs={{0,1},{1,0},{2,3},{3,2},{4,5},{5,4},{6,7},{7,6},{8,9},{9,8},{10,11... | collective-permute-start | bytes 3342344 | tf_op jit(solution)/shard_map/ppermute | solution.py:28
  83.2 13.5 %collective-permute-start.15 = (bf16[2,17,8,8,256]{4,3,2,1,0:T(8,128)(2,1)}, bf16[2,17,8,8,256]{4,3,2,1,0:T(8,128)(2,1)}, u32[]{:S(2)}, u32[]{:S(2)}) collective-permute-start(bf16[2,17,8,8,256]{4,3,2,1,0:T(8,128)(2,1)} %collective-permute-done.11.refs_2_), channel_id=1, source_target_pairs={{0,1},{1,0},{2,3},{3,2},{4,5},{5,4},{6,7},{7,6},{8,9},{9,8},{10,11... | collective-permute-start | bytes 3342344 | tf_op jit(solution)/shard_map/ppermute | solution.py:28
  84.2 12.5 %collective-permute-start.16 = (bf16[2,17,8,8,256]{4,3,2,1,0:T(8,128)(2,1)}, bf16[2,17,8,8,256]{4,3,2,1,0:T(8,128)(2,1)}, u32[]{:S(2)}, u32[]{:S(2)}) collective-permute-start(bf16[2,17,8,8,256]{4,3,2,1,0:T(8,128)(2,1)} %collective-permute-done.12.refs_3_), channel_id=1, source_target_pairs={{0,1},{1,0},{2,3},{3,2},{4,5},{5,4},{6,7},{7,6},{8,9},{9,8},{10,11... | collective-permute-start | bytes 3342344 | tf_op jit(solution)/shard_map/ppermute | solution.py:28

commit v4 on v3

--- a/solution.py
+++ b/solution.py
@@ -223,11 +223,11 @@
     first_y = from_y(first)
     t_first = jnp.stack([near_half, from_x(near_half, 0)])
     t_second = from_x(t_first, 1)
-    t_second, cells = lax.optimization_barrier((t_second, cells))
     tight_parts = [t_first, t_second, from_core(t_first), from_core(t_second)]
     second, first_y = lax.optimization_barrier((second, first_y))
     own = [first, second, first_y, from_y(second)]
-    parts = own + [from_core(piece) for piece in own]
+    late, cells = lax.optimization_barrier((own[2], cells))
+    parts = own + [from_core(late if n == 2 else piece) for n, piece in enumerate(own)]
 
     near = block(near_kernel, cells, tight_parts, 1, where, False)
     out = block(far_kernel, near, parts, 4, where, True)

time: 153 us -> 154 us (level)
  waiting for transfers between devices: 41.6 us -> 40 us
  starting transfers between devices: 38.2 us -> 39.8 us
    all_to_all x1, waiting for transfers between devices: 3.24 us -> 0.66 us  [shards(): cells = lax.all_to_all(cells, PEERS, 0, 0).reshape(ROWS, LINE, ch)]
    ppermute x17, starting transfers between devices: 23.4 us -> 25 us  [moved(): return lax.ppermute(array, AXES, pairs)]
where the time goes in v4:
time: 154 us; the launch traced here: 153 us
  waiting for transfers between devices  40 us (26%)
  starting transfers between devices  39.8 us (26%)
  blocking collectives  38.1 us (25%)
  Pallas kernels  25.1 us (16%)
  local copies, waits for them, and re-layouts  8.04 us (5%)
  other arithmetic  2.13 us (1%)
    ppermute x17, waiting for transfers between devices, moved(): return lax.ppermute(array, AXES, pairs)  39.4 us
    all_to_all x1, blocking collectives, shards(): out = lax.all_to_all(out.reshape(64, 16, ch), PEERS, 0, 0)  38.1 us
    pallas_call x2, Pallas kernels, block(): pl.pallas_call(functools.partial(kernel, step), out_shape=jax.ShapeDtypeS...  25.1 us
    ppermute x17, starting transfers between devices, moved(): return lax.ppermute(array, AXES, pairs)  25 us
    all_to_all x1, starting transfers between devices, shards(): cells = lax.all_to_all(cells, PEERS, 0, 0).reshape(ROWS, LINE, ch)  14.8 us
  transfers between devices with their start and end apart: 18, of which 9 were waited for; matrix products, arithmetic and copies ran while one was open for 3% of the time, Pallas kernels for 6%

profile of v4, /device:TPU:33, one launch (start us, length us, event | category | flops | bytes accessed | tf_op | source)
XLA Modules:
  0.0 153.4 jit_solution(17576040496702958975)
XLA Ops:
  2.4 5.2 %collective-permute-start = (bf16[26,1,8,256]{3,2,1,0:T(8,128)(2,1)S(1)}, bf16[26,1,8,256]{3,2,1,0:T(8,128)(2,1)S(1)}, u32[]{:S(2)}, u32[]{:S(2)}) collective-permute-start(bf16[26,1,8,256]{3,2,1,0:T(8,128)(2,1)S(1)} %maximum_bitcast_fusion), channel_id=1, source_target_pairs={{0,96},{1,97},{2,98},{3,99},{4,100},{5,101},{6,102},{7,103},{8,104... | collective-permute-start | bytes 319496 | tf_op jit(solution)/shard_map/ppermute | solution.py:28
  7.6 1.2 collective-permute-start.1
  9.8 3.1 %collective-permute-done = bf16[26,1,8,256]{3,2,1,0:T(8,128)(2,1)S(1)} collective-permute-done((bf16[26,1,8,256]{3,2,1,0:T(8,128)(2,1)S(1)}, bf16[26,1,8,256]{3,2,1,0:T(8,128)(2,1)S(1)}, u32[]{:S(2)}, u32[]{:S(2)}) %collective-permute-start) | collective-permute-done | bytes 106528 | tf_op jit(solution)/shard_map/ppermute | solution.py:28
  12.9 2.6 %collective-permute-done.1 = bf16[26,1,8,256]{3,2,1,0:T(8,128)(2,1)S(1)} collective-permute-done((bf16[26,1,8,256]{3,2,1,0:T(8,128)(2,1)S(1)}, bf16[26,1,8,256]{3,2,1,0:T(8,128)(2,1)S(1)}, u32[]{:S(2)}, u32[]{:S(2)}) %collective-permute-start.1) | collective-permute-done | bytes 106528 | tf_op jit(solution)/shard_map/ppermute | solution.py:28
  15.5 2.3 %collective-permute-done.2 = bf16[26,1,8,256]{3,2,1,0:T(8,128)(2,1)S(1)} collective-permute-done((bf16[26,1,8,256]{3,2,1,0:T(8,128)(2,1)S(1)}, bf16[26,1,8,256]{3,2,1,0:T(8,128)(2,1)S(1)}, u32[]{:S(2)}, u32[]{:S(2)}) %collective-permute-start.2) | collective-permute-done | bytes 106528 | tf_op jit(solution)/shard_map/ppermute | solution.py:28
  19.1 1.2 copy.7
  20.3 1.2 reshape.39
  21.6 3.7 %collective-permute-done.3 = bf16[26,4,8,256]{3,2,1,0:T(8,128)(2,1)S(1)} collective-permute-done((bf16[26,4,8,256]{3,2,1,0:T(8,128)(2,1)S(1)}, bf16[26,4,8,256]{3,2,1,0:T(8,128)(2,1)S(1)}, u32[]{:S(2)}, u32[]{:S(2)}) %collective-permute-start.3) | collective-permute-done | bytes 426016 | tf_op jit(solution)/shard_map/ppermute | solution.py:28
  25.6 2.6 %collective-permute-start.4 = (bf16[17,8,8,256]{3,2,1,0:T(8,128)(2,1)S(1)}, bf16[17,8,8,256]{3,2,1,0:T(8,128)(2,1)S(1)}, u32[]{:S(2)}, u32[]{:S(2)}) collective-permute-start(bf16[17,8,8,256]{3,2,1,0:T(8,128)(2,1)S(1)} %get-tuple-element.20), channel_id=1, source_target_pairs={{0,4},{1,13},{2,6},{3,15},{4,0},{5,9},{6,2},{7,11},{8,12},{9,5},{1... | collective-permute-start | bytes 1671176 | tf_op jit(solution)/shard_map/ppermute | solution.py:28
  28.9 2.7 %collective-permute-start.7 = (bf16[9,8,8,256]{3,2,1,0:T(8,128)(2,1)}, bf16[9,8,8,256]{3,2,1,0:T(8,128)(2,1)S(1)}, u32[]{:S(2)}, u32[]{:S(2)}) collective-permute-start(bf16[9,8,8,256]{3,2,1,0:T(8,128)(2,1)} %get-tuple-element.18), channel_id=1, source_target_pairs={{0,128},{1,131},{2,130},{3,129},{4,132},{5,135},{6,134},{7,133},{8... | collective-permute-start | bytes 884744 | tf_op jit(solution)/shard_map/ppermute | solution.py:28
  31.7 3.6 %collective-permute-done.4 = bf16[17,8,8,256]{3,2,1,0:T(8,128)(2,1)S(1)} collective-permute-done((bf16[17,8,8,256]{3,2,1,0:T(8,128)(2,1)S(1)}, bf16[17,8,8,256]{3,2,1,0:T(8,128)(2,1)S(1)}, u32[]{:S(2)}, u32[]{:S(2)}) %collective-permute-start.4) | collective-permute-done | bytes 557088 | tf_op jit(solution)/shard_map/ppermute | solution.py:28
  35.8 2.7 %collective-permute-start.6 = (bf16[2,17,8,8,256]{4,3,2,1,0:T(8,128)(2,1)S(1)}, bf16[2,17,8,8,256]{4,3,2,1,0:T(8,128)(2,1)}, u32[]{:S(2)}, u32[]{:S(2)}) collective-permute-start(bf16[2,17,8,8,256]{4,3,2,1,0:T(8,128)(2,1)S(1)} %pad_maximum_fusion.1.refs_0_), channel_id=1, source_target_pairs={{0,128},{1,131},{2,130},{3,129},{4,132},{5,135},{6,134},{7,133},{8... | collective-permute-start | bytes 3342344 | tf_op jit(solution)/shard_map/ppermute | solution.py:28
  38.5 14.8 %all-to-all-start = ((bf16[64,16,512]{2,1,0:T(8,128)(2,1)}), bf16[64,16,512]{2,1,0:T(8,128)(2,1)S(1)}, u32[]{:S(2)}, u32[]{:S(2)}) async-start(bf16[64,16,512]{2,1,0:T(8,128)(2,1)} %reshape.39), calls=%async_computation | async-start | bytes 2097152 | tf_op jit(solution)/shard_map/all_to_all | solution.py:217
  53.6 10.0 %collective-permute-done.8 = bf16[2,9,8,8,256]{4,3,2,1,0:T(8,128)(2,1)S(1)} collective-permute-done((bf16[2,9,8,8,256]{4,3,2,1,0:T(8,128)(2,1)S(1)}, bf16[2,9,8,8,256]{4,3,2,1,0:T(8,128)(2,1)S(1)}, u32[]{:S(2)}, u32[]{:S(2)}) %collective-permute-start.8) | collective-permute-done | bytes 589856 | tf_op jit(solution)/shard_map/ppermute | solution.py:28
  64.4 2.5 %collective-permute-start.12 = (bf16[2,17,8,8,256]{4,3,2,1,0:T(8,128)(2,1)}, bf16[2,17,8,8,256]{4,3,2,1,0:T(8,128)(2,1)}, u32[]{:S(2)}, u32[]{:S(2)}) collective-permute-start(bf16[2,17,8,8,256]{4,3,2,1,0:T(8,128)(2,1)} %collective-permute-done.5.refs_1_), channel_id=1, source_target_pairs={{0,128},{1,131},{2,130},{3,129},{4,132},{5,135},{6,134},{7,133},{8... | collective-permute-start | bytes 3342344 | tf_op jit(solution)/shard_map/ppermute | solution.py:28
  66.9 12.4 %collective-permute-done.9.refs_1_ = bf16[2,2,9,8,8,256]{5,4,3,2,1,0:T(8,128)(2,1)} collective-permute-done((bf16[2,2,9,8,8,256]{5,4,3,2,1,0:T(8,128)(2,1)S(1)}, bf16[2,2,9,8,8,256]{5,4,3,2,1,0:T(8,128)(2,1)}, u32[]{:S(2)}, u32[]{:S(2)}) %collective-permute-start.9) | collective-permute-done | bytes 1179680 | tf_op jit(solution)/shard_map/ppermute | solution.py:28
  79.4 2.1 %collective-permute-start.11 = (bf16[2,2,9,8,8,256]{5,4,3,2,1,0:T(8,128)(2,1)}, bf16[2,2,9,8,8,256]{5,4,3,2,1,0:T(8,128)(2,1)}, u32[]{:S(2)}, u32[]{:S(2)}) collective-permute-start(bf16[2,2,9,8,8,256]{5,4,3,2,1,0:T(8,128)(2,1)} %collective-permute-done.9.refs_1_), channel_id=1, source_target_pairs={{0,1},{1,0},{2,3},{3,2},{4,5},{5,4},{6,7},{7,6},{8,9},{9,8},{10,11... | collective-permute-start | bytes 3538952 | tf_op jit(solution)/shard_map/ppermute | solution.py:28
  82.6 1.6 %collective-permute-done.12.refs_3_ = bf16[2,17,8,8,256]{4,3,2,1,0:T(8,128)(2,1)} collective-permute-done((bf16[2,17,8,8,256]{4,3,2,1,0:T(8,128)(2,1)}, bf16[2,17,8,8,256]{4,3,2,1,0:T(8,128)(2,1)}, u32[]{:S(2)}, u32[]{:S(2)}) %collective-permute-start.12) | collective-permute-done | bytes 1114144 | tf_op jit(solution)/shard_map/ppermute | solution.py:28
  84.2 2.4 %collective-permute-start.16 = (bf16[2,17,8,8,256]{4,3,2,1,0:T(8,128)(2,1)}, bf16[2,17,8,8,256]{4,3,2,1,0:T(8,128)(2,1)}, u32[]{:S(2)}, u32[]{:S(2)}) collective-permute-start(bf16[2,17,8,8,256]{4,3,2,1,0:T(8,128)(2,1)} %collective-permute-done.12.refs_3_), channel_id=1, source_target_pairs={{0,1},{1,0},{2,3},{3,2},{4,5},{5,4},{6,7},{7,6},{8,9},{9,8},{10,11... | collective-permute-start | bytes 3342344 | tf_op jit(solution)/shard_map/ppermute | solution.py:28
  87.3 9.4 %shard_map.55.cells = bf16[16,64,512]{2,1,0:T(8,128)(2,1)} custom-call(s32[3]{0:T(128)} %pad_add_fusion.where, bf16[16,64,512]{2,1,0:T(8,128)(2,1)} %bitcast.52, bf16[2,2,9,8,8,256]{5,4,3,2,1,0:T(8,128)(2,1)} %copy-done.1, bf16[2,2,9,8,8,256]{5,4,3,2,1,0:T(8,128)(2,1)} %collective-permute-done.9.refs_1_, ...), custom_call_target="tpu_custom_call" | custom-call | flops 1000 | bytes 1000 | tf_op jit(solution)/shard_map/pallas_call | solution.py:185
  96.7 15.8 %shard_map.56 = bf16[16,64,512]{2,1,0:T(8,128)(2,1)} custom-call(s32[3]{0:T(128)} %pad_add_fusion.where, bf16[16,64,512]{2,1,0:T(8,128)(2,1)} %shard_map.55.cells, bf16[2,17,8,8,256]{4,3,2,1,0:T(8,128)(2,1)} %copy-done.2, bf16[2,17,8,8,256]{4,3,2,1,0:T(8,128)(2,1)} %collective-permute-done.5.refs_1_, ...), custom_call_target="tpu_custom_call" | custom-call | flops 1000 | bytes 1000 | tf_op jit(solution)/shard_map/pallas_call | solution.py:185
  112.5 38.1 %all_to_all.10 = bf16[64,16,512]{2,1,0:T(8,128)(2,1)S(1)} all-to-all(bf16[64,16,512]{2,1,0:T(8,128)(2,1)} %bitcast.53), channel_id=1, replica_groups=mesh['ylo'=2,'z'=8,'x'=4,'yhi'=2,'core'=2] {'ylo','z','yhi','core'}, dimensions={0} | all-to-all | bytes 2097152 | tf_op jit(solution)/shard_map/all_to_all | solution.py:234
  151.0 1.2 copy.10
  152.2 1.2 reshape.43
  (47 shorter events, 9.6 us)
Async XLA Ops:
  0.0 0.8 copy-start
  1.5 17.2 %copy-start.4 = (bf16[2,4,128,512]{3,2,1,0:T(8,128)(2,1)S(1)}, bf16[2,4,128,512]{3,2,1,0:T(8,128)(2,1)}, u32[]{:S(2)}) copy-start(bf16[2,4,128,512]{3,2,1,0:T(8,128)(2,1)} %param.5) | copy-start | bytes 3145732
  2.4 10.5 %collective-permute-start = (bf16[26,1,8,256]{3,2,1,0:T(8,128)(2,1)S(1)}, bf16[26,1,8,256]{3,2,1,0:T(8,128)(2,1)S(1)}, u32[]{:S(2)}, u32[]{:S(2)}) collective-permute-start(bf16[26,1,8,256]{3,2,1,0:T(8,128)(2,1)S(1)} %maximum_bitcast_fusion), channel_id=1, source_target_pairs={{0,96},{1,97},{2,98},{3,99},{4,100},{5,101},{6,102},{7,103},{8,104... | collective-permute-start | bytes 319496 | tf_op jit(solution)/shard_map/ppermute | solution.py:28
  7.6 7.9 %collective-permute-start.1 = (bf16[26,1,8,256]{3,2,1,0:T(8,128)(2,1)S(1)}, bf16[26,1,8,256]{3,2,1,0:T(8,128)(2,1)S(1)}, u32[]{:S(2)}, u32[]{:S(2)}) collective-permute-start(bf16[26,1,8,256]{3,2,1,0:T(8,128)(2,1)S(1)} %maximum_bitcast_fusion), channel_id=1, source_target_pairs={{0,64},{1,65},{2,66},{3,67},{4,68},{5,69},{6,70},{7,71},{8,72},{9,... | collective-permute-start | bytes 319496 | tf_op jit(solution)/shard_map/ppermute | solution.py:28
  8.8 9.0 %collective-permute-start.2 = (bf16[26,1,8,256]{3,2,1,0:T(8,128)(2,1)S(1)}, bf16[26,1,8,256]{3,2,1,0:T(8,128)(2,1)S(1)}, u32[]{:S(2)}, u32[]{:S(2)}) collective-permute-start(bf16[26,1,8,256]{3,2,1,0:T(8,128)(2,1)S(1)} %maximum_bitcast_fusion), channel_id=1, source_target_pairs={{0,32},{1,33},{2,34},{3,35},{4,36},{5,37},{6,38},{7,39},{8,40},{9,... | collective-permute-start | bytes 319496 | tf_op jit(solution)/shard_map/ppermute | solution.py:28
  17.9 7.4 %collective-permute-start.3 = (bf16[26,4,8,256]{3,2,1,0:T(8,128)(2,1)S(1)}, bf16[26,4,8,256]{3,2,1,0:T(8,128)(2,1)S(1)}, u32[]{:S(2)}, u32[]{:S(2)}) collective-permute-start(bf16[26,4,8,256]{3,2,1,0:T(8,128)(2,1)S(1)} %pad_maximum_fusion.4), channel_id=1, source_target_pairs={{0,16},{1,113},{2,18},{3,115},{4,20},{5,117},{6,22},{7,119},{8,24}... | collective-permute-start | bytes 1277960 | tf_op jit(solution)/shard_map/ppermute | solution.py:28
  25.6 9.7 %collective-permute-start.4 = (bf16[17,8,8,256]{3,2,1,0:T(8,128)(2,1)S(1)}, bf16[17,8,8,256]{3,2,1,0:T(8,128)(2,1)S(1)}, u32[]{:S(2)}, u32[]{:S(2)}) collective-permute-start(bf16[17,8,8,256]{3,2,1,0:T(8,128)(2,1)S(1)} %get-tuple-element.20), channel_id=1, source_target_pairs={{0,4},{1,13},{2,6},{3,15},{4,0},{5,9},{6,2},{7,11},{8,12},{9,5},{1... | collective-permute-start | bytes 1671176 | tf_op jit(solution)/shard_map/ppermute | solution.py:28
  28.9 24.3 %collective-permute-start.7 = (bf16[9,8,8,256]{3,2,1,0:T(8,128)(2,1)}, bf16[9,8,8,256]{3,2,1,0:T(8,128)(2,1)S(1)}, u32[]{:S(2)}, u32[]{:S(2)}) collective-permute-start(bf16[9,8,8,256]{3,2,1,0:T(8,128)(2,1)} %get-tuple-element.18), channel_id=1, source_target_pairs={{0,128},{1,131},{2,130},{3,129},{4,132},{5,135},{6,134},{7,133},{8... | collective-permute-start | bytes 884744 | tf_op jit(solution)/shard_map/ppermute | solution.py:28
  35.4 46.1 %copy-start.2 = (bf16[2,17,8,8,256]{4,3,2,1,0:T(8,128)(2,1)}, bf16[2,17,8,8,256]{4,3,2,1,0:T(8,128)(2,1)S(1)}, u32[]{:S(2)}) copy-start(bf16[2,17,8,8,256]{4,3,2,1,0:T(8,128)(2,1)S(1)} %pad_maximum_fusion.1.refs_0_) | copy-start | bytes 3342340
  35.4 29.0 %collective-permute-start.5 = (bf16[2,17,8,8,256]{4,3,2,1,0:T(8,128)(2,1)S(1)}, bf16[2,17,8,8,256]{4,3,2,1,0:T(8,128)(2,1)}, u32[]{:S(2)}, u32[]{:S(2)}) collective-permute-start(bf16[2,17,8,8,256]{4,3,2,1,0:T(8,128)(2,1)S(1)} %pad_maximum_fusion.1.refs_0_), channel_id=1, source_target_pairs={{0,12},{1,5},{2,14},{3,7},{4,8},{5,1},{6,10},{7,3},{8,4},{9,13},{1... | collective-permute-start | bytes 3342344 | tf_op jit(solution)/shard_map/ppermute | solution.py:28
  35.8 28.6 %collective-permute-start.6 = (bf16[2,17,8,8,256]{4,3,2,1,0:T(8,128)(2,1)S(1)}, bf16[2,17,8,8,256]{4,3,2,1,0:T(8,128)(2,1)}, u32[]{:S(2)}, u32[]{:S(2)}) collective-permute-start(bf16[2,17,8,8,256]{4,3,2,1,0:T(8,128)(2,1)S(1)} %pad_maximum_fusion.1.refs_0_), channel_id=1, source_target_pairs={{0,128},{1,131},{2,130},{3,129},{4,132},{5,135},{6,134},{7,133},{8... | collective-permute-start | bytes 3342344 | tf_op jit(solution)/shard_map/ppermute | solution.py:28
  38.5 44.1 %all-to-all-start = ((bf16[64,16,512]{2,1,0:T(8,128)(2,1)}), bf16[64,16,512]{2,1,0:T(8,128)(2,1)S(1)}, u32[]{:S(2)}, u32[]{:S(2)}) async-start(bf16[64,16,512]{2,1,0:T(8,128)(2,1)} %reshape.39), calls=%async_computation | async-start | bytes 2097152 | tf_op jit(solution)/shard_map/all_to_all | solution.py:217
  53.4 10.3 %collective-permute-start.8 = (bf16[2,9,8,8,256]{4,3,2,1,0:T(8,128)(2,1)S(1)}, bf16[2,9,8,8,256]{4,3,2,1,0:T(8,128)(2,1)S(1)}, u32[]{:S(2)}, u32[]{:S(2)}) collective-permute-start(bf16[2,9,8,8,256]{4,3,2,1,0:T(8,128)(2,1)S(1)} %get-tuple-element.24), channel_id=1, source_target_pairs={{0,4},{1,13},{2,6},{3,15},{4,0},{5,9},{6,2},{7,11},{8,12},{9,5},{1... | collective-permute-start | bytes 1769480 | tf_op jit(solution)/shard_map/ppermute | solution.py:28
  63.8 23.5 %copy-start.1 = (bf16[2,2,9,8,8,256]{5,4,3,2,1,0:T(8,128)(2,1)}, bf16[2,2,9,8,8,256]{5,4,3,2,1,0:T(8,128)(2,1)S(1)}, u32[]{:S(2)}) copy-start(bf16[2,2,9,8,8,256]{5,4,3,2,1,0:T(8,128)(2,1)S(1)} %pad_maximum_fusion.refs_0_) | copy-start | bytes 3538948
  63.8 15.5 %collective-permute-start.9 = (bf16[2,2,9,8,8,256]{5,4,3,2,1,0:T(8,128)(2,1)S(1)}, bf16[2,2,9,8,8,256]{5,4,3,2,1,0:T(8,128)(2,1)}, u32[]{:S(2)}, u32[]{:S(2)}) collective-permute-start(bf16[2,2,9,8,8,256]{5,4,3,2,1,0:T(8,128)(2,1)S(1)} %pad_maximum_fusion.refs_0_), channel_id=1, source_target_pairs={{0,12},{1,5},{2,14},{3,7},{4,8},{5,1},{6,10},{7,3},{8,4},{9,13},{1... | collective-permute-start | bytes 3538952 | tf_op jit(solution)/shard_map/ppermute | solution.py:28
  63.9 18.7 %collective-permute-start.10 = (bf16[2,2,9,8,8,256]{5,4,3,2,1,0:T(8,128)(2,1)S(1)}, bf16[2,2,9,8,8,256]{5,4,3,2,1,0:T(8,128)(2,1)}, u32[]{:S(2)}, u32[]{:S(2)}) collective-permute-start(bf16[2,2,9,8,8,256]{5,4,3,2,1,0:T(8,128)(2,1)S(1)} %pad_maximum_fusion.refs_0_), channel_id=1, source_target_pairs={{0,1},{1,0},{2,3},{3,2},{4,5},{5,4},{6,7},{7,6},{8,9},{9,8},{10,11... | collective-permute-start | bytes 3538952 | tf_op jit(solution)/shard_map/ppermute | solution.py:28
  64.4 19.8 %collective-permute-start.12 = (bf16[2,17,8,8,256]{4,3,2,1,0:T(8,128)(2,1)}, bf16[2,17,8,8,256]{4,3,2,1,0:T(8,128)(2,1)}, u32[]{:S(2)}, u32[]{:S(2)}) collective-permute-start(bf16[2,17,8,8,256]{4,3,2,1,0:T(8,128)(2,1)} %collective-permute-done.5.refs_1_), channel_id=1, source_target_pairs={{0,128},{1,131},{2,130},{3,129},{4,132},{5,135},{6,134},{7,133},{8... | collective-permute-start | bytes 3342344 | tf_op jit(solution)/shard_map/ppermute | solution.py:28
  79.4 7.9 %collective-permute-start.11 = (bf16[2,2,9,8,8,256]{5,4,3,2,1,0:T(8,128)(2,1)}, bf16[2,2,9,8,8,256]{5,4,3,2,1,0:T(8,128)(2,1)}, u32[]{:S(2)}, u32[]{:S(2)}) collective-permute-start(bf16[2,2,9,8,8,256]{5,4,3,2,1,0:T(8,128)(2,1)} %collective-permute-done.9.refs_1_), channel_id=1, source_target_pairs={{0,1},{1,0},{2,3},{3,2},{4,5},{5,4},{6,7},{7,6},{8,9},{9,8},{10,11... | collective-permute-start | bytes 3538952 | tf_op jit(solution)/shard_map/ppermute | solution.py:28
  81.4 15.2 %collective-permute-start.13 = (bf16[2,17,8,8,256]{4,3,2,1,0:T(8,128)(2,1)S(1)}, bf16[2,17,8,8,256]{4,3,2,1,0:T(8,128)(2,1)}, u32[]{:S(2)}, u32[]{:S(2)}) collective-permute-start(bf16[2,17,8,8,256]{4,3,2,1,0:T(8,128)(2,1)S(1)} %pad_maximum_fusion.1.refs_0_), channel_id=1, source_target_pairs={{0,1},{1,0},{2,3},{3,2},{4,5},{5,4},{6,7},{7,6},{8,9},{9,8},{10,11... | collective-permute-start | bytes 3342344 | tf_op jit(solution)/shard_map/ppermute | solution.py:28
  81.4 15.3 %collective-permute-start.14 = (bf16[2,17,8,8,256]{4,3,2,1,0:T(8,128)(2,1)}, bf16[2,17,8,8,256]{4,3,2,1,0:T(8,128)(2,1)}, u32[]{:S(2)}, u32[]{:S(2)}) collective-permute-start(bf16[2,17,8,8,256]{4,3,2,1,0:T(8,128)(2,1)} %collective-permute-done.5.refs_1_), channel_id=1, source_target_pairs={{0,1},{1,0},{2,3},{3,2},{4,5},{5,4},{6,7},{7,6},{8,9},{9,8},{10,11... | collective-permute-start | bytes 3342344 | tf_op jit(solution)/shard_map/ppermute | solution.py:28
  82.6 4.7 %copy-start.3 = (bf16[64,16,512]{2,1,0:T(8,128)(2,1)}, bf16[64,16,512]{2,1,0:T(8,128)(2,1)S(1)}, u32[]{:S(2)}) copy-start(bf16[64,16,512]{2,1,0:T(8,128)(2,1)S(1)} %all-to-all-done) | copy-start | bytes 3145732
  82.6 14.1 %collective-permute-start.15 = (bf16[2,17,8,8,256]{4,3,2,1,0:T(8,128)(2,1)}, bf16[2,17,8,8,256]{4,3,2,1,0:T(8,128)(2,1)}, u32[]{:S(2)}, u32[]{:S(2)}) collective-permute-start(bf16[2,17,8,8,256]{4,3,2,1,0:T(8,128)(2,1)} %collective-permute-done.6.refs_2_), channel_id=1, source_target_pairs={{0,1},{1,0},{2,3},{3,2},{4,5},{5,4},{6,7},{7,6},{8,9},{9,8},{10,11... | collective-permute-start | bytes 3342344 | tf_op jit(solution)/shard_map/ppermute | solution.py:28
  84.2 12.5 %collective-permute-start.16 = (bf16[2,17,8,8,256]{4,3,2,1,0:T(8,128)(2,1)}, bf16[2,17,8,8,256]{4,3,2,1,0:T(8,128)(2,1)}, u32[]{:S(2)}, u32[]{:S(2)}) collective-permute-start(bf16[2,17,8,8,256]{4,3,2,1,0:T(8,128)(2,1)} %collective-permute-done.12.refs_3_), channel_id=1, source_target_pairs={{0,1},{1,0},{2,3},{3,2},{4,5},{5,4},{6,7},{7,6},{8,9},{9,8},{10,11... | collective-permute-start | bytes 3342344 | tf_op jit(solution)/shard_map/ppermute | solution.py:28

commit v5 on v4

--- a/solution.py
+++ b/solution.py
@@ -226,8 +226,8 @@
     tight_parts = [t_first, t_second, from_core(t_first), from_core(t_second)]
     second, first_y = lax.optimization_barrier((second, first_y))
     own = [first, second, first_y, from_y(second)]
-    late, cells = lax.optimization_barrier((own[2], cells))
-    parts = own + [from_core(late if n == 2 else piece) for n, piece in enumerate(own)]
+    late, cells = lax.optimization_barrier((own[3], cells))
+    parts = own + [from_core(late if n == 3 else piece) for n, piece in enumerate(own)]
 
     near = block(near_kernel, cells, tight_parts, 1, where, False)
     out = block(far_kernel, near, parts, 4, where, True)

time: 154 us -> 155 us (level)
  transfers between devices with their start and end apart: 18 -> 18, of which waited for: 9 -> 8; matrix products, arithmetic and copies ran while one was open for 3% -> 3% of each run, Pallas kernels for 6% -> 6%
where the time goes in v5:
time: 155 us; the launch traced here: 154 us
  waiting for transfers between devices  40.7 us (26%)
  starting transfers between devices  39.8 us (26%)
  blocking collectives  37.5 us (24%)
  Pallas kernels  25.2 us (16%)
  local copies, waits for them, and re-layouts  8.47 us (5%)
  other arithmetic  2.23 us (1%)
    ppermute x17, waiting for transfers between devices, moved(): return lax.ppermute(array, AXES, pairs)  40.7 us
    all_to_all x1, blocking collectives, shards(): out = lax.all_to_all(out.reshape(64, 16, ch), PEERS, 0, 0)  37.5 us
    pallas_call x2, Pallas kernels, block(): pl.pallas_call(functools.partial(kernel, step), out_shape=jax.ShapeDtypeS...  25.2 us
    ppermute x17, starting transfers between devices, moved(): return lax.ppermute(array, AXES, pairs)  25.1 us
    all_to_all x1, starting transfers between devices, shards(): cells = lax.all_to_all(cells, PEERS, 0, 0).reshape(ROWS, LINE, ch)  14.8 us
  transfers between devices with their start and end apart: 18, of which 8 were waited for; matrix products, arithmetic and copies ran while one was open for 3% of the time, Pallas kernels for 6%

profile of v5, /device:TPU:33, one launch (start us, length us, event | category | flops | bytes accessed | tf_op | source)
XLA Modules:
  0.0 154.1 jit_solution(6167482571536713793)
XLA Ops:
  2.4 5.2 %collective-permute-start = (bf16[26,1,8,256]{3,2,1,0:T(8,128)(2,1)S(1)}, bf16[26,1,8,256]{3,2,1,0:T(8,128)(2,1)S(1)}, u32[]{:S(2)}, u32[]{:S(2)}) collective-permute-start(bf16[26,1,8,256]{3,2,1,0:T(8,128)(2,1)S(1)} %maximum_bitcast_fusion), channel_id=1, source_target_pairs={{0,96},{1,97},{2,98},{3,99},{4,100},{5,101},{6,102},{7,103},{8,104... | collective-permute-start | bytes 319496 | tf_op jit(solution)/shard_map/ppermute | solution.py:28
  7.6 1.2 collective-permute-start.1
  9.8 3.1 %collective-permute-done = bf16[26,1,8,256]{3,2,1,0:T(8,128)(2,1)S(1)} collective-permute-done((bf16[26,1,8,256]{3,2,1,0:T(8,128)(2,1)S(1)}, bf16[26,1,8,256]{3,2,1,0:T(8,128)(2,1)S(1)}, u32[]{:S(2)}, u32[]{:S(2)}) %collective-permute-start) | collective-permute-done | bytes 106528 | tf_op jit(solution)/shard_map/ppermute | solution.py:28
  12.9 2.6 %collective-permute-done.1 = bf16[26,1,8,256]{3,2,1,0:T(8,128)(2,1)S(1)} collective-permute-done((bf16[26,1,8,256]{3,2,1,0:T(8,128)(2,1)S(1)}, bf16[26,1,8,256]{3,2,1,0:T(8,128)(2,1)S(1)}, u32[]{:S(2)}, u32[]{:S(2)}) %collective-permute-start.1) | collective-permute-done | bytes 106528 | tf_op jit(solution)/shard_map/ppermute | solution.py:28
  15.5 2.3 %collective-permute-done.2 = bf16[26,1,8,256]{3,2,1,0:T(8,128)(2,1)S(1)} collective-permute-done((bf16[26,1,8,256]{3,2,1,0:T(8,128)(2,1)S(1)}, bf16[26,1,8,256]{3,2,1,0:T(8,128)(2,1)S(1)}, u32[]{:S(2)}, u32[]{:S(2)}) %collective-permute-start.2) | collective-permute-done | bytes 106528 | tf_op jit(solution)/shard_map/ppermute | solution.py:28
  19.1 1.2 copy.7
  20.3 1.2 reshape.39
  21.6 3.7 %collective-permute-done.3 = bf16[26,4,8,256]{3,2,1,0:T(8,128)(2,1)S(1)} collective-permute-done((bf16[26,4,8,256]{3,2,1,0:T(8,128)(2,1)S(1)}, bf16[26,4,8,256]{3,2,1,0:T(8,128)(2,1)S(1)}, u32[]{:S(2)}, u32[]{:S(2)}) %collective-permute-start.3) | collective-permute-done | bytes 426016 | tf_op jit(solution)/shard_map/ppermute | solution.py:28
  25.6 2.6 %collective-permute-start.4 = (bf16[17,8,8,256]{3,2,1,0:T(8,128)(2,1)S(1)}, bf16[17,8,8,256]{3,2,1,0:T(8,128)(2,1)S(1)}, u32[]{:S(2)}, u32[]{:S(2)}) collective-permute-start(bf16[17,8,8,256]{3,2,1,0:T(8,128)(2,1)S(1)} %get-tuple-element.20), channel_id=1, source_target_pairs={{0,4},{1,13},{2,6},{3,15},{4,0},{5,9},{6,2},{7,11},{8,12},{9,5},{1... | collective-permute-start | bytes 1671176 | tf_op jit(solution)/shard_map/ppermute | solution.py:28
  28.2 2.8 %collective-permute-start.8 = (bf16[9,8,8,256]{3,2,1,0:T(8,128)(2,1)S(1)}, bf16[9,8,8,256]{3,2,1,0:T(8,128)(2,1)S(1)}, u32[]{:S(2)}, u32[]{:S(2)}) collective-permute-start(bf16[9,8,8,256]{3,2,1,0:T(8,128)(2,1)S(1)} %get-tuple-element.18), channel_id=1, source_target_pairs={{0,128},{1,131},{2,130},{3,129},{4,132},{5,135},{6,134},{7,133},{8... | collective-permute-start | bytes 884744 | tf_op jit(solution)/shard_map/ppermute | solution.py:28
  31.0 4.2 %collective-permute-done.4 = bf16[17,8,8,256]{3,2,1,0:T(8,128)(2,1)S(1)} collective-permute-done((bf16[17,8,8,256]{3,2,1,0:T(8,128)(2,1)S(1)}, bf16[17,8,8,256]{3,2,1,0:T(8,128)(2,1)S(1)}, u32[]{:S(2)}, u32[]{:S(2)}) %collective-permute-start.4) | collective-permute-done | bytes 557088 | tf_op jit(solution)/shard_map/ppermute | solution.py:28
  35.8 2.7 %collective-permute-start.6 = (bf16[2,17,8,8,256]{4,3,2,1,0:T(8,128)(2,1)S(1)}, bf16[2,17,8,8,256]{4,3,2,1,0:T(8,128)(2,1)}, u32[]{:S(2)}, u32[]{:S(2)}) collective-permute-start(bf16[2,17,8,8,256]{4,3,2,1,0:T(8,128)(2,1)S(1)} %pad_maximum_fusion.1.refs_0_), channel_id=1, source_target_pairs={{0,128},{1,131},{2,130},{3,129},{4,132},{5,135},{6,134},{7,133},{8... | collective-permute-start | bytes 3342344 | tf_op jit(solution)/shard_map/ppermute | solution.py:28
  38.5 14.8 %all-to-all-start = ((bf16[64,16,512]{2,1,0:T(8,128)(2,1)}), bf16[64,16,512]{2,1,0:T(8,128)(2,1)S(1)}, u32[]{:S(2)}, u32[]{:S(2)}) async-start(bf16[64,16,512]{2,1,0:T(8,128)(2,1)} %reshape.39), calls=%async_computation | async-start | bytes 2097152 | tf_op jit(solution)/shard_map/all_to_all | solution.py:217
  53.6 10.0 %collective-permute-done.9 = bf16[2,9,8,8,256]{4,3,2,1,0:T(8,128)(2,1)S(1)} collective-permute-done((bf16[2,9,8,8,256]{4,3,2,1,0:T(8,128)(2,1)S(1)}, bf16[2,9,8,8,256]{4,3,2,1,0:T(8,128)(2,1)S(1)}, u32[]{:S(2)}, u32[]{:S(2)}) %collective-permute-start.9) | collective-permute-done | bytes 589856 | tf_op jit(solution)/shard_map/ppermute | solution.py:28
  64.4 2.5 %collective-permute-start.7 = (bf16[2,17,8,8,256]{4,3,2,1,0:T(8,128)(2,1)}, bf16[2,17,8,8,256]{4,3,2,1,0:T(8,128)(2,1)S(1)}, u32[]{:S(2)}, u32[]{:S(2)}) collective-permute-start(bf16[2,17,8,8,256]{4,3,2,1,0:T(8,128)(2,1)} %collective-permute-done.5.refs_1_), channel_id=1, source_target_pairs={{0,128},{1,131},{2,130},{3,129},{4,132},{5,135},{6,134},{7,133},{8... | collective-permute-start | bytes 3342344 | tf_op jit(solution)/shard_map/ppermute | solution.py:28
  66.9 12.4 %collective-permute-done.10.refs_1_ = bf16[2,2,9,8,8,256]{5,4,3,2,1,0:T(8,128)(2,1)} collective-permute-done((bf16[2,2,9,8,8,256]{5,4,3,2,1,0:T(8,128)(2,1)S(1)}, bf16[2,2,9,8,8,256]{5,4,3,2,1,0:T(8,128)(2,1)}, u32[]{:S(2)}, u32[]{:S(2)}) %collective-permute-start.10) | collective-permute-done | bytes 1179680 | tf_op jit(solution)/shard_map/ppermute | solution.py:28
  79.4 2.1 %collective-permute-start.12 = (bf16[2,2,9,8,8,256]{5,4,3,2,1,0:T(8,128)(2,1)}, bf16[2,2,9,8,8,256]{5,4,3,2,1,0:T(8,128)(2,1)}, u32[]{:S(2)}, u32[]{:S(2)}) collective-permute-start(bf16[2,2,9,8,8,256]{5,4,3,2,1,0:T(8,128)(2,1)} %collective-permute-done.10.refs_1_), channel_id=1, source_target_pairs={{0,1},{1,0},{2,3},{3,2},{4,5},{5,4},{6,7},{7,6},{8,9},{9,8},{10,11... | collective-permute-start | bytes 3538952 | tf_op jit(solution)/shard_map/ppermute | solution.py:28
  81.9 2.2 %collective-permute-done.7.refs_3_ = bf16[2,17,8,8,256]{4,3,2,1,0:T(8,128)(2,1)S(1)} collective-permute-done((bf16[2,17,8,8,256]{4,3,2,1,0:T(8,128)(2,1)}, bf16[2,17,8,8,256]{4,3,2,1,0:T(8,128)(2,1)S(1)}, u32[]{:S(2)}, u32[]{:S(2)}) %collective-permute-start.7) | collective-permute-done | bytes 1114144 | tf_op jit(solution)/shard_map/ppermute | solution.py:28
  85.3 2.3 %collective-permute-start.15 = (bf16[2,17,8,8,256]{4,3,2,1,0:T(8,128)(2,1)}, bf16[2,17,8,8,256]{4,3,2,1,0:T(8,128)(2,1)}, u32[]{:S(2)}, u32[]{:S(2)}) collective-permute-start(bf16[2,17,8,8,256]{4,3,2,1,0:T(8,128)(2,1)} %collective-permute-done.6.refs_2_), channel_id=1, source_target_pairs={{0,1},{1,0},{2,3},{3,2},{4,5},{5,4},{6,7},{7,6},{8,9},{9,8},{10,11... | collective-permute-start | bytes 3342344 | tf_op jit(solution)/shard_map/ppermute | solution.py:28
  88.6 9.4 %shard_map.55.cells = bf16[16,64,512]{2,1,0:T(8,128)(2,1)} custom-call(s32[3]{0:T(128)} %pad_add_fusion.where, bf16[16,64,512]{2,1,0:T(8,128)(2,1)} %bitcast.52, bf16[2,2,9,8,8,256]{5,4,3,2,1,0:T(8,128)(2,1)} %copy-done.1, bf16[2,2,9,8,8,256]{5,4,3,2,1,0:T(8,128)(2,1)} %collective-permute-done.10.refs_1_, ...), custom_call_target="tpu_custom_call" | custom-call | flops 1000 | bytes 1000 | tf_op jit(solution)/shard_map/pallas_call | solution.py:185
  98.0 15.8 %shard_map.56 = bf16[16,64,512]{2,1,0:T(8,128)(2,1)} custom-call(s32[3]{0:T(128)} %pad_add_fusion.where, bf16[16,64,512]{2,1,0:T(8,128)(2,1)} %shard_map.55.cells, bf16[2,17,8,8,256]{4,3,2,1,0:T(8,128)(2,1)} %copy-done.2, bf16[2,17,8,8,256]{4,3,2,1,0:T(8,128)(2,1)} %collective-permute-done.5.refs_1_, ...), custom_call_target="tpu_custom_call" | custom-call | flops 1000 | bytes 1000 | tf_op jit(solution)/shard_map/pallas_call | solution.py:185
  113.8 37.5 %all_to_all.10 = bf16[64,16,512]{2,1,0:T(8,128)(2,1)S(1)} all-to-all(bf16[64,16,512]{2,1,0:T(8,128)(2,1)} %bitcast.53), channel_id=1, replica_groups=mesh['ylo'=2,'z'=8,'x'=4,'yhi'=2,'core'=2] {'ylo','z','yhi','core'}, dimensions={0} | all-to-all | bytes 2097152 | tf_op jit(solution)/shard_map/all_to_all | solution.py:234
  151.7 1.2 copy.10
  152.8 1.2 reshape.43
  (49 shorter events, 9.6 us)
Async XLA Ops:
  0.0 0.8 copy-start
  1.5 17.2 %copy-start.5 = (bf16[2,4,128,512]{3,2,1,0:T(8,128)(2,1)S(1)}, bf16[2,4,128,512]{3,2,1,0:T(8,128)(2,1)}, u32[]{:S(2)}) copy-start(bf16[2,4,128,512]{3,2,1,0:T(8,128)(2,1)} %param.5) | copy-start | bytes 3145732
  2.4 10.5 %collective-permute-start = (bf16[26,1,8,256]{3,2,1,0:T(8,128)(2,1)S(1)}, bf16[26,1,8,256]{3,2,1,0:T(8,128)(2,1)S(1)}, u32[]{:S(2)}, u32[]{:S(2)}) collective-permute-start(bf16[26,1,8,256]{3,2,1,0:T(8,128)(2,1)S(1)} %maximum_bitcast_fusion), channel_id=1, source_target_pairs={{0,96},{1,97},{2,98},{3,99},{4,100},{5,101},{6,102},{7,103},{8,104... | collective-permute-start | bytes 319496 | tf_op jit(solution)/shard_map/ppermute | solution.py:28
  7.6 7.9 %collective-permute-start.1 = (bf16[26,1,8,256]{3,2,1,0:T(8,128)(2,1)S(1)}, bf16[26,1,8,256]{3,2,1,0:T(8,128)(2,1)S(1)}, u32[]{:S(2)}, u32[]{:S(2)}) collective-permute-start(bf16[26,1,8,256]{3,2,1,0:T(8,128)(2,1)S(1)} %maximum_bitcast_fusion), channel_id=1, source_target_pairs={{0,64},{1,65},{2,66},{3,67},{4,68},{5,69},{6,70},{7,71},{8,72},{9,... | collective-permute-start | bytes 319496 | tf_op jit(solution)/shard_map/ppermute | solution.py:28
  8.8 9.0 %collective-permute-start.2 = (bf16[26,1,8,256]{3,2,1,0:T(8,128)(2,1)S(1)}, bf16[26,1,8,256]{3,2,1,0:T(8,128)(2,1)S(1)}, u32[]{:S(2)}, u32[]{:S(2)}) collective-permute-start(bf16[26,1,8,256]{3,2,1,0:T(8,128)(2,1)S(1)} %maximum_bitcast_fusion), channel_id=1, source_target_pairs={{0,32},{1,33},{2,34},{3,35},{4,36},{5,37},{6,38},{7,39},{8,40},{9,... | collective-permute-start | bytes 319496 | tf_op jit(solution)/shard_map/ppermute | solution.py:28
  17.9 7.4 %collective-permute-start.3 = (bf16[26,4,8,256]{3,2,1,0:T(8,128)(2,1)S(1)}, bf16[26,4,8,256]{3,2,1,0:T(8,128)(2,1)S(1)}, u32[]{:S(2)}, u32[]{:S(2)}) collective-permute-start(bf16[26,4,8,256]{3,2,1,0:T(8,128)(2,1)S(1)} %pad_maximum_fusion.4), channel_id=1, source_target_pairs={{0,16},{1,113},{2,18},{3,115},{4,20},{5,117},{6,22},{7,119},{8,24}... | collective-permute-start | bytes 1277960 | tf_op jit(solution)/shard_map/ppermute | solution.py:28
  25.6 9.7 %collective-permute-start.4 = (bf16[17,8,8,256]{3,2,1,0:T(8,128)(2,1)S(1)}, bf16[17,8,8,256]{3,2,1,0:T(8,128)(2,1)S(1)}, u32[]{:S(2)}, u32[]{:S(2)}) collective-permute-start(bf16[17,8,8,256]{3,2,1,0:T(8,128)(2,1)S(1)} %get-tuple-element.20), channel_id=1, source_target_pairs={{0,4},{1,13},{2,6},{3,15},{4,0},{5,9},{6,2},{7,11},{8,12},{9,5},{1... | collective-permute-start | bytes 1671176 | tf_op jit(solution)/shard_map/ppermute | solution.py:28
  28.2 25.1 %collective-permute-start.8 = (bf16[9,8,8,256]{3,2,1,0:T(8,128)(2,1)S(1)}, bf16[9,8,8,256]{3,2,1,0:T(8,128)(2,1)S(1)}, u32[]{:S(2)}, u32[]{:S(2)}) collective-permute-start(bf16[9,8,8,256]{3,2,1,0:T(8,128)(2,1)S(1)} %get-tuple-element.18), channel_id=1, source_target_pairs={{0,128},{1,131},{2,130},{3,129},{4,132},{5,135},{6,134},{7,133},{8... | collective-permute-start | bytes 884744 | tf_op jit(solution)/shard_map/ppermute | solution.py:28
  35.4 46.1 %copy-start.2 = (bf16[2,17,8,8,256]{4,3,2,1,0:T(8,128)(2,1)}, bf16[2,17,8,8,256]{4,3,2,1,0:T(8,128)(2,1)S(1)}, u32[]{:S(2)}) copy-start(bf16[2,17,8,8,256]{4,3,2,1,0:T(8,128)(2,1)S(1)} %pad_maximum_fusion.1.refs_0_) | copy-start | bytes 3342340
  35.4 29.0 %collective-permute-start.5 = (bf16[2,17,8,8,256]{4,3,2,1,0:T(8,128)(2,1)S(1)}, bf16[2,17,8,8,256]{4,3,2,1,0:T(8,128)(2,1)}, u32[]{:S(2)}, u32[]{:S(2)}) collective-permute-start(bf16[2,17,8,8,256]{4,3,2,1,0:T(8,128)(2,1)S(1)} %pad_maximum_fusion.1.refs_0_), channel_id=1, source_target_pairs={{0,12},{1,5},{2,14},{3,7},{4,8},{5,1},{6,10},{7,3},{8,4},{9,13},{1... | collective-permute-start | bytes 3342344 | tf_op jit(solution)/shard_map/ppermute | solution.py:28
  35.8 28.6 %collective-permute-start.6 = (bf16[2,17,8,8,256]{4,3,2,1,0:T(8,128)(2,1)S(1)}, bf16[2,17,8,8,256]{4,3,2,1,0:T(8,128)(2,1)}, u32[]{:S(2)}, u32[]{:S(2)}) collective-permute-start(bf16[2,17,8,8,256]{4,3,2,1,0:T(8,128)(2,1)S(1)} %pad_maximum_fusion.1.refs_0_), channel_id=1, source_target_pairs={{0,128},{1,131},{2,130},{3,129},{4,132},{5,135},{6,134},{7,133},{8... | collective-permute-start | bytes 3342344 | tf_op jit(solution)/shard_map/ppermute | solution.py:28
  38.5 49.1 %all-to-all-start = ((bf16[64,16,512]{2,1,0:T(8,128)(2,1)}), bf16[64,16,512]{2,1,0:T(8,128)(2,1)S(1)}, u32[]{:S(2)}, u32[]{:S(2)}) async-start(bf16[64,16,512]{2,1,0:T(8,128)(2,1)} %reshape.39), calls=%async_computation | async-start | bytes 2097152 | tf_op jit(solution)/shard_map/all_to_all | solution.py:217
  53.4 10.3 %collective-permute-start.9 = (bf16[2,9,8,8,256]{4,3,2,1,0:T(8,128)(2,1)S(1)}, bf16[2,9,8,8,256]{4,3,2,1,0:T(8,128)(2,1)S(1)}, u32[]{:S(2)}, u32[]{:S(2)}) collective-permute-start(bf16[2,9,8,8,256]{4,3,2,1,0:T(8,128)(2,1)S(1)} %get-tuple-element.24), channel_id=1, source_target_pairs={{0,4},{1,13},{2,6},{3,15},{4,0},{5,9},{6,2},{7,11},{8,12},{9,5},{1... | collective-permute-start | bytes 1769480 | tf_op jit(solution)/shard_map/ppermute | solution.py:28
  63.8 24.7 %copy-start.1 = (bf16[2,2,9,8,8,256]{5,4,3,2,1,0:T(8,128)(2,1)}, bf16[2,2,9,8,8,256]{5,4,3,2,1,0:T(8,128)(2,1)S(1)}, u32[]{:S(2)}) copy-start(bf16[2,2,9,8,8,256]{5,4,3,2,1,0:T(8,128)(2,1)S(1)} %pad_maximum_fusion.refs_0_) | copy-start | bytes 3538948
  63.8 15.5 %collective-permute-start.10 = (bf16[2,2,9,8,8,256]{5,4,3,2,1,0:T(8,128)(2,1)S(1)}, bf16[2,2,9,8,8,256]{5,4,3,2,1,0:T(8,128)(2,1)}, u32[]{:S(2)}, u32[]{:S(2)}) collective-permute-start(bf16[2,2,9,8,8,256]{5,4,3,2,1,0:T(8,128)(2,1)S(1)} %pad_maximum_fusion.refs_0_), channel_id=1, source_target_pairs={{0,12},{1,5},{2,14},{3,7},{4,8},{5,1},{6,10},{7,3},{8,4},{9,13},{1... | collective-permute-start | bytes 3538952 | tf_op jit(solution)/shard_map/ppermute | solution.py:28
  63.9 23.7 %collective-permute-start.11 = (bf16[2,2,9,8,8,256]{5,4,3,2,1,0:T(8,128)(2,1)S(1)}, bf16[2,2,9,8,8,256]{5,4,3,2,1,0:T(8,128)(2,1)}, u32[]{:S(2)}, u32[]{:S(2)}) collective-permute-start(bf16[2,2,9,8,8,256]{5,4,3,2,1,0:T(8,128)(2,1)S(1)} %pad_maximum_fusion.refs_0_), channel_id=1, source_target_pairs={{0,1},{1,0},{2,3},{3,2},{4,5},{5,4},{6,7},{7,6},{8,9},{9,8},{10,11... | collective-permute-start | bytes 3538952 | tf_op jit(solution)/shard_map/ppermute | solution.py:28
  64.4 19.8 %collective-permute-start.7 = (bf16[2,17,8,8,256]{4,3,2,1,0:T(8,128)(2,1)}, bf16[2,17,8,8,256]{4,3,2,1,0:T(8,128)(2,1)S(1)}, u32[]{:S(2)}, u32[]{:S(2)}) collective-permute-start(bf16[2,17,8,8,256]{4,3,2,1,0:T(8,128)(2,1)} %collective-permute-done.5.refs_1_), channel_id=1, source_target_pairs={{0,128},{1,131},{2,130},{3,129},{4,132},{5,135},{6,134},{7,133},{8... | collective-permute-start | bytes 3342344 | tf_op jit(solution)/shard_map/ppermute | solution.py:28
  79.4 9.1 %collective-permute-start.12 = (bf16[2,2,9,8,8,256]{5,4,3,2,1,0:T(8,128)(2,1)}, bf16[2,2,9,8,8,256]{5,4,3,2,1,0:T(8,128)(2,1)}, u32[]{:S(2)}, u32[]{:S(2)}) collective-permute-start(bf16[2,2,9,8,8,256]{5,4,3,2,1,0:T(8,128)(2,1)} %collective-permute-done.10.refs_1_), channel_id=1, source_target_pairs={{0,1},{1,0},{2,3},{3,2},{4,5},{5,4},{6,7},{7,6},{8,9},{9,8},{10,11... | collective-permute-start | bytes 3538952 | tf_op jit(solution)/shard_map/ppermute | solution.py:28
  81.4 16.5 %collective-permute-start.13 = (bf16[2,17,8,8,256]{4,3,2,1,0:T(8,128)(2,1)S(1)}, bf16[2,17,8,8,256]{4,3,2,1,0:T(8,128)(2,1)}, u32[]{:S(2)}, u32[]{:S(2)}) collective-permute-start(bf16[2,17,8,8,256]{4,3,2,1,0:T(8,128)(2,1)S(1)} %pad_maximum_fusion.1.refs_0_), channel_id=1, source_target_pairs={{0,1},{1,0},{2,3},{3,2},{4,5},{5,4},{6,7},{7,6},{8,9},{9,8},{10,11... | collective-permute-start | bytes 3342344 | tf_op jit(solution)/shard_map/ppermute | solution.py:28
  81.4 16.5 %collective-permute-start.14 = (bf16[2,17,8,8,256]{4,3,2,1,0:T(8,128)(2,1)}, bf16[2,17,8,8,256]{4,3,2,1,0:T(8,128)(2,1)}, u32[]{:S(2)}, u32[]{:S(2)}) collective-permute-start(bf16[2,17,8,8,256]{4,3,2,1,0:T(8,128)(2,1)} %collective-permute-done.5.refs_1_), channel_id=1, source_target_pairs={{0,1},{1,0},{2,3},{3,2},{4,5},{5,4},{6,7},{7,6},{8,9},{9,8},{10,11... | collective-permute-start | bytes 3342344 | tf_op jit(solution)/shard_map/ppermute | solution.py:28
  84.2 1.1 copy-start.4
  85.3 12.7 %collective-permute-start.15 = (bf16[2,17,8,8,256]{4,3,2,1,0:T(8,128)(2,1)}, bf16[2,17,8,8,256]{4,3,2,1,0:T(8,128)(2,1)}, u32[]{:S(2)}, u32[]{:S(2)}) collective-permute-start(bf16[2,17,8,8,256]{4,3,2,1,0:T(8,128)(2,1)} %collective-permute-done.6.refs_2_), channel_id=1, source_target_pairs={{0,1},{1,0},{2,3},{3,2},{4,5},{5,4},{6,7},{7,6},{8,9},{9,8},{10,11... | collective-permute-start | bytes 3342344 | tf_op jit(solution)/shard_map/ppermute | solution.py:28
  87.6 1.0 copy-start.3
  87.6 10.4 %collective-permute-start.16 = (bf16[2,17,8,8,256]{4,3,2,1,0:T(8,128)(2,1)}, bf16[2,17,8,8,256]{4,3,2,1,0:T(8,128)(2,1)}, u32[]{:S(2)}, u32[]{:S(2)}) collective-permute-start(bf16[2,17,8,8,256]{4,3,2,1,0:T(8,128)(2,1)} %copy-done.4), channel_id=1, source_target_pairs={{0,1},{1,0},{2,3},{3,2},{4,5},{5,4},{6,7},{7,6},{8,9},{9,8},{10,11... | collective-permute-start | bytes 3342344 | tf_op jit(solution)/shard_map/ppermute | solution.py:28
